TPU v7x, 128 devices: a whole 4x4x4 slice. The times are simulated.
128 devices in a mesh: grp: 8 (over z, core), ad: 16 (over y, x).
Axes of the slice: x: 4, y: 4, z: 4, core: 2. Of those that a mesh axis runs over, the one named last changes fastest.
Arguments:
- tokens: bfloat16 [4096, 5120], P(('grp', 'ad')), may hold values from -6 to 6
- prompt_cache: bfloat16 [32, 8, 4096, 256], P('grp', None, 'ad'), may hold values from -100 to 100
- generated_cache: bfloat16 [1024, 256, 256], P('grp', 'ad'), may hold values from -9 to 9
- suffix_lengths: int32 [1024], P('grp'), may hold values from 1 to 32
- fanout: int32 [32, 2], replicated, may hold values from 0 to 7, as said below
- prompt_adapter: int32 [32], replicated, may hold values from 0 to 3
- query_weight: bfloat16 [5120, 8192], P(None, 'ad'), may hold values from -0.078125 to 0.078125
- key_value_weight: bfloat16 [5120, 2, 1024], P(None, None, 'ad'), may hold values from -0.078125 to 0.078125
- output_weight: bfloat16 [8192, 5120], P('ad'), may hold values from -0.0625 to 0.0625
- adapter_down_maps: bfloat16 [5120, 4, 128], P('ad'), may hold values from -0.078125 to 0.078125
- adapter_up_maps: bfloat16 [4, 128, 8192], P(None, None, 'ad'), may hold values from -0.5 to 0.5
- query_norm_gain: float32 [128], replicated, may hold values from 1 to 8
- key_norm_gain: float32 [128], replicated, may hold values from 1 to 3
Outputs:
- mixed: bfloat16 [4096, 5120], P(('grp', 'ad'))
Inputs may be any that keep to these rules, and one draw needn't show every extreme that they name: `fanout`: each row lists 2 different groups. Among the 4 prompts of one owner group every group is listed exactly once.
All inputs are finite; a program needn't handle non-finite values.
Results may differ from a plain program's by a relative error of at most 0.035.
Values may be sent and summed in bfloat16 or wider, within the bound.
No kernel may reach another device: no remote copies, remote signals or barrier semaphores. Data moves between devices by JAX's collectives and lax.ppermute only.
A program may use at most 192 MiB of HBM per device.

v0:
```python
import jax
import jax.numpy as jnp
from jax import lax
from jax.sharding import PartitionSpec as P

MODEL_WIDTH = 5120
KEY_VALUE_HEADS = 8
HEAD_SIZE = 128
ADAPTER_RANK = 128
FAN = 2
DECODE_STEPS = 4
ADAPTER_COUNT = 4
PROMPT_TOKENS = 4096


theta_base = 1000000.0
norm_eps = 1e-06
masked_low = -1e30


def from_partner(block, axis, stride):
    count = lax.axis_size(axis)
    route = []
    for low in range(count):
        high = low | 1 << stride
        if high != low and high < count:
            route += [(low, high), (high, low)]
    return lax.ppermute(block, axis, route)


def rms_scale(vector, gain_vec):
    mean_sq = jnp.mean(vector * vector, axis=-1, keepdims=True)
    return vector * lax.rsqrt(mean_sq + norm_eps) * gain_vec


def rotate(vector, position):
    half_len = vector.shape[-1] // 2
    inverse = theta_base ** (-2.0 * jnp.arange(half_len, dtype=jnp.float32) / vector.shape[-1])
    angles = position[..., None] * inverse
    cosine = jnp.cos(angles)
    sine_part = jnp.sin(angles)
    first_half = vector[..., :half_len]
    second_half = vector[..., half_len:]
    return jnp.concatenate(
        [
            first_half * cosine - second_half * sine_part,
            second_half * cosine + first_half * sine_part,
        ],
        axis=-1,
    )


def slot_prompts(fanout, groups, owned_count):
    listed = jnp.any(
        fanout[:, :, None] == jnp.arange(groups, dtype=jnp.int32)[None, None, :], axis=1
    )
    listed = listed.astype(jnp.int32).reshape(groups, owned_count, groups)
    local_index = jnp.sum(listed * jnp.arange(owned_count, dtype=jnp.int32)[None, :, None], axis=1)
    prompt_ids = jnp.arange(groups, dtype=jnp.int32)[:, None] * owned_count + local_index
    return prompt_ids.T


def score_parts(query_row_block, prompt_keys, generated_keys, suffix_pos, lengths, latest_keys):
    score_scale = query_row_block.shape[-1] ** (-0.5)
    per_slot_order = query_row_block.reshape(prompt_keys.shape[0], -1, query_row_block.shape[-1])
    prefix_part = (
        jnp.einsum("pzl,pfl->pzf", per_slot_order, prompt_keys, preferred_element_type=jnp.float32)
        * score_scale
    )
    suffix_part = (
        jnp.einsum(
            "pzl,pfl->pzf", query_row_block, generated_keys, preferred_element_type=jnp.float32
        )
        * score_scale
    )
    suffix_part = jnp.where(
        suffix_pos[None, None, :] < lengths[:, None, None], suffix_part, masked_low
    )
    score_list = [prefix_part, suffix_part]
    fresh_part = (
        jnp.einsum("pzl,pfl->pzf", query_row_block, latest_keys, preferred_element_type=jnp.float32)
        * score_scale
    )
    head_count = query_row_block.shape[1] // latest_keys.shape[1]
    step_of = jnp.arange(query_row_block.shape[1], dtype=jnp.int32) // head_count
    fresh_part = jnp.where(
        jnp.arange(latest_keys.shape[1], dtype=jnp.int32)[None, None, :] <= step_of[None, :, None],
        fresh_part,
        masked_low,
    )
    score_list.append(fresh_part)
    return score_list


def row_peak(score_list, samples):
    peak = jnp.max(score_list[0], axis=-1).reshape(samples, -1)
    for part_scores in score_list[1:]:
        peak = jnp.maximum(peak, jnp.max(part_scores, axis=-1))
    return peak


def weigh_parts(score_list, value_list, peak):
    samples = peak.shape[0]
    slot_count = score_list[0].shape[0]
    spread = jnp.exp(score_list[0] - peak.reshape(slot_count, -1)[..., None])
    denominator = jnp.sum(spread, axis=-1).reshape(samples, -1)
    summed = jnp.einsum(
        "fup,fpe->fue",
        spread.astype(jnp.bfloat16),
        value_list[0],
        preferred_element_type=jnp.float32,
    )
    summed = summed.reshape(samples, peak.shape[1], -1)
    for part_scores, part_values in zip(score_list[1:], value_list[1:]):
        spread = jnp.exp(part_scores - peak[..., None])
        denominator = denominator + jnp.sum(spread, axis=-1)
        summed = summed + jnp.einsum(
            "fup,fpe->fue",
            spread.astype(jnp.bfloat16),
            part_values,
            preferred_element_type=jnp.float32,
        )
    return (summed, denominator)


def attend(query_vectors, pages, suffix, lengths, latest_keys, fresh_values, sub_part):
    samples = suffix.shape[0]
    suffix_span = suffix.shape[1]
    own_pos = sub_part * suffix_span + jnp.arange(suffix_span, dtype=jnp.int32)

    def per_slot_order(page_set):
        return page_set

    prefix_pages = per_slot_order(pages)
    other_prefix, other_suffix = from_partner((pages, suffix), "ad", 0)
    prefix_pages = jnp.concatenate([prefix_pages, per_slot_order(other_prefix)], axis=1)
    suffix_pages = jnp.concatenate([suffix, other_suffix], axis=1)
    suffix_pos = jnp.concatenate(
        [own_pos, (1 - sub_part) * suffix_span + jnp.arange(suffix_span, dtype=jnp.int32)]
    )
    score_list = score_parts(
        query_vectors,
        prefix_pages[..., :HEAD_SIZE],
        suffix_pages[..., :HEAD_SIZE],
        suffix_pos,
        lengths,
        latest_keys,
    )
    peak = row_peak(score_list, samples)
    summed, denominator = weigh_parts(
        score_list,
        (prefix_pages[..., HEAD_SIZE:], suffix_pages[..., HEAD_SIZE:], fresh_values),
        peak,
    )
    return (summed / denominator[..., None]).astype(jnp.bfloat16)


def shards(
    tokens,
    prompt_cache,
    generated_cache,
    suffix_lengths,
    fanout,
    prompt_adapter,
    query_weight,
    key_value_weight,
    output_weight,
    adapter_down_maps,
    adapter_up_maps,
    query_norm_gain,
    key_norm_gain,
):
    groups = lax.axis_size("grp")
    device_shards = lax.axis_size("ad")
    piece_count = device_shards // KEY_VALUE_HEADS
    my_group = lax.axis_index("grp")
    my_shard = lax.axis_index("ad")
    sub_part = my_shard % piece_count
    owned_count = groups // FAN
    samples = generated_cache.shape[0]
    per_slot = samples // groups
    row_count = samples * DECODE_STEPS
    query_span_width = query_weight.shape[1]
    head_count = query_span_width // HEAD_SIZE
    key_width = key_value_weight.shape[2]
    prompt_total = fanout.shape[0]
    slot_table = slot_prompts(fanout, groups, owned_count)
    my_prompts = lax.dynamic_index_in_dim(slot_table, my_group, 0, keepdims=False)
    prompt_hit = (my_prompts[:, None] == jnp.arange(prompt_total, dtype=jnp.int32)[None, :]).astype(
        jnp.int32
    )
    slot_tasks = jnp.sum(prompt_hit * prompt_adapter[None, :], axis=1)
    row_tasks = jnp.repeat(slot_tasks, per_slot * DECODE_STEPS)
    adapter_row_block = (
        row_tasks[:, None] == jnp.arange(ADAPTER_COUNT, dtype=jnp.int32)[None, :]
    ).astype(jnp.float32)
    adapter_tiles = lax.all_gather(adapter_down_maps, "ad", axis=0, tiled=True).reshape(
        MODEL_WIDTH, ADAPTER_COUNT * ADAPTER_RANK
    )
    flat_keyval = key_value_weight.reshape(MODEL_WIDTH, 2 * key_width)
    part_rows = lax.all_gather(tokens, "ad", axis=0, tiled=True)
    piece_len = part_rows.shape[0]
    query_part = jnp.dot(part_rows, query_weight, preferred_element_type=jnp.float32)
    keyval_part = jnp.dot(part_rows, flat_keyval, preferred_element_type=jnp.float32)
    rank_part = jnp.sum(
        jnp.dot(part_rows, adapter_tiles, preferred_element_type=jnp.float32).reshape(
            piece_len, ADAPTER_COUNT, ADAPTER_RANK
        )
        * adapter_row_block[:, :, None],
        axis=1,
    )
    projected = jnp.concatenate([query_part, keyval_part, rank_part], axis=1)
    query_plain = projected[:, :query_span_width]
    key_value_rows = projected[:, query_span_width : query_span_width + 2 * key_width]
    low_rank_term = projected[:, query_span_width + 2 * key_width :]
    spread_rank_term = (
        low_rank_term.astype(jnp.bfloat16)[:, None, :]
        * adapter_row_block.astype(jnp.bfloat16)[:, :, None]
    ).reshape(row_count, ADAPTER_COUNT * ADAPTER_RANK)
    query_complete = query_plain + jnp.dot(
        spread_rank_term,
        adapter_up_maps.reshape(ADAPTER_COUNT * ADAPTER_RANK, query_span_width),
        preferred_element_type=jnp.float32,
    )
    position = (
        PROMPT_TOKENS
        + jnp.repeat(suffix_lengths, DECODE_STEPS)
        + jnp.tile(jnp.arange(DECODE_STEPS, dtype=jnp.int32), samples)
    ).astype(jnp.float32)
    query_vectors = rotate(
        rms_scale(query_complete.reshape(row_count, head_count, HEAD_SIZE), query_norm_gain),
        position[:, None],
    ).astype(jnp.bfloat16)
    query_vectors = query_vectors.reshape(samples, DECODE_STEPS * head_count, HEAD_SIZE)
    keyval16 = lax.optimization_barrier(key_value_rows.astype(jnp.bfloat16)).reshape(
        row_count, 2, key_width
    )
    partner_keyval = from_partner(keyval16, "ad", 0)
    low_half = jnp.where(sub_part == 0, keyval16, partner_keyval)
    high_half = jnp.where(sub_part == 0, partner_keyval, keyval16)
    keyval16 = jnp.concatenate([low_half, high_half], axis=2)
    incoming_keys = rotate(
        rms_scale(keyval16[:, 0].astype(jnp.float32), key_norm_gain), position
    ).astype(jnp.bfloat16)
    incoming_keys = incoming_keys.reshape(samples, DECODE_STEPS, HEAD_SIZE)
    incoming_values = keyval16[:, 1].reshape(samples, DECODE_STEPS, HEAD_SIZE)
    own_lists = lax.dynamic_slice_in_dim(fanout, my_group * owned_count, owned_count, 0)
    listed = jnp.any(
        own_lists[:, :, None] == jnp.arange(groups, dtype=jnp.int32)[None, None, :], axis=1
    ).astype(jnp.int32)
    chosen = jnp.sum(listed * jnp.arange(owned_count, dtype=jnp.int32)[:, None], axis=0)
    block_len = prompt_cache.shape[2] // piece_count
    page_sets = prompt_cache.reshape(owned_count, device_shards, block_len, 2 * HEAD_SIZE)
    outgoing = jnp.take(page_sets, chosen, axis=0)
    arrived = lax.all_to_all(
        lax.all_to_all(outgoing, "grp", split_axis=0, concat_axis=0, tiled=True),
        "ad",
        split_axis=1,
        concat_axis=1,
        tiled=True,
    )
    arrived = arrived.reshape(groups, device_shards * block_len, 2 * HEAD_SIZE)
    attended = attend(
        query_vectors,
        arrived,
        generated_cache,
        suffix_lengths,
        incoming_keys,
        incoming_values,
        sub_part,
    )
    attended = attended.reshape(row_count, query_span_width)
    return lax.psum_scatter(
        jnp.dot(attended, output_weight, preferred_element_type=jnp.float32).astype(jnp.bfloat16),
        "ad",
        scatter_dimension=0,
        tiled=True,
    )


def solution(mesh):
    return jax.shard_map(
        shards,
        mesh=mesh,
        in_specs=(
            P(("grp", "ad"), None),
            P("grp", None, "ad", None),
            P("grp", "ad", None),
            P("grp"),
            P(),
            P(),
            P(None, "ad"),
            P(None, None, "ad"),
            P("ad", None),
            P("ad", None, None),
            P(None, None, "ad"),
            P(),
            P(),
        ),
        out_specs=P(("grp", "ad"), None),
        check_vma=False,
    )
```

profile of v0, /device:TPU:1, one launch (start us, length us, event | category | flops | bytes accessed | tf_op | source)
XLA Modules:
  0.0 668.7 jit_solution(11790854023871448572)
XLA Ops:
  8.2 6.8 %gather_fusion = bf16[8,16,128,256]{3,2,1,0:T(8,128)(2,1)} fusion(bf16[4,16,128,256]{3,2,1,0:T(8,128)(2,1)} %bitcast.61, s32[1024]{0:T(1024)S(1)} %pad_clamp_fusion), kind=kCustom, calls=%fused_computation | custom fusion | bytes 16777248 | tf_op jit(solution)/shard_map/jit(_take)/gather | solution.py:254
  14.9 7.5 %broadcast_select_fusion = bf16[8,16,128,256]{3,2,1,0:T(8,128)(2,1)} fusion(bf16[8,16,128,256]{3,2,1,0:T(8,128)(2,1)} %gather_fusion, pred[8]{0:T(512)(128)(4,1)S(1)} %compare_and_fusion), kind=kLoop, calls=%fused_computation.14 | loop fusion | flops 4194304 | bytes 16777224 | tf_op jit(solution)/shard_map/jit(_take)/select_n | solution.py:254
  22.4 100.9 %all_to_all.10 = bf16[8,16,128,256]{3,2,1,0:T(8,128)(2,1)} all-to-all(bf16[8,16,128,256]{3,2,1,0:T(8,128)(2,1)} %broadcast_select_fusion), channel_id=1, replica_groups=mesh['grp'=8,'ad'=16] {'grp'}, dimensions={0} | all-to-all | bytes 16777216 | tf_op jit(solution)/shard_map/all_to_all | solution.py:256
  123.3 7.7 %copy.82 = bf16[8,16,128,256]{3,2,0,1:T(8,128)(2,1)} copy(bf16[8,16,128,256]{3,2,1,0:T(8,128)(2,1)} %all_to_all.10) | data formatting | bytes 16777216 | tf_op jit(solution)/shard_map/all_to_all | solution.py:256
  131.0 6.8 %all-to-all-start.1 = ((bf16[8,16,128,256]{3,2,0,1:T(8,128)(2,1)}), bf16[8,16,128,256]{3,2,0,1:T(8,128)(2,1)}, u32[]{:S(2)}, u32[]{:S(2)}) async-start(bf16[8,16,128,256]{3,2,0,1:T(8,128)(2,1)} %copy.82), calls=%async_computation.1 | async-start | bytes 16777216 | tf_op jit(solution)/shard_map/all_to_all | solution.py:255
  138.7 137.2 %all-to-all-done.1 = bf16[8,16,128,256]{3,2,0,1:T(8,128)(2,1)} async-done(((bf16[8,16,128,256]{3,2,0,1:T(8,128)(2,1)}), bf16[8,16,128,256]{3,2,0,1:T(8,128)(2,1)}, u32[]{:S(2)}, u32[]{:S(2)}) %all-to-all-start.1) | async-done | bytes 8388640 | tf_op jit(solution)/shard_map/all_to_all | solution.py:255
  275.9 7.7 %copy.83 = bf16[8,16,128,256]{3,2,1,0:T(8,128)(2,1)} copy(bf16[8,16,128,256]{3,2,0,1:T(8,128)(2,1)} %all-to-all-done.1) | data formatting | bytes 16777216 | tf_op jit(solution)/shard_map/all_to_all | solution.py:255
  283.6 1.5 collective-permute-start.1
  286.1 1.1 constant_dynamic-update-slice_fusion.1
  287.3 195.1 %collective-permute-done.1 = bf16[128,16,256]{2,1,0:T(8,128)(2,1)S(1)} collective-permute-done((bf16[128,16,256]{2,1,0:T(8,128)(2,1)S(1)}, bf16[128,16,256]{2,1,0:T(8,128)(2,1)S(1)}, u32[]{:S(2)}, u32[]{:S(2)}) %collective-permute-start.1) | collective-permute-done | bytes 1048608 | tf_op jit(solution)/shard_map/ppermute | solution.py:28
  482.4 1.1 constant_dynamic-update-slice_fusion
  483.5 4.0 convolution_convert_fusion.1
  488.2 9.1 %copy.91 = bf16[5120,4,128]{0,2,1:T(8,128)(2,1)} copy(bf16[5120,4,128]{2,1,0:T(4,128)(2,1)} %all-gather.5.cloned.1.call-done) | data formatting | bytes 10485760 | tf_op jit(solution)/shard_map/reshape | solution.py:197
  497.3 6.5 fusion.20
  503.8 6.5 fusion.65
  510.3 2.0 multiply_reduce_fusion.1
  515.2 2.1 fusion.64
  517.4 15.4 %multiply_reduce_fusion = (f32[8,256]{1,0:T(8,128)S(1)}, f32[8,256,4096]{2,1,0:T(8,128)}) fusion(bf16[8,2048,256]{2,1,0:T(8,128)(2,1)} %bitcast.59, bf16[8,2048,256]{2,1,0:T(8,128)(2,1)} %collective-permute-done, bf16[8,256,64]{2,1,0:T(8,128)(2,1)S(1)} %bitcast.67, bf16[8,256,64]{2,1,0:T(8,128)(2,1)S(1)} %bitcast.64), kind=kOutput, calls=%fused_computation.2 | convolution fusion | flops 2182084608 | bytes 50864128 | tf_op jit(solution)/shard_map/pzl,pfl->pzf/dot_general | solution.py:67
  532.9 1.7 fusion.26
  535.3 14.0 %fusion = f32[8,256]{1,0:T(8,128)S(1)} fusion(f32[8,256,4096]{2,1,0:T(8,128)} %get-tuple-element.20, f32[8,256]{1,0:T(8,128)S(1)} %maximum_maximum_fusion.1), kind=kLoop, calls=%fused_computation.3 | loop fusion | flops 25163776 | bytes 33570816 | tf_op jit(solution)/shard_map/reduce_sum | solution.py:106
  549.7 17.4 %fusion.2 = f32[8,256,128]{2,1,0:T(8,128)} fusion(f32[8,256,4096]{2,1,0:T(8,128)} %get-tuple-element.20, f32[8,256]{1,0:T(8,128)S(1)} %maximum_maximum_fusion.1, bf16[8,2048,256]{2,1,0:T(8,128)(2,1)} %collective-permute-done, bf16[8,2048,256]{2,1,0:T(8,128)(2,1)} %bitcast.60), kind=kOutput, calls=%fused_computation.5 | convolution fusion | flops 2189426688 | bytes 51388416 | tf_op jit(solution)/shard_map/fup,fpe->fue/dot_general | solution.py:107
  567.1 1.8 divide_convert_fusion
  569.2 7.2 %convolution_convert_fusion = bf16[512,5120]{1,0:T(8,128)(2,1)} fusion(bf16[512,512]{1,0:T(8,128)(2,1)S(1)} %reshape.350, bf16[512,5120]{1,0:T(8,128)(2,1)} %param.21), kind=kOutput, calls=%fused_computation.15 | convolution fusion | flops 2686976000 | bytes 11010048 | tf_op jit(solution)/shard_map/dot_general | solution.py:274
  576.4 85.8 %reduce-scatter.2.cloned.1.call-done = bf16[32,5120]{1,0:T(8,128)(2,1)} async-done(((bf16[512,5120]{1,0:T(8,128)(2,1)}), bf16[32,5120]{1,0:T(8,128)(2,1)}) %reduce-scatter.2.cloned.1.call-update) | async-done | bytes 327696 | tf_op jit(solution)/shard_map/reduce_scatter | solution.py:273
  (81 shorter events, 8.5 us)
Async XLA Ops:
  6.5 477.0 %copy-start = (bf16[5120,2,64]{0,2,1:T(8,128)(2,1)S(1)}, bf16[5120,2,64]{0,2,1:T(8,128)(2,1)}, u32[]{:S(2)}) copy-start(bf16[5120,2,64]{0,2,1:T(8,128)(2,1)} %param.20) | copy-start | bytes 3932164
  6.5 477.0 %all-gather.3.cloned.1.call-start = ((), (), s32[]{:S(2)}) async-start(), calls=%async_computation.3 | async-start | bytes 5570560 | tf_op jit(solution)/shard_map/all_gather | solution.py:201
  131.0 144.9 %all-to-all-start.1 = ((bf16[8,16,128,256]{3,2,0,1:T(8,128)(2,1)}), bf16[8,16,128,256]{3,2,0,1:T(8,128)(2,1)}, u32[]{:S(2)}, u32[]{:S(2)}) async-start(bf16[8,16,128,256]{3,2,0,1:T(8,128)(2,1)} %copy.82), calls=%async_computation.1 | async-start | bytes 16777216 | tf_op jit(solution)/shard_map/all_to_all | solution.py:255
  137.8 350.4 %all-gather.5.cloned.1.call-start = ((), (), s32[]{:S(2)}) async-start(), calls=%async_computation.4 | async-start | bytes 5570560 | tf_op jit(solution)/shard_map/all_gather | solution.py:197
  138.6 145.0 %copy-start.2 = (bf16[128,16,256]{2,1,0:T(8,128)(2,1)S(1)}, bf16[128,16,256]{2,1,0:T(8,128)(2,1)}, u32[]{:S(2)}) copy-start(bf16[128,16,256]{2,1,0:T(8,128)(2,1)} %param.15) | copy-start | bytes 3145732
  138.6 146.5 %copy-start.4 = (s32[32,2]{0,1:T(2,128)S(1)}, s32[32,2]{0,1:T(2,128)}, u32[]{:S(2)}) copy-start(s32[32,2]{0,1:T(2,128)} %param.17) | copy-start | bytes 772
  138.6 146.9 %copy-start.8 = (s32[32]{0:T(128)S(1)}, s32[32]{0:T(128)}, u32[]{:S(2)}) copy-start(s32[32]{0:T(128)} %param.18) | copy-start | bytes 388
  138.6 147.0 %copy-start.7 = (s32[128]{0:T(128)S(1)}, s32[128]{0:T(128)}, u32[]{:S(2)}) copy-start(s32[128]{0:T(128)} %param.16) | copy-start | bytes 1540
  138.6 523.5 %reduce-scatter.2.cloned.1.call-start = ((), (), s32[]{:S(2)}) async-start(), calls=%async_computation.5 | async-start | bytes 5570560 | tf_op jit(solution)/shard_map/reduce_scatter | solution.py:273
  283.6 233.8 %collective-permute-start = (bf16[8,2048,256]{2,1,0:T(8,128)(2,1)}, bf16[8,2048,256]{2,1,0:T(8,128)(2,1)}, u32[]{:S(2)}, u32[]{:S(2)}) collective-permute-start(bf16[8,2048,256]{2,1,0:T(8,128)(2,1)} %bitcast.58), channel_id=1, source_target_pairs={{0,1},{1,0},{2,3},{3,2},{4,5},{5,4},{6,7},{7,6},{8,9},{9,8},{10,11... | collective-permute-start | bytes 25165832 | tf_op jit(solution)/shard_map/ppermute | solution.py:28
  283.6 198.8 %collective-permute-start.1 = (bf16[128,16,256]{2,1,0:T(8,128)(2,1)S(1)}, bf16[128,16,256]{2,1,0:T(8,128)(2,1)S(1)}, u32[]{:S(2)}, u32[]{:S(2)}) collective-permute-start(bf16[128,16,256]{2,1,0:T(8,128)(2,1)S(1)} %copy-done.2), channel_id=1, source_target_pairs={{0,1},{1,0},{2,3},{3,2},{4,5},{5,4},{6,7},{7,6},{8,9},{9,8},{10,11... | collective-permute-start | bytes 3145736 | tf_op jit(solution)/shard_map/ppermute | solution.py:28
  487.6 24.9 %collective-permute-start.2 = (bf16[512,2,64]{0,2,1:T(8,128)(2,1)S(1)}, bf16[512,2,64]{0,2,1:T(8,128)(2,1)S(1)}, u32[]{:S(2)}, u32[]{:S(2)}) collective-permute-start(bf16[512,2,64]{0,2,1:T(8,128)(2,1)S(1)} %bitcast.68), channel_id=1, source_target_pairs={{0,1},{1,0},{2,3},{3,2},{4,5},{5,4},{6,7},{7,6},{8,9},{9,8},{10,11... | collective-permute-start | bytes 393224 | tf_op jit(solution)/shard_map/ppermute | solution.py:28
  503.7 6.6 copy-start.3
  503.8 8.5 %copy-start.5 = (f32[128]{0:T(128)S(1)}, f32[128]{0:T(128)}, u32[]{:S(2)}) copy-start(f32[128]{0:T(128)} %param.24) | copy-start | bytes 1540
  503.8 9.0 %copy-start.6 = (f32[128]{0:T(128)S(1)}, f32[128]{0:T(128)}, u32[]{:S(2)}) copy-start(f32[128]{0:T(128)} %param.25) | copy-start | bytes 1540
  568.9 93.3 %copy-start.1 = (bf16[5120,2,64]{0,2,1:T(8,128)(2,1)S(1)}, bf16[5120,2,64]{0,2,1:T(8,128)(2,1)}, u32[]{:S(2)}) copy-start(bf16[5120,2,64]{0,2,1:T(8,128)(2,1)} %param.20) | copy-start | bytes 3932164
Sparse Core Ops, SparseCore 0:
  9.5 59.4 all-gather.2
  140.8 143.4 all-gather.4
  576.5 85.6 reduce-scatter.1
where the time goes:
time: 670 us; the launch traced here: 669 us
  waiting for transfers between devices  420 us (63%)
  blocking collectives  101 us (15%)
  matrix products  65.1 us (10%)
  local copies, waits for them, and re-layouts  36.5 us (5%)
  other arithmetic  24.2 us (4%)
  between operations  13.5 us (2%)
  starting transfers between devices  8.91 us (1%)
    ppermute x3, waiting for transfers between devices, from_partner(): return lax.ppermute(block, axis, route)  195 us
    all_to_all x1, waiting for transfers between devices, shards(): lax.all_to_all(lax.all_to_all(outgoing, 'grp', split_axis=0, concat_axis=...  137 us
    all_to_all x1, blocking collectives, shards(): lax.all_to_all(outgoing, 'grp', split_axis=0, concat_axis=0, tiled=True)  101 us
    reduce_scatter x1, waiting for transfers between devices, shards(): lax.psum_scatter(jnp.dot(attended, output_weight, preferred_element_type=...  85.8 us
    dot_general x1, matrix products, weigh_parts(): jnp.einsum('fup,fpe->fue', spread.astype(jnp.bfloat16), value_list[0], pr...  17.4 us
    dot_general x1, matrix products, score_parts(): jnp.einsum('pzl,pfl->pzf', per_slot_order, prompt_keys, preferred_element...  15.4 us
    reduce_sum x1, other arithmetic, weigh_parts(): denominator = jnp.sum(spread, axis=-1).reshape(samples, -1)  14 us
  transfers between devices with their start and end apart: 7, of which 3 were waited for; matrix products, arithmetic and copies ran while one was open for 10% of the time, Pallas kernels for 0%

commit v1 on v0

v1 whole, which is shorter than its diff:
```python
import functools

import jax
import jax.numpy as jnp
from jax import lax
from jax.experimental import pallas as pl
from jax.experimental.pallas import tpu as pltpu
from jax.sharding import PartitionSpec as P

MODEL_WIDTH = 5120
KEY_VALUE_HEADS = 8
HEAD_SIZE = 128
ADAPTER_RANK = 128
FAN = 2
DECODE_STEPS = 4
ADAPTER_COUNT = 4
PROMPT_TOKENS = 4096
GROUPS = 8
SHARDS = 16
OWNED = 4
SLOT_SAMPLES = 16
SLOT_ROWS = SLOT_SAMPLES * DECODE_STEPS
HALF_ROWS = SLOT_ROWS // 2
ROWS = GROUPS * SLOT_ROWS
OWN_HEADS = 4
OWN_WIDTH = OWN_HEADS * HEAD_SIZE
HEAD_FAN = 2 * OWN_HEADS
SENT_WIDTH = OWN_WIDTH + HEAD_SIZE
BACK_WIDTH = HEAD_FAN * HEAD_SIZE + HEAD_SIZE

theta_base = 1000000.0
norm_eps = 1e-06
masked_low = -1e30
exponent_scale = HEAD_SIZE**-0.5 * 1.4426950408889634

ROLE_GROUPS = [[0, 3, 4, 7, 8, 11, 12, 15], [1, 2, 5, 6, 9, 10, 13, 14]]
HEAD_GROUPS = [
    [group * SHARDS + 2 * head + half for group in range(GROUPS) for half in range(2)]
    for head in range(KEY_VALUE_HEADS)
]
PARTNERS = [(shard, shard ^ 1) for shard in range(SHARDS)]


def slot_prompts(fanout, groups, owned_count):
    listed = jnp.any(
        fanout[:, :, None] == jnp.arange(groups, dtype=jnp.int32)[None, None, :], axis=1
    )
    listed = listed.astype(jnp.int32).reshape(groups, owned_count, groups)
    return jnp.sum(listed * jnp.arange(owned_count, dtype=jnp.int32)[None, :, None], axis=1)


def angle_tables(position):
    half_len = HEAD_SIZE // 2
    inverse = theta_base ** (-2.0 * jnp.arange(half_len, dtype=jnp.float32) / HEAD_SIZE)
    angles = position[..., None] * inverse
    cosine = jnp.cos(angles)
    sine = jnp.sin(angles)
    return (
        jnp.concatenate([cosine, cosine], axis=-1),
        jnp.concatenate([-sine, sine], axis=-1),
    )


def norm_rotate(vector, gain, cosine, sine):
    mean_sq = jnp.mean(vector * vector, axis=-1, keepdims=True)
    scaled = vector * lax.rsqrt(mean_sq + norm_eps) * gain
    return scaled * cosine + pltpu.roll(scaled, HEAD_SIZE // 2, 1) * sine


def dot_nt(left, right):
    return lax.dot_general(
        left, right, (((1,), (1,)), ((), ())), preferred_element_type=jnp.float32
    )


def project_kernel(
    task_ref,
    tokens_ref,
    query_ref,
    keyval_ref,
    rank_ref,
    up_ref,
    cos_ref,
    sin_ref,
    gain_ref,
    out_ref,
    query_sum,
    keyval_sum,
):
    step = pl.program_id(0)

    @pl.when(step == 0)
    def _():
        query_sum[...] = jnp.zeros_like(query_sum)
        keyval_sum[...] = jnp.zeros_like(keyval_sum)

    part = tokens_ref[...]
    query_sum[...] += jnp.dot(part, query_ref[...], preferred_element_type=jnp.float32)
    keyval_sum[...] += dot_nt(part, keyval_ref[...])

    @pl.when(step == pl.num_programs(0) - 1)
    def _():
        for slot in range(GROUPS):
            rows = slice(slot * SLOT_ROWS, (slot + 1) * SLOT_ROWS)
            query = query_sum[rows, :] + jnp.dot(
                rank_ref[rows, :], up_ref[task_ref[slot]], preferred_element_type=jnp.float32
            )
            for head in range(OWN_HEADS):
                lanes = slice(head * HEAD_SIZE, (head + 1) * HEAD_SIZE)
                out_ref[rows, lanes] = norm_rotate(
                    query[:, lanes], gain_ref[...], cos_ref[rows, :], sin_ref[rows, :]
                ).astype(jnp.bfloat16)
        out_ref[:, OWN_WIDTH:] = keyval_sum[...].astype(jnp.bfloat16)


def project(tasks, tokens, query_weight, keyval_weight, low_rank, up_maps, cosine, sine, gain):
    tile = 512
    whole = lambda *shape: pl.BlockSpec(shape, lambda k, tasks: (0,) * len(shape))
    return pl.pallas_call(
        project_kernel,
        grid_spec=pltpu.PrefetchScalarGridSpec(
            num_scalar_prefetch=1,
            grid=(MODEL_WIDTH // tile,),
            in_specs=[
                pl.BlockSpec((ROWS, tile), lambda k, tasks: (0, k)),
                pl.BlockSpec((tile, OWN_WIDTH), lambda k, tasks: (k, 0)),
                pl.BlockSpec((HEAD_SIZE, tile), lambda k, tasks: (0, k)),
                whole(ROWS, ADAPTER_RANK),
                whole(ADAPTER_COUNT, ADAPTER_RANK, OWN_WIDTH),
                whole(ROWS, HEAD_SIZE),
                whole(ROWS, HEAD_SIZE),
                whole(1, HEAD_SIZE),
            ],
            out_specs=whole(ROWS, SENT_WIDTH),
            scratch_shapes=[
                pltpu.VMEM((ROWS, OWN_WIDTH), jnp.float32),
                pltpu.VMEM((ROWS, HEAD_SIZE), jnp.float32),
            ],
        ),
        out_shape=jax.ShapeDtypeStruct((ROWS, SENT_WIDTH), jnp.bfloat16),
        compiler_params=pltpu.CompilerParams(vmem_limit_bytes=40 * 2**20),
        cost_estimate=pl.CostEstimate(
            flops=2 * ROWS * MODEL_WIDTH * SENT_WIDTH, bytes_accessed=13_000_000, transcendentals=0
        ),
        name="project",
    )(tasks, tokens, query_weight, keyval_weight, low_rank, up_maps, cosine, sine, gain)


def attend_kernel(
    order_ref,
    local_ref,
    place_ref,
    sent_ref,
    page_ref,
    suffix_ref,
    cos_ref,
    sin_ref,
    gain_ref,
    out_ref,
):
    half = place_ref[0]
    flip = place_ref[1]
    span = GROUPS * PROMPT_TOKENS // SHARDS
    pages = page_ref[...].reshape(span, 2 * HEAD_SIZE)
    keys = pages[:, :HEAD_SIZE]
    values = jnp.concatenate(
        [jnp.ones((span, HEAD_SIZE), jnp.bfloat16), pages[:, HEAD_SIZE:]], axis=1
    )
    low_part = sent_ref[0, 0, :, OWN_WIDTH:].astype(jnp.float32)
    high_part = sent_ref[0, 1, :, OWN_WIDTH:].astype(jnp.float32)
    lane = lax.broadcasted_iota(jnp.int32, (SLOT_ROWS, HEAD_SIZE), 1)
    low_lanes = lane < HEAD_SIZE // 2
    new_keys = jnp.where(low_lanes, low_part, pltpu.roll(high_part, HEAD_SIZE // 2, 1))
    new_values = jnp.where(low_lanes, pltpu.roll(low_part, HEAD_SIZE // 2, 1), high_part)
    new_keys = norm_rotate(new_keys, gain_ref[...], cos_ref[0], sin_ref[0])
    suffix_rows = SLOT_SAMPLES * 16
    extra = suffix_rows + 2 * SLOT_ROWS
    suffix = suffix_ref[0, :suffix_rows, :]
    zeros = jnp.zeros((SLOT_ROWS, HEAD_SIZE), jnp.bfloat16)
    extra_keys = jnp.concatenate(
        [suffix[:, :HEAD_SIZE], new_keys.astype(jnp.bfloat16), zeros], axis=0
    )
    extra_values = jnp.concatenate(
        [suffix[:, HEAD_SIZE:], new_values.astype(jnp.bfloat16), zeros], axis=0
    )
    extra_values = jnp.concatenate(
        [jnp.ones((extra, HEAD_SIZE), jnp.bfloat16), extra_values], axis=1
    )
    lengths = suffix_ref[0, suffix_rows:, :].astype(jnp.float32)
    sample_of = lax.broadcasted_iota(jnp.int32, (SLOT_SAMPLES, suffix_rows), 0)
    column_sample = lax.broadcasted_iota(jnp.int32, (SLOT_SAMPLES, suffix_rows), 1) // 16
    column_length = jnp.sum(
        jnp.where(sample_of == column_sample, lengths, 0.0), axis=0, keepdims=True
    )
    row = lax.broadcasted_iota(jnp.int32, (SLOT_ROWS, suffix_rows), 0)
    column = lax.broadcasted_iota(jnp.int32, (SLOT_ROWS, suffix_rows), 1)
    suffix_seen = (row // DECODE_STEPS == column // 16) & (
        (half * 16 + column % 16).astype(jnp.float32) < column_length
    )
    row = lax.broadcasted_iota(jnp.int32, (SLOT_ROWS, 2 * SLOT_ROWS), 0)
    column = lax.broadcasted_iota(jnp.int32, (SLOT_ROWS, 2 * SLOT_ROWS), 1)
    new_seen = (
        (row // DECODE_STEPS == column // DECODE_STEPS)
        & (column % DECODE_STEPS <= row % DECODE_STEPS)
        & (column // HALF_ROWS == half)
    )
    bias = jnp.concatenate(
        [jnp.where(suffix_seen, 0.0, masked_low), jnp.where(new_seen, 0.0, masked_low)], axis=1
    )
    pair_bias = jnp.concatenate([bias, bias], axis=0)
    logs = jnp.zeros((SLOT_ROWS, HEAD_SIZE), jnp.float32)
    for first in range(0, HEAD_FAN, 2):
        source, start = divmod(first, OWN_HEADS)
        start = start * HEAD_SIZE
        query = jnp.concatenate(
            [
                sent_ref[0, source, :, start : start + HEAD_SIZE],
                sent_ref[0, source, :, start + HEAD_SIZE : start + 2 * HEAD_SIZE],
            ],
            axis=0,
        )
        prefix_score = dot_nt(query, keys)
        extra_score = dot_nt(query, extra_keys) + pair_bias
        peak = jnp.maximum(
            jnp.max(prefix_score, axis=-1, keepdims=True),
            jnp.max(extra_score, axis=-1, keepdims=True),
        )
        scaled_peak = peak * exponent_scale
        prefix_weight = jnp.exp2(prefix_score * exponent_scale - scaled_peak).astype(jnp.bfloat16)
        extra_weight = jnp.exp2(extra_score * exponent_scale - scaled_peak).astype(jnp.bfloat16)
        total = jnp.dot(prefix_weight, values, preferred_element_type=jnp.float32) + jnp.dot(
            extra_weight, extra_values, preferred_element_type=jnp.float32
        )
        denominator = total[:, :HEAD_SIZE]
        attended = total[:, HEAD_SIZE:] / denominator
        log_sum = scaled_peak + jnp.log2(denominator)
        for index in range(2):
            head = first + index
            rows = slice(index * SLOT_ROWS, (index + 1) * SLOT_ROWS)
            top = attended[index * SLOT_ROWS : index * SLOT_ROWS + HALF_ROWS].astype(jnp.bfloat16)
            low = attended[index * SLOT_ROWS + HALF_ROWS : (index + 1) * SLOT_ROWS].astype(
                jnp.bfloat16
            )
            lanes = slice(head * HEAD_SIZE, (head + 1) * HEAD_SIZE)
            out_ref[0, 0, :, lanes] = jnp.where(flip == 0, top, low)
            out_ref[0, 1, :, lanes] = jnp.where(flip == 0, low, top)
            logs = jnp.where(lane == head, log_sum[rows], logs)
    high_term = logs.astype(jnp.bfloat16).astype(jnp.float32)
    rest = logs - high_term
    mid_term = rest.astype(jnp.bfloat16).astype(jnp.float32)
    low_term = rest - mid_term
    packed = (
        high_term + pltpu.roll(mid_term, HEAD_FAN, 1) + pltpu.roll(low_term, 2 * HEAD_FAN, 1)
    ).astype(jnp.bfloat16)
    top = packed[:HALF_ROWS]
    low = packed[HALF_ROWS:]
    out_ref[0, 0, :, HEAD_FAN * HEAD_SIZE :] = jnp.where(flip == 0, top, low)
    out_ref[0, 1, :, HEAD_FAN * HEAD_SIZE :] = jnp.where(flip == 0, low, top)


def attend(order, local, place, sent, pages, suffix, cosine, sine, gain):
    block = PROMPT_TOKENS // SHARDS
    return pl.pallas_call(
        attend_kernel,
        grid_spec=pltpu.PrefetchScalarGridSpec(
            num_scalar_prefetch=3,
            grid=(GROUPS,),
            in_specs=[
                pl.BlockSpec((1, 2, SLOT_ROWS, SENT_WIDTH), lambda i, o, l, p: (o[i], 0, 0, 0)),
                pl.BlockSpec(
                    (GROUPS, 1, block, 2 * HEAD_SIZE), lambda i, o, l, p: (0, l[i], 0, 0)
                ),
                pl.BlockSpec(
                    (1, suffix.shape[1], 2 * HEAD_SIZE), lambda i, o, l, p: (o[i], 0, 0)
                ),
                pl.BlockSpec((1, SLOT_ROWS, HEAD_SIZE), lambda i, o, l, p: (o[i], 0, 0)),
                pl.BlockSpec((1, SLOT_ROWS, HEAD_SIZE), lambda i, o, l, p: (o[i], 0, 0)),
                pl.BlockSpec((1, HEAD_SIZE), lambda i, o, l, p: (0, 0)),
            ],
            out_specs=pl.BlockSpec(
                (1, 2, HALF_ROWS, BACK_WIDTH), lambda i, o, l, p: (o[i], 0, 0, 0)
            ),
        ),
        out_shape=jax.ShapeDtypeStruct((GROUPS, 2, HALF_ROWS, BACK_WIDTH), jnp.bfloat16),
        compiler_params=pltpu.CompilerParams(vmem_limit_bytes=48 * 2**20),
        cost_estimate=pl.CostEstimate(
            flops=2 * GROUPS * 512 * 2432 * 384,
            bytes_accessed=8_000_000,
            transcendentals=GROUPS * 512 * 2432,
        ),
        name="attend",
    )(order, local, place, sent, pages, suffix, cosine, sine, gain)


def output_kernel(place_ref, back_ref, own_ref, other_ref, out_ref, mixed):
    half = place_ref[0]
    rows = GROUPS * HALF_ROWS

    @pl.when(pl.program_id(0) == 0)
    def _():
        lane = lax.broadcasted_iota(jnp.int32, (rows, HEAD_SIZE), 1)

        def log_of(source):
            packed = back_ref[:, source, :, HEAD_FAN * HEAD_SIZE :]
            packed = packed.reshape(rows, HEAD_SIZE).astype(jnp.float32)
            return (
                packed
                + pltpu.roll(packed, HEAD_SIZE - HEAD_FAN, 1)
                + pltpu.roll(packed, HEAD_SIZE - 2 * HEAD_FAN, 1)
            )

        first_log = log_of(0)
        second_log = log_of(1)
        peak = jnp.maximum(first_log, second_log)
        first_part = jnp.exp2(first_log - peak)
        second_part = jnp.exp2(second_log - peak)
        both = first_part + second_part
        first_part = first_part / both
        second_part = second_part / both

        def attended(head):
            lanes = slice(head * HEAD_SIZE, (head + 1) * HEAD_SIZE)
            first = back_ref[:, 0, :, lanes].reshape(rows, HEAD_SIZE).astype(jnp.float32)
            second = back_ref[:, 1, :, lanes].reshape(rows, HEAD_SIZE).astype(jnp.float32)
            return (
                first * first_part[:, head : head + 1] + second * second_part[:, head : head + 1]
            ).astype(jnp.bfloat16)

        for head in range(OWN_HEADS):
            low = attended(head)
            high = attended(head + OWN_HEADS)
            lanes = slice(head * HEAD_SIZE, (head + 1) * HEAD_SIZE)
            mixed[0, :, lanes] = jnp.where(half == 0, low, high)
            mixed[1, :, lanes] = jnp.where(half == 0, high, low)

    out_ref[...] = (
        jnp.dot(mixed[0], own_ref[...], preferred_element_type=jnp.float32)
        + jnp.dot(mixed[1], other_ref[...], preferred_element_type=jnp.float32)
    ).astype(jnp.bfloat16)


def output_part(place, back, own_weight, other_weight):
    tile = 1024
    rows = GROUPS * HALF_ROWS
    return pl.pallas_call(
        output_kernel,
        grid_spec=pltpu.PrefetchScalarGridSpec(
            num_scalar_prefetch=1,
            grid=(MODEL_WIDTH // tile,),
            in_specs=[
                pl.BlockSpec((GROUPS, 2, HALF_ROWS, BACK_WIDTH), lambda n, p: (0, 0, 0, 0)),
                pl.BlockSpec((OWN_WIDTH, tile), lambda n, p: (0, n)),
                pl.BlockSpec((OWN_WIDTH, tile), lambda n, p: (0, n)),
            ],
            out_specs=pl.BlockSpec((rows, tile), lambda n, p: (0, n)),
            scratch_shapes=[pltpu.VMEM((2, rows, OWN_WIDTH), jnp.bfloat16)],
        ),
        out_shape=jax.ShapeDtypeStruct((rows, MODEL_WIDTH), jnp.bfloat16),
        compiler_params=pltpu.CompilerParams(vmem_limit_bytes=40 * 2**20),
        cost_estimate=pl.CostEstimate(
            flops=2 * rows * MODEL_WIDTH * 1024, bytes_accessed=14_000_000, transcendentals=0
        ),
        name="output_part",
    )(place, back, own_weight, other_weight)


def swap(block, axes, groups=None):
    return lax.all_to_all(
        block, axes, split_axis=0, concat_axis=0, tiled=True, axis_index_groups=groups
    )


def shards(
    tokens,
    prompt_cache,
    generated_cache,
    suffix_lengths,
    fanout,
    prompt_adapter,
    query_weight,
    key_value_weight,
    output_weight,
    adapter_down_maps,
    adapter_up_maps,
    query_norm_gain,
    key_norm_gain,
):
    group = lax.axis_index("grp")
    shard = lax.axis_index("ad")
    head = shard // 2
    half = shard % 2
    local_table = slot_prompts(fanout, GROUPS, OWNED)

    arrived = swap(jnp.swapaxes(prompt_cache, 0, 1), "ad", ROLE_GROUPS)
    part_rows = lax.all_gather(tokens, "ad", axis=0, tiled=True)

    slot_suffix = generated_cache.reshape(GROUPS, SLOT_SAMPLES * 16, 2 * HEAD_SIZE)
    slot_lengths = suffix_lengths.reshape(GROUPS, SLOT_SAMPLES, 1).astype(jnp.bfloat16)
    slot_suffix = jnp.concatenate(
        [slot_suffix, jnp.broadcast_to(slot_lengths, (GROUPS, SLOT_SAMPLES, 2 * HEAD_SIZE))], axis=1
    )
    suffix = swap(slot_suffix, "grp")

    slice_rows = OWN_WIDTH // GROUPS
    weight_slice = lax.dynamic_slice_in_dim(output_weight, group * slice_rows, slice_rows, 0)
    other_weight = lax.all_gather(
        lax.ppermute(weight_slice, "ad", PARTNERS), "grp", axis=0, tiled=True
    )

    owners = jnp.arange(GROUPS, dtype=jnp.int32)
    local_of_slot = lax.dynamic_index_in_dim(local_table, group, 1, keepdims=False)
    prompts = owners * OWNED + local_of_slot
    hit = prompts[:, None] == jnp.arange(prompt_adapter.shape[0], dtype=jnp.int32)[None, :]
    tasks = jnp.sum(hit.astype(jnp.int32) * prompt_adapter[None, :], axis=1)
    own_rows = tokens.shape[0]
    columns = swap(jnp.swapaxes(tokens.reshape(own_rows, SHARDS, -1), 0, 1), "ad")
    rank_all = jnp.dot(
        columns.reshape(ROWS, -1),
        adapter_down_maps.reshape(-1, ADAPTER_COUNT * ADAPTER_RANK),
        preferred_element_type=jnp.float32,
    ).reshape(GROUPS, SLOT_ROWS, ADAPTER_COUNT, ADAPTER_RANK)
    chosen = (tasks[:, None] == jnp.arange(ADAPTER_COUNT, dtype=jnp.int32)[None, :]).astype(
        jnp.float32
    )
    rank_part = jnp.sum(rank_all * chosen[:, None, :, None], axis=2)
    rank_rows = jnp.sum(swap(rank_part.reshape(SHARDS, own_rows, ADAPTER_RANK), "ad"), axis=0)
    rank_rows = rank_rows.astype(jnp.bfloat16)
    low_rank = swap(jnp.broadcast_to(rank_rows[None], (SHARDS,) + rank_rows.shape), "ad")

    steps = jnp.arange(DECODE_STEPS, dtype=jnp.int32)
    position = (PROMPT_TOKENS + suffix_lengths[:, None] + steps[None, :]).astype(jnp.float32)
    cosine, sine = angle_tables(position.reshape(ROWS))
    sent = project(
        tasks,
        part_rows,
        query_weight,
        key_value_weight.transpose(1, 2, 0).reshape(HEAD_SIZE, MODEL_WIDTH),
        low_rank.reshape(ROWS, ADAPTER_RANK),
        adapter_up_maps,
        cosine,
        sine,
        query_norm_gain.reshape(1, HEAD_SIZE),
    )
    received = swap(
        jnp.broadcast_to(
            sent.reshape(GROUPS, 1, SLOT_ROWS, SENT_WIDTH), (GROUPS, 2, SLOT_ROWS, SENT_WIDTH)
        ).reshape(2 * GROUPS, SLOT_ROWS, SENT_WIDTH),
        ("grp", "ad"),
        HEAD_GROUPS,
    ).reshape(GROUPS, 2, SLOT_ROWS, SENT_WIDTH)

    local = lax.dynamic_index_in_dim(local_table, group, 0, keepdims=False)
    rank_key = local * GROUPS + owners
    spot = jnp.sum((rank_key[None, :] < rank_key[:, None]).astype(jnp.int32), axis=1)
    placed = (spot[None, :] == owners[:, None]).astype(jnp.int32)
    order = jnp.sum(placed * owners[None, :], axis=1)
    local_sorted = jnp.sum(placed * local[None, :], axis=1)
    flip = (head + group) % 2
    place = jnp.stack([half, flip]).astype(jnp.int32)
    far_lengths = suffix[:, SLOT_SAMPLES * 16 :, 0].astype(jnp.float32)
    far_position = PROMPT_TOKENS + far_lengths[:, :, None] + steps.astype(jnp.float32)
    far_cosine, far_sine = angle_tables(far_position.reshape(GROUPS, SLOT_ROWS))
    partial = attend(
        order,
        local_sorted,
        place,
        received,
        arrived,
        suffix,
        far_cosine,
        far_sine,
        key_norm_gain.reshape(1, HEAD_SIZE),
    )
    back = swap(
        partial.reshape(2 * GROUPS, HALF_ROWS, BACK_WIDTH), ("grp", "ad"), HEAD_GROUPS
    ).reshape(GROUPS, 2, HALF_ROWS, BACK_WIDTH)
    product = output_part(place, back, output_weight, other_weight)
    blocks = swap(product.reshape(GROUPS, HALF_ROWS, MODEL_WIDTH), "ad", ROLE_GROUPS)
    return jnp.sum(blocks.astype(jnp.float32), axis=0).astype(jnp.bfloat16)


def solution(mesh):
    return jax.shard_map(
        shards,
        mesh=mesh,
        in_specs=(
            P(("grp", "ad"), None),
            P("grp", None, "ad", None),
            P("grp", "ad", None),
            P("grp"),
            P(),
            P(),
            P(None, "ad"),
            P(None, None, "ad"),
            P("ad", None),
            P("ad", None, None),
            P(None, None, "ad"),
            P(),
            P(),
        ),
        out_specs=P(("grp", "ad"), None),
        check_vma=False,
    )
```

time: 670 us -> 283 us (0.42)
  waiting for transfers between devices: 420 us -> 121 us
  blocking collectives: 101 us -> 36.7 us
  matrix products: 65.1 us -> 1.14 us
  Pallas kernels: 0 us -> 35.9 us
  starting transfers between devices: 8.91 us -> 43.3 us
  other arithmetic: 24.2 us -> 6.45 us
  local copies, waits for them, and re-layouts: 36.5 us -> 23.6 us
    ppermute x3 -> x1, waiting for transfers between devices: 195 us -> 13.9 us  [shards(): lax.ppermute(weight_slice, 'ad', PARTNERS)]
    reduce_scatter x1 -> x0, waiting for transfers between devices: 85.8 us -> none  [shards(): lax.psum_scatter(jnp.dot(attended, output_weight, preferred_element_type=...]
    all_to_all x1, blocking collectives: 101 us -> 36.7 us  [swap(): lax.all_to_all(block, axes, split_axis=0, concat_axis=0, tiled=True, axis...]
    dot_general x11 -> x1, matrix products: 65.1 us -> 1.14 us  [shards(): jnp.dot(columns.reshape(ROWS, -1), adapter_down_maps.reshape(-1, ADAPTER_...]
    pallas_call x0 -> x3, Pallas kernels: none -> 35.9 us  [the longest x1 20 us: attend(): pl.pallas_call(attend_kernel, grid_spec=pltpu.PrefetchScalarGridSpec(num_...]
    all_to_all x1 -> x7, starting transfers between devices: 6.82 us -> 41.1 us  [swap(): lax.all_to_all(block, axes, split_axis=0, concat_axis=0, tiled=True, axis...]
    all_to_all x1 -> x7, waiting for transfers between devices: 137 us -> 106 us  [swap(): lax.all_to_all(block, axes, split_axis=0, concat_axis=0, tiled=True, axis...]
    unnamed x19 -> x35, local copies, waits for them, and re-layouts: 1.15 us -> 18.7 us
  transfers between devices with their start and end apart: 7 -> 10, of which waited for: 3 -> 8; matrix products, arithmetic and copies ran while one was open for 10% -> 6% of each run, Pallas kernels for 0% -> 11%
where the time goes in v1:
time: 283 us; the launch traced here: 282 us
  waiting for transfers between devices  121 us (43%)
  starting transfers between devices  43.3 us (15%)
  blocking collectives  36.7 us (13%)
  Pallas kernels  35.9 us (13%)
  local copies, waits for them, and re-layouts  23.6 us (8%)
  between operations  13.7 us (5%)
  other arithmetic  6.45 us (2%)
    all_to_all x7, waiting for transfers between devices, swap(): lax.all_to_all(block, axes, split_axis=0, concat_axis=0, tiled=True, axis...  106 us
    all_to_all x7, starting transfers between devices, swap(): lax.all_to_all(block, axes, split_axis=0, concat_axis=0, tiled=True, axis...  41.1 us
    all_to_all x1, blocking collectives, swap(): lax.all_to_all(block, axes, split_axis=0, concat_axis=0, tiled=True, axis...  36.7 us
    pallas_call x1, Pallas kernels, attend(): pl.pallas_call(attend_kernel, grid_spec=pltpu.PrefetchScalarGridSpec(num_...  20 us
    unnamed x35, local copies, waits for them, and re-layouts  18.7 us
    ppermute x1, waiting for transfers between devices, shards(): lax.ppermute(weight_slice, 'ad', PARTNERS)  13.9 us
    pallas_call x1, Pallas kernels, project(): pl.pallas_call(project_kernel, grid_spec=pltpu.PrefetchScalarGridSpec(num...  10 us
    pallas_call x1, Pallas kernels, output_part(): pl.pallas_call(output_kernel, grid_spec=pltpu.PrefetchScalarGridSpec(num_...  5.81 us
  transfers between devices with their start and end apart: 10, of which 8 were waited for; matrix products, arithmetic and copies ran while one was open for 6% of the time, Pallas kernels for 11%

profile of v1, /device:TPU:1, one launch (start us, length us, event | category | flops | bytes accessed | tf_op | source)
XLA Modules:
  0.0 281.8 jit_solution(8551093490050551477)
XLA Ops:
  10.6 13.9 %collective-permute-done = bf16[64,5120]{1,0:T(8,128)(2,1)S(1)} collective-permute-done((bf16[64,5120]{1,0:T(8,128)(2,1)S(1)}, bf16[64,5120]{1,0:T(8,128)(2,1)S(1)}, u32[]{:S(2)}, u32[]{:S(2)}) %collective-permute-start) | collective-permute-done | bytes 655392 | tf_op jit(solution)/shard_map/ppermute | solution.py:407
  26.6 7.3 %all-to-all-start = ((bf16[16,32,320]{2,1,0:T(8,128)(2,1)}), bf16[16,32,320]{2,1,0:T(8,128)(2,1)S(1)}, u32[]{:S(2)}, u32[]{:S(2)}) async-start(bf16[16,32,320]{2,1,0:T(8,128)(2,1)} %bitcast.51), calls=%async_computation | async-start | bytes 786432 | tf_op jit(solution)/shard_map/all_to_all | solution.py:368
  34.5 7.7 %all-to-all-done = bf16[16,32,320]{2,1,0:T(8,128)(2,1)S(1)} async-done(((bf16[16,32,320]{2,1,0:T(8,128)(2,1)}), bf16[16,32,320]{2,1,0:T(8,128)(2,1)S(1)}, u32[]{:S(2)}, u32[]{:S(2)}) %all-to-all-start) | async-done | bytes 327712 | tf_op jit(solution)/shard_map/all_to_all | solution.py:368
  43.4 3.5 %all-to-all-start.1 = ((f32[16,32,128]{2,1,0:T(8,128)}), f32[16,32,128]{2,1,0:T(8,128)S(1)}, u32[]{:S(2)}, u32[]{:S(2)}) async-start(f32[16,32,128]{2,1,0:T(8,128)} %bitcast.13), calls=%async_computation.1 | async-start | bytes 524288 | tf_op jit(solution)/shard_map/all_to_all | solution.py:368
  47.0 10.2 %all-to-all-done.1 = f32[16,32,128]{2,1,0:T(8,128)S(1)} async-done(((f32[16,32,128]{2,1,0:T(8,128)}), f32[16,32,128]{2,1,0:T(8,128)S(1)}, u32[]{:S(2)}, u32[]{:S(2)}) %all-to-all-start.1) | async-done | bytes 262176 | tf_op jit(solution)/shard_map/all_to_all | solution.py:368
  57.9 3.5 %all-to-all-start.2 = ((bf16[16,32,128]{2,1,0:T(8,128)(2,1)}), bf16[16,32,128]{2,1,0:T(8,128)(2,1)S(1)}, u32[]{:S(2)}, u32[]{:S(2)}) async-start(bf16[16,32,128]{2,1,0:T(8,128)(2,1)} %broadcast_in_dim.8), calls=%async_computation.2 | async-start | bytes 262144 | tf_op jit(solution)/shard_map/all_to_all | solution.py:368
  62.6 7.0 %all-to-all-done.2 = bf16[16,32,128]{2,1,0:T(8,128)(2,1)S(1)} async-done(((bf16[16,32,128]{2,1,0:T(8,128)(2,1)}), bf16[16,32,128]{2,1,0:T(8,128)(2,1)S(1)}, u32[]{:S(2)}, u32[]{:S(2)}) %all-to-all-start.2) | async-done | bytes 131104 | tf_op jit(solution)/shard_map/all_to_all | solution.py:368
  69.6 12.2 %all-to-all-start.5 = ((bf16[8,272,256]{2,1,0:T(8,128)(2,1)}), bf16[8,272,256]{2,1,0:T(8,128)(2,1)S(1)}, u32[]{:S(2)}, u32[]{:S(2)}) async-start(bf16[8,272,256]{2,1,0:T(8,128)(2,1)} %pad_maximum_fusion), calls=%async_computation.5 | async-start | bytes 2228224 | tf_op jit(solution)/shard_map/all_to_all | solution.py:368
  81.8 4.7 %copy.52 = bf16[4,8,256,256]{3,2,0,1:T(8,128)(2,1)} copy(bf16[4,8,256,256]{3,2,1,0:T(8,128)(2,1)} %param.14) | data formatting | bytes 8388608 | tf_op args[1]
  86.5 19.3 %all-to-all-done.5.suffix_ref = bf16[8,272,256]{2,1,0:T(8,128)(2,1)S(1)} async-done(((bf16[8,272,256]{2,1,0:T(8,128)(2,1)}), bf16[8,272,256]{2,1,0:T(8,128)(2,1)S(1)}, u32[]{:S(2)}, u32[]{:S(2)}) %all-to-all-start.5) | async-done | bytes 1114144 | tf_op jit(solution)/shard_map/all_to_all | solution.py:368
  105.8 4.6 %all-to-all-start.4 = ((bf16[8,4,256,256]{3,2,1,0:T(8,128)(2,1)}), bf16[8,4,256,256]{3,2,1,0:T(8,128)(2,1)}, u32[]{:S(2)}, u32[]{:S(2)}) async-start(bf16[8,4,256,256]{3,2,1,0:T(8,128)(2,1)} %bitcast.61), calls=%async_computation.4 | async-start | bytes 8388608 | tf_op jit(solution)/shard_map/all_to_all | solution.py:368
  112.7 2.6 copy-done.1
  115.2 2.5 copy-done.3
  119.7 10.0 %project.1 = bf16[512,640]{1,0:T(8,128)(2,1)S(1)} custom-call(s32[8]{0:T(128)S(1)} %select_reduce_fusion.1.task_ref, bf16[512,5120]{1,0:T(8,128)(2,1)S(1)} %copy-done.3, bf16[5120,512]{1,0:T(8,128)(2,1)S(1)} %copy-done.1, bf16[128,5120]{1,0:T(8,128)(2,1)S(1)} %bitcast.56, bf16[512,128]{1,0:T(8,128)(2,1)S(1)} %bitcast.58, bf16[4,128,512]{2,1,0:T(8,128)(2,1)S(1)} %copy-done.7, ...), custom_call_target="tpu_custom_call" | custom-call | flops 3355443200 | bytes 13000000 | tf_op jit(solution)/shard_map/project/pallas_call | solution.py:119
  129.8 29.4 %all-to-all-done.4.page_ref = bf16[8,4,256,256]{3,2,1,0:T(8,128)(2,1)} async-done(((bf16[8,4,256,256]{3,2,1,0:T(8,128)(2,1)}), bf16[8,4,256,256]{3,2,1,0:T(8,128)(2,1)}, u32[]{:S(2)}, u32[]{:S(2)}) %all-to-all-start.4) | async-done | bytes 4194336 | tf_op jit(solution)/shard_map/all_to_all | solution.py:368
  160.5 6.4 %all-to-all-start.3 = ((bf16[16,64,640]{2,1,0:T(8,128)(2,1)}), bf16[16,64,640]{2,1,0:T(8,128)(2,1)S(1)}, u32[]{:S(2)}, u32[]{:S(2)}) async-start(bf16[16,64,640]{2,1,0:T(8,128)(2,1)} %bitcast.62), calls=%async_computation.3 | async-start | bytes 2621440 | tf_op jit(solution)/shard_map/all_to_all | solution.py:368
  168.8 16.1 %all-to-all-done.3 = bf16[16,64,640]{2,1,0:T(8,128)(2,1)S(1)} async-done(((bf16[16,64,640]{2,1,0:T(8,128)(2,1)}), bf16[16,64,640]{2,1,0:T(8,128)(2,1)S(1)}, u32[]{:S(2)}, u32[]{:S(2)}) %all-to-all-start.3) | async-done | bytes 1310752 | tf_op jit(solution)/shard_map/all_to_all | solution.py:368
  185.0 20.0 %attend.1 = bf16[8,2,32,1152]{3,2,1,0:T(8,128)(2,1)S(1)} custom-call(s32[8]{0:T(128)S(1)} %get-tuple-element.6.order_ref, s32[8]{0:T(128)S(1)} %get-tuple-element.5.local_ref, s32[2]{0:T(128)S(1)} %pad_add_fusion.place_ref, bf16[8,2,64,640]{3,2,1,0:T(8,128)(2,1)S(1)} %bitcast.55, bf16[8,4,256,256]{3,2,1,0:T(8,128)(2,1)} %all-to-all-done.4.page_ref, ...), custom_call_target="tpu_custom_call" | custom-call | flops 7650410496 | bytes 8000000 | tf_op jit(solution)/shard_map/attend/pallas_call | solution.py:263
  206.0 3.7 %all-to-all-start.6 = ((bf16[16,32,1152]{2,1,0:T(8,128)(2,1)}), bf16[16,32,1152]{2,1,0:T(8,128)(2,1)S(1)}, u32[]{:S(2)}, u32[]{:S(2)}) async-start(bf16[16,32,1152]{2,1,0:T(8,128)(2,1)} %bitcast.57), calls=%async_computation.6 | async-start | bytes 2359296 | tf_op jit(solution)/shard_map/all_to_all | solution.py:368
  209.7 16.7 %all-to-all-done.6 = bf16[16,32,1152]{2,1,0:T(8,128)(2,1)S(1)} async-done(((bf16[16,32,1152]{2,1,0:T(8,128)(2,1)}), bf16[16,32,1152]{2,1,0:T(8,128)(2,1)S(1)}, u32[]{:S(2)}, u32[]{:S(2)}) %all-to-all-start.6) | async-done | bytes 1179680 | tf_op jit(solution)/shard_map/all_to_all | solution.py:368
  226.4 2.5 copy-done
  228.9 2.5 copy-done.2
  231.3 5.8 %output_part.1 = bf16[256,5120]{1,0:T(8,128)(2,1)S(1)} custom-call(s32[2]{0:T(128)S(1)} %pad_add_fusion.place_ref, bf16[8,2,32,1152]{3,2,1,0:T(8,128)(2,1)S(1)} %bitcast.53, bf16[512,5120]{1,0:T(8,128)(2,1)S(1)} %copy-done, bf16[512,5120]{1,0:T(8,128)(2,1)S(1)} %copy-done.2), custom_call_target="tpu_custom_call" | custom-call | flops 2684354560 | bytes 14000000 | tf_op jit(solution)/shard_map/output_part/pallas_call | solution.py:345
  237.2 36.7 %all_to_all.40 = bf16[8,32,5120]{2,1,0:T(8,128)(2,1)S(1)} all-to-all(bf16[8,32,5120]{2,1,0:T(8,128)(2,1)S(1)} %bitcast.52), channel_id=1, replica_groups={{0,3,4,7,8,11,12,15},{1,2,5,6,9,10,13,14},{16,19,20,23,24,27,28,31},{17..., dimensions={0} | all-to-all | bytes 5242880 | tf_op jit(solution)/shard_map/all_to_all | solution.py:368
  (75 shorter events, 19.4 us)
Async XLA Ops:
  6.5 18.9 %copy-start.10 = (bf16[32,5120]{1,0:T(8,128)(2,1)S(1)}, bf16[32,5120]{1,0:T(8,128)(2,1)}, u32[]{:S(2)}) copy-start(bf16[32,5120]{1,0:T(8,128)(2,1)} %param.13) | copy-start | bytes 983044
  6.5 27.4 %copy-start.13 = (s32[32,2]{0,1:T(2,128)S(1)}, s32[32,2]{0,1:T(2,128)}, u32[]{:S(2)}) copy-start(s32[32,2]{0,1:T(2,128)} %param.17) | copy-start | bytes 772
  6.5 106.1 %all-gather.3.cloned.1.call-start = ((), (), s32[]{:S(2)}) async-start(), calls=%async_computation.8 | async-start | bytes 5570560 | tf_op jit(solution)/shard_map/all_gather | solution.py:395
  7.3 27.0 %copy-start.15 = (s32[32]{0:T(128)S(1)}, s32[32]{0:T(128)}, u32[]{:S(2)}) copy-start(s32[32]{0:T(128)} %param.18) | copy-start | bytes 388
  7.3 35.0 %copy-start.14 = (bf16[320,4,128]{2,1,0:T(4,128)(2,1)S(1)}, bf16[320,4,128]{2,1,0:T(4,128)(2,1)}, u32[]{:S(2)}) copy-start(bf16[320,4,128]{2,1,0:T(4,128)(2,1)} %param.22) | copy-start | bytes 983044
  7.3 202.4 %all-gather.5.cloned.1.call-start = ((), (), s32[]{:S(2)}) async-start(), calls=%async_computation.9 | async-start | bytes 5898240 | tf_op jit(solution)/shard_map/all_gather | solution.py:406
  8.5 16.1 %collective-permute-start = (bf16[64,5120]{1,0:T(8,128)(2,1)S(1)}, bf16[64,5120]{1,0:T(8,128)(2,1)S(1)}, u32[]{:S(2)}, u32[]{:S(2)}) collective-permute-start(bf16[64,5120]{1,0:T(8,128)(2,1)S(1)} %constant_dynamic-slice_fusion), channel_id=1, source_target_pairs={{0,1},{1,0},{2,3},{3,2},{4,5},{5,4},{6,7},{7,6},{8,9},{9,8},{10,11... | collective-permute-start | bytes 1966088 | tf_op jit(solution)/shard_map/ppermute | solution.py:407
  25.4 21.5 %copy-start.16 = (s32[128]{0:T(128)S(1)}, s32[128]{0:T(128)}, u32[]{:S(2)}) copy-start(s32[128]{0:T(128)} %param.16) | copy-start | bytes 1540
  25.8 35.7 %copy-start.11 = (bf16[128,16,256]{2,1,0:T(8,128)(2,1)S(1)}, bf16[128,16,256]{2,1,0:T(8,128)(2,1)}, u32[]{:S(2)}) copy-start(bf16[128,16,256]{2,1,0:T(8,128)(2,1)} %param.15) | copy-start | bytes 3145732
  26.6 15.6 %all-to-all-start = ((bf16[16,32,320]{2,1,0:T(8,128)(2,1)}), bf16[16,32,320]{2,1,0:T(8,128)(2,1)S(1)}, u32[]{:S(2)}, u32[]{:S(2)}) async-start(bf16[16,32,320]{2,1,0:T(8,128)(2,1)} %bitcast.51), calls=%async_computation | async-start | bytes 786432 | tf_op jit(solution)/shard_map/all_to_all | solution.py:368
  43.4 13.8 %all-to-all-start.1 = ((f32[16,32,128]{2,1,0:T(8,128)}), f32[16,32,128]{2,1,0:T(8,128)S(1)}, u32[]{:S(2)}, u32[]{:S(2)}) async-start(f32[16,32,128]{2,1,0:T(8,128)} %bitcast.13), calls=%async_computation.1 | async-start | bytes 524288 | tf_op jit(solution)/shard_map/all_to_all | solution.py:368
  57.9 11.7 %all-to-all-start.2 = ((bf16[16,32,128]{2,1,0:T(8,128)(2,1)}), bf16[16,32,128]{2,1,0:T(8,128)(2,1)S(1)}, u32[]{:S(2)}, u32[]{:S(2)}) async-start(bf16[16,32,128]{2,1,0:T(8,128)(2,1)} %broadcast_in_dim.8), calls=%async_computation.2 | async-start | bytes 262144 | tf_op jit(solution)/shard_map/all_to_all | solution.py:368
  69.6 36.2 %all-to-all-start.5 = ((bf16[8,272,256]{2,1,0:T(8,128)(2,1)}), bf16[8,272,256]{2,1,0:T(8,128)(2,1)S(1)}, u32[]{:S(2)}, u32[]{:S(2)}) async-start(bf16[8,272,256]{2,1,0:T(8,128)(2,1)} %pad_maximum_fusion), calls=%async_computation.5 | async-start | bytes 2228224 | tf_op jit(solution)/shard_map/all_to_all | solution.py:368
  105.8 53.4 %all-to-all-start.4 = ((bf16[8,4,256,256]{3,2,1,0:T(8,128)(2,1)}), bf16[8,4,256,256]{3,2,1,0:T(8,128)(2,1)}, u32[]{:S(2)}, u32[]{:S(2)}) async-start(bf16[8,4,256,256]{3,2,1,0:T(8,128)(2,1)} %bitcast.61), calls=%async_computation.4 | async-start | bytes 8388608 | tf_op jit(solution)/shard_map/all_to_all | solution.py:368
  110.3 2.3 copy-start.4
  110.3 2.3 copy-start.8
  112.6 2.6 copy-start.1
  115.2 2.5 copy-start.3
  160.5 24.5 %copy-start.9 = (f32[128]{0:T(128)S(1)}, f32[128]{0:T(128)}, u32[]{:S(2)}) copy-start(f32[128]{0:T(128)} %param.25) | copy-start | bytes 1540
  160.5 24.5 %all-to-all-start.3 = ((bf16[16,64,640]{2,1,0:T(8,128)(2,1)}), bf16[16,64,640]{2,1,0:T(8,128)(2,1)S(1)}, u32[]{:S(2)}, u32[]{:S(2)}) async-start(bf16[16,64,640]{2,1,0:T(8,128)(2,1)} %bitcast.62), calls=%async_computation.3 | async-start | bytes 2621440 | tf_op jit(solution)/shard_map/all_to_all | solution.py:368
  205.0 1.0 copy-start.5
  206.0 20.3 %all-to-all-start.6 = ((bf16[16,32,1152]{2,1,0:T(8,128)(2,1)}), bf16[16,32,1152]{2,1,0:T(8,128)(2,1)S(1)}, u32[]{:S(2)}, u32[]{:S(2)}) async-start(bf16[16,32,1152]{2,1,0:T(8,128)(2,1)} %bitcast.57), calls=%async_computation.6 | async-start | bytes 2359296 | tf_op jit(solution)/shard_map/all_to_all | solution.py:368
  226.4 2.5 copy-start
  228.9 2.5 copy-start.2
  (3 other events, 2.8 us)
Sparse Core Ops, SparseCore 0:
  9.5 64.4 all-gather.2
  75.6 44.9 all-gather.4

commit v2 on v1

--- a/solution.py
+++ b/solution.py
@@ -75,6 +75,7 @@
 
 def project_kernel(
     task_ref,
+    spot_ref,
     tokens_ref,
     query_ref,
     keyval_ref,
@@ -102,8 +103,11 @@
     def _():
         for slot in range(GROUPS):
             rows = slice(slot * SLOT_ROWS, (slot + 1) * SLOT_ROWS)
+            low_rank = jnp.concatenate(
+                [rank_ref[spot_ref[2 * slot]], rank_ref[spot_ref[2 * slot + 1]]], axis=0
+            )
             query = query_sum[rows, :] + jnp.dot(
-                rank_ref[rows, :], up_ref[task_ref[slot]], preferred_element_type=jnp.float32
+                low_rank, up_ref[task_ref[slot]], preferred_element_type=jnp.float32
             )
             for head in range(OWN_HEADS):
                 lanes = slice(head * HEAD_SIZE, (head + 1) * HEAD_SIZE)
@@ -113,19 +117,19 @@
         out_ref[:, OWN_WIDTH:] = keyval_sum[...].astype(jnp.bfloat16)
 
 
-def project(tasks, tokens, query_weight, keyval_weight, low_rank, up_maps, cosine, sine, gain):
+def project(tasks, spots, tokens, query_weight, keyval_weight, low_rank, up_maps, cosine, sine, gain):
     tile = 512
-    whole = lambda *shape: pl.BlockSpec(shape, lambda k, tasks: (0,) * len(shape))
+    whole = lambda *shape: pl.BlockSpec(shape, lambda k, t, s: (0,) * len(shape))
     return pl.pallas_call(
         project_kernel,
         grid_spec=pltpu.PrefetchScalarGridSpec(
-            num_scalar_prefetch=1,
+            num_scalar_prefetch=2,
             grid=(MODEL_WIDTH // tile,),
             in_specs=[
-                pl.BlockSpec((ROWS, tile), lambda k, tasks: (0, k)),
-                pl.BlockSpec((tile, OWN_WIDTH), lambda k, tasks: (k, 0)),
-                pl.BlockSpec((HEAD_SIZE, tile), lambda k, tasks: (0, k)),
-                whole(ROWS, ADAPTER_RANK),
+                pl.BlockSpec((ROWS, tile), lambda k, t, s: (0, k)),
+                pl.BlockSpec((tile, OWN_WIDTH), lambda k, t, s: (k, 0)),
+                pl.BlockSpec((HEAD_SIZE, tile), lambda k, t, s: (0, k)),
+                whole(SHARDS, HALF_ROWS, ADAPTER_RANK),
                 whole(ADAPTER_COUNT, ADAPTER_RANK, OWN_WIDTH),
                 whole(ROWS, HEAD_SIZE),
                 whole(ROWS, HEAD_SIZE),
@@ -138,17 +142,18 @@
             ],
         ),
         out_shape=jax.ShapeDtypeStruct((ROWS, SENT_WIDTH), jnp.bfloat16),
-        compiler_params=pltpu.CompilerParams(vmem_limit_bytes=40 * 2**20),
+        compiler_params=pltpu.CompilerParams(vmem_limit_bytes=60 * 2**20),
         cost_estimate=pl.CostEstimate(
             flops=2 * ROWS * MODEL_WIDTH * SENT_WIDTH, bytes_accessed=13_000_000, transcendentals=0
         ),
         name="project",
-    )(tasks, tokens, query_weight, keyval_weight, low_rank, up_maps, cosine, sine, gain)
+    )(tasks, spots, tokens, query_weight, keyval_weight, low_rank, up_maps, cosine, sine, gain)
 
 
 def attend_kernel(
     order_ref,
     local_ref,
+    reach_ref,
     place_ref,
     sent_ref,
     page_ref,
@@ -258,38 +263,38 @@
     out_ref[0, 1, :, HEAD_FAN * HEAD_SIZE :] = jnp.where(flip == 0, low, top)
 
 
-def attend(order, local, place, sent, pages, suffix, cosine, sine, gain):
+def attend(order, local, reach, place, sent, pages, suffix, cosine, sine, gain):
     block = PROMPT_TOKENS // SHARDS
     return pl.pallas_call(
         attend_kernel,
         grid_spec=pltpu.PrefetchScalarGridSpec(
-            num_scalar_prefetch=3,
+            num_scalar_prefetch=4,
             grid=(GROUPS,),
             in_specs=[
-                pl.BlockSpec((1, 2, SLOT_ROWS, SENT_WIDTH), lambda i, o, l, p: (o[i], 0, 0, 0)),
+                pl.BlockSpec((1, 2, SLOT_ROWS, SENT_WIDTH), lambda i, o, l, r, p: (o[i], 0, 0, 0)),
                 pl.BlockSpec(
-                    (GROUPS, 1, block, 2 * HEAD_SIZE), lambda i, o, l, p: (0, l[i], 0, 0)
+                    (GROUPS, 1, block, 2 * HEAD_SIZE), lambda i, o, l, r, p: (0, l[i], 0, 0)
                 ),
                 pl.BlockSpec(
-                    (1, suffix.shape[1], 2 * HEAD_SIZE), lambda i, o, l, p: (o[i], 0, 0)
+                    (1, suffix.shape[1], 2 * HEAD_SIZE), lambda i, o, l, r, p: (r[i], 0, 0)
                 ),
-                pl.BlockSpec((1, SLOT_ROWS, HEAD_SIZE), lambda i, o, l, p: (o[i], 0, 0)),
-                pl.BlockSpec((1, SLOT_ROWS, HEAD_SIZE), lambda i, o, l, p: (o[i], 0, 0)),
-                pl.BlockSpec((1, HEAD_SIZE), lambda i, o, l, p: (0, 0)),
+                pl.BlockSpec((1, SLOT_ROWS, HEAD_SIZE), lambda i, o, l, r, p: (r[i], 0, 0)),
+                pl.BlockSpec((1, SLOT_ROWS, HEAD_SIZE), lambda i, o, l, r, p: (r[i], 0, 0)),
+                pl.BlockSpec((1, HEAD_SIZE), lambda i, o, l, r, p: (0, 0)),
             ],
             out_specs=pl.BlockSpec(
-                (1, 2, HALF_ROWS, BACK_WIDTH), lambda i, o, l, p: (o[i], 0, 0, 0)
+                (1, 2, HALF_ROWS, BACK_WIDTH), lambda i, o, l, r, p: (o[i], 0, 0, 0)
             ),
         ),
         out_shape=jax.ShapeDtypeStruct((GROUPS, 2, HALF_ROWS, BACK_WIDTH), jnp.bfloat16),
-        compiler_params=pltpu.CompilerParams(vmem_limit_bytes=48 * 2**20),
+        compiler_params=pltpu.CompilerParams(vmem_limit_bytes=60 * 2**20),
         cost_estimate=pl.CostEstimate(
             flops=2 * GROUPS * 512 * 2432 * 384,
             bytes_accessed=8_000_000,
             transcendentals=GROUPS * 512 * 2432,
         ),
         name="attend",
-    )(order, local, place, sent, pages, suffix, cosine, sine, gain)
+    )(order, local, reach, place, sent, pages, suffix, cosine, sine, gain)
 
 
 def output_kernel(place_ref, back_ref, own_ref, other_ref, out_ref, mixed):
@@ -356,12 +361,20 @@
             scratch_shapes=[pltpu.VMEM((2, rows, OWN_WIDTH), jnp.bfloat16)],
         ),
         out_shape=jax.ShapeDtypeStruct((rows, MODEL_WIDTH), jnp.bfloat16),
-        compiler_params=pltpu.CompilerParams(vmem_limit_bytes=40 * 2**20),
+        compiler_params=pltpu.CompilerParams(vmem_limit_bytes=60 * 2**20),
         cost_estimate=pl.CostEstimate(
             flops=2 * rows * MODEL_WIDTH * 1024, bytes_accessed=14_000_000, transcendentals=0
         ),
         name="output_part",
     )(place, back, own_weight, other_weight)
+
+
+def along_x(distance):
+    return [(shard, shard // 4 * 4 + (shard + distance) % 4) for shard in range(SHARDS)]
+
+
+def along_y(distance):
+    return [(shard, (shard + 4 * distance) % SHARDS) for shard in range(SHARDS)]
 
 
 def swap(block, axes, groups=None):
@@ -391,21 +404,7 @@
     half = shard % 2
     local_table = slot_prompts(fanout, GROUPS, OWNED)
 
-    arrived = swap(jnp.swapaxes(prompt_cache, 0, 1), "ad", ROLE_GROUPS)
     part_rows = lax.all_gather(tokens, "ad", axis=0, tiled=True)
-
-    slot_suffix = generated_cache.reshape(GROUPS, SLOT_SAMPLES * 16, 2 * HEAD_SIZE)
-    slot_lengths = suffix_lengths.reshape(GROUPS, SLOT_SAMPLES, 1).astype(jnp.bfloat16)
-    slot_suffix = jnp.concatenate(
-        [slot_suffix, jnp.broadcast_to(slot_lengths, (GROUPS, SLOT_SAMPLES, 2 * HEAD_SIZE))], axis=1
-    )
-    suffix = swap(slot_suffix, "grp")
-
-    slice_rows = OWN_WIDTH // GROUPS
-    weight_slice = lax.dynamic_slice_in_dim(output_weight, group * slice_rows, slice_rows, 0)
-    other_weight = lax.all_gather(
-        lax.ppermute(weight_slice, "ad", PARTNERS), "grp", axis=0, tiled=True
-    )
 
     owners = jnp.arange(GROUPS, dtype=jnp.int32)
     local_of_slot = lax.dynamic_index_in_dim(local_table, group, 1, keepdims=False)
@@ -425,17 +424,48 @@
     rank_part = jnp.sum(rank_all * chosen[:, None, :, None], axis=2)
     rank_rows = jnp.sum(swap(rank_part.reshape(SHARDS, own_rows, ADAPTER_RANK), "ad"), axis=0)
     rank_rows = rank_rows.astype(jnp.bfloat16)
-    low_rank = swap(jnp.broadcast_to(rank_rows[None], (SHARDS,) + rank_rows.shape), "ad")
+
+    rank_rows, page_source, suffix_source, weight_source = lax.optimization_barrier(
+        (rank_rows, prompt_cache, generated_cache, output_weight)
+    )
+
+    arrived = swap(jnp.swapaxes(page_source, 0, 1), "ad", ROLE_GROUPS)
+
+    ring = [rank_rows] + [lax.ppermute(rank_rows, "ad", along_x(k)) for k in (1, 2, 3)]
+    ring = jnp.stack(ring)
+    low_rank = jnp.stack([ring] + [lax.ppermute(ring, "ad", along_y(k)) for k in (1, 2, 3)])
+    every = jnp.arange(SHARDS, dtype=jnp.int32)
+    spots = ((shard // 4 - every // 4) % 4) * 4 + (shard % 4 - every % 4) % 4
+
+    slot_suffix = suffix_source.reshape(GROUPS, SLOT_SAMPLES * 16, 2 * HEAD_SIZE)
+    slot_lengths = suffix_lengths.reshape(GROUPS, SLOT_SAMPLES, 1).astype(jnp.bfloat16)
+    slot_suffix = jnp.concatenate(
+        [slot_suffix, jnp.broadcast_to(slot_lengths, (GROUPS, SLOT_SAMPLES, 2 * HEAD_SIZE))], axis=1
+    )
+    suffix = []
+    for k in range(GROUPS):
+        block = lax.dynamic_index_in_dim(slot_suffix, group ^ k, 0, keepdims=False)
+        if k:
+            block = lax.ppermute(block, "grp", [(g, g ^ k) for g in range(GROUPS)])
+        suffix.append(block)
+    suffix = jnp.stack(suffix)
+
+    slice_rows = OWN_WIDTH // GROUPS
+    weight_slice = lax.dynamic_slice_in_dim(weight_source, group * slice_rows, slice_rows, 0)
+    other_weight = lax.all_gather(
+        lax.ppermute(weight_slice, "ad", PARTNERS), "grp", axis=0, tiled=True
+    )
 
     steps = jnp.arange(DECODE_STEPS, dtype=jnp.int32)
     position = (PROMPT_TOKENS + suffix_lengths[:, None] + steps[None, :]).astype(jnp.float32)
     cosine, sine = angle_tables(position.reshape(ROWS))
     sent = project(
         tasks,
+        spots,
         part_rows,
         query_weight,
         key_value_weight.transpose(1, 2, 0).reshape(HEAD_SIZE, MODEL_WIDTH),
-        low_rank.reshape(ROWS, ADAPTER_RANK),
+        low_rank.reshape(SHARDS, own_rows, ADAPTER_RANK),
         adapter_up_maps,
         cosine,
         sine,
@@ -463,6 +493,7 @@
     partial = attend(
         order,
         local_sorted,
+        order ^ group,
         place,
         received,
         arrived,

time: 283 us -> 281 us (level)
  waiting for transfers between devices: 121 us -> 95.1 us
  starting transfers between devices: 43.3 us -> 61.3 us
  Pallas kernels: 35.9 us -> 46.7 us
  local copies, waits for them, and re-layouts: 23.6 us -> 14.2 us
    all_to_all x7 -> x5, waiting for transfers between devices: 106 us -> 49 us  [swap(): lax.all_to_all(block, axes, split_axis=0, concat_axis=0, tiled=True, axis...]
    ppermute x0 -> x13, starting transfers between devices: none -> 36.5 us  [the longest x7 28.1 us: shards(): block = lax.ppermute(block, 'grp', [(g, g ^ k) for g in range(GROUPS)])]
    ppermute x0 -> x13, waiting for transfers between devices: none -> 24.3 us  [the longest x3 21.2 us: shards(): lax.ppermute(rank_rows, 'ad', along_x(k))]
    all_to_all x7 -> x5, starting transfers between devices: 41.1 us -> 23.7 us  [swap(): lax.all_to_all(block, axes, split_axis=0, concat_axis=0, tiled=True, axis...]
    unnamed x35 -> x28, local copies, waits for them, and re-layouts: 18.7 us -> 3.15 us
    ppermute x1, waiting for transfers between devices: 13.9 us -> 21 us  [shards(): lax.ppermute(weight_slice, 'ad', PARTNERS)]
    pallas_call x1, Pallas kernels: 10 us -> 15.3 us  [project(): pl.pallas_call(project_kernel, grid_spec=pltpu.PrefetchScalarGridSpec(num...]
    optimization_barrier x0 -> x1, local copies, waits for them, and re-layouts: none -> 4.65 us  [shards(): lax.optimization_barrier((rank_rows, prompt_cache, generated_cache, outpu...]
  transfers between devices with their start and end apart: 10 -> 21, of which waited for: 8 -> 9; matrix products, arithmetic and copies ran while one was open for 6% -> 7% of each run, Pallas kernels for 11% -> 13%
where the time goes in v2:
time: 281 us; the launch traced here: 280 us
  waiting for transfers between devices  95.1 us (34%)
  starting transfers between devices  61.3 us (22%)
  Pallas kernels  46.7 us (17%)
  blocking collectives  38 us (14%)
  local copies, waits for them, and re-layouts  14.2 us (5%)
  between operations  13.9 us (5%)
  other arithmetic  9.17 us (3%)
    all_to_all x5, waiting for transfers between devices, swap(): lax.all_to_all(block, axes, split_axis=0, concat_axis=0, tiled=True, axis...  49 us
    all_to_all x1, blocking collectives, swap(): lax.all_to_all(block, axes, split_axis=0, concat_axis=0, tiled=True, axis...  38 us
    ppermute x7, starting transfers between devices, shards(): block = lax.ppermute(block, 'grp', [(g, g ^ k) for g in range(GROUPS)])  28.1 us
    all_to_all x5, starting transfers between devices, swap(): lax.all_to_all(block, axes, split_axis=0, concat_axis=0, tiled=True, axis...  23.7 us
    ppermute x3, waiting for transfers between devices, shards(): lax.ppermute(rank_rows, 'ad', along_x(k))  21.2 us
    pallas_call x1, Pallas kernels, attend(): pl.pallas_call(attend_kernel, grid_spec=pltpu.PrefetchScalarGridSpec(num_...  21.2 us
    ppermute x1, waiting for transfers between devices, shards(): lax.ppermute(weight_slice, 'ad', PARTNERS)  21 us
    pallas_call x1, Pallas kernels, project(): pl.pallas_call(project_kernel, grid_spec=pltpu.PrefetchScalarGridSpec(num...  15.3 us
  transfers between devices with their start and end apart: 21, of which 9 were waited for; matrix products, arithmetic and copies ran while one was open for 7% of the time, Pallas kernels for 13%

profile of v2, /device:TPU:1, one launch (start us, length us, event | category | flops | bytes accessed | tf_op | source)
XLA Modules:
  0.0 279.5 jit_solution(14878640132238711519)
XLA Ops:
  9.5 7.6 %all-to-all-start = ((bf16[16,32,320]{2,1,0:T(8,128)(2,1)}), bf16[16,32,320]{2,1,0:T(8,128)(2,1)S(1)}, u32[]{:S(2)}, u32[]{:S(2)}) async-start(bf16[16,32,320]{2,1,0:T(8,128)(2,1)} %bitcast.88), calls=%async_computation | async-start | bytes 786432 | tf_op jit(solution)/shard_map/all_to_all | solution.py:381
  17.7 8.6 %all-to-all-done = bf16[16,32,320]{2,1,0:T(8,128)(2,1)S(1)} async-done(((bf16[16,32,320]{2,1,0:T(8,128)(2,1)}), bf16[16,32,320]{2,1,0:T(8,128)(2,1)S(1)}, u32[]{:S(2)}, u32[]{:S(2)}) %all-to-all-start) | async-done | bytes 327712 | tf_op jit(solution)/shard_map/all_to_all | solution.py:381
  27.4 3.5 %all-to-all-start.1 = ((f32[16,32,128]{2,1,0:T(8,128)}), f32[16,32,128]{2,1,0:T(8,128)S(1)}, u32[]{:S(2)}, u32[]{:S(2)}) async-start(f32[16,32,128]{2,1,0:T(8,128)} %bitcast.13), calls=%async_computation.1 | async-start | bytes 524288 | tf_op jit(solution)/shard_map/all_to_all | solution.py:381
  31.0 8.1 %all-to-all-done.1 = f32[16,32,128]{2,1,0:T(8,128)S(1)} async-done(((f32[16,32,128]{2,1,0:T(8,128)}), f32[16,32,128]{2,1,0:T(8,128)S(1)}, u32[]{:S(2)}, u32[]{:S(2)}) %all-to-all-start.1) | async-done | bytes 262176 | tf_op jit(solution)/shard_map/all_to_all | solution.py:381
  41.3 21.0 %collective-permute-done.13 = bf16[64,5120]{1,0:T(8,128)(2,1)S(1)} collective-permute-done((bf16[64,5120]{1,0:T(8,128)(2,1)S(1)}, bf16[64,5120]{1,0:T(8,128)(2,1)S(1)}, u32[]{:S(2)}, u32[]{:S(2)}) %collective-permute-start.13) | collective-permute-done | bytes 655392 | tf_op jit(solution)/shard_map/ppermute | solution.py:456
  63.2 4.6 %copy.52 = bf16[4,8,256,256]{3,2,0,1:T(8,128)(2,1)} copy(bf16[4,8,256,256]{3,2,1,0:T(8,128)(2,1)} %param.14) | data formatting | bytes 8388608 | tf_op jit(solution)/shard_map/optimization_barrier | solution.py:428
  67.9 4.6 %all-to-all-start.3 = ((bf16[8,4,256,256]{3,2,1,0:T(8,128)(2,1)}), bf16[8,4,256,256]{3,2,1,0:T(8,128)(2,1)}, u32[]{:S(2)}, u32[]{:S(2)}) async-start(bf16[8,4,256,256]{3,2,1,0:T(8,128)(2,1)} %bitcast.89), calls=%async_computation.3 | async-start | bytes 8388608 | tf_op jit(solution)/shard_map/all_to_all | solution.py:381
  77.6 2.5 collective-permute-start.2
  82.5 8.4 %collective-permute-start.6 = (bf16[272,256]{1,0:T(8,128)(2,1)S(1)}, bf16[272,256]{1,0:T(8,128)(2,1)S(1)}, u32[]{:S(2)}, u32[]{:S(2)}) collective-permute-start(bf16[272,256]{1,0:T(8,128)(2,1)S(1)} %get-tuple-element.19), channel_id=1, source_target_pairs={{0,16},{16,0},{32,48},{48,32},{64,80},{80,64},{96,112},{112,96},{1... | collective-permute-start | bytes 417800 | tf_op jit(solution)/shard_map/ppermute | solution.py:449
  92.0 19.4 %collective-permute-done.2 = bf16[32,128]{1,0:T(8,128)(2,1)S(1)} collective-permute-done((bf16[32,128]{1,0:T(8,128)(2,1)S(1)}, bf16[32,128]{1,0:T(8,128)(2,1)S(1)}, u32[]{:S(2)}, u32[]{:S(2)}) %collective-permute-start.2) | collective-permute-done | bytes 8224 | tf_op jit(solution)/shard_map/ppermute | solution.py:434
  113.3 2.5 collective-permute-start.5
  117.4 10.4 %collective-permute-start.8 = (bf16[272,256]{1,0:T(8,128)(2,1)S(1)}, bf16[272,256]{1,0:T(8,128)(2,1)S(1)}, u32[]{:S(2)}, u32[]{:S(2)}) collective-permute-start(bf16[272,256]{1,0:T(8,128)(2,1)S(1)} %get-tuple-element.21), channel_id=1, source_target_pairs={{0,48},{16,32},{32,16},{48,0},{64,112},{80,96},{96,80},{112,64},{1... | collective-permute-start | bytes 417800 | tf_op jit(solution)/shard_map/ppermute | solution.py:449
  127.8 2.5 collective-permute-start.9
  130.3 3.3 %collective-permute-start.10 = (bf16[272,256]{1,0:T(8,128)(2,1)S(1)}, bf16[272,256]{1,0:T(8,128)(2,1)S(1)}, u32[]{:S(2)}, u32[]{:S(2)}) collective-permute-start(bf16[272,256]{1,0:T(8,128)(2,1)S(1)} %get-tuple-element.24), channel_id=1, source_target_pairs={{0,80},{16,64},{32,112},{48,96},{64,16},{80,0},{96,48},{112,32},{1... | collective-permute-start | bytes 417800 | tf_op jit(solution)/shard_map/ppermute | solution.py:449
  136.7 2.6 collective-permute-done.10
  139.4 15.3 %project.1 = bf16[512,640]{1,0:T(8,128)(2,1)} custom-call(s32[8]{0:T(128)} %copy-done.5, s32[16]{0:T(128)} %fusion.25.spot_ref, bf16[512,5120]{1,0:T(8,128)(2,1)} %all-gather.3.cloned.1.call-done.tokens_ref, bf16[5120,512]{1,0:T(8,128)(2,1)} %query_ref.1, bf16[128,5120]{1,0:T(8,128)(2,1)} %bitcast.96, bf16[16,32,128]{2,1,0:T(8,128)(2,1)} %bitcast.98, ...), custom_call_target="tpu_custom_call" | custom-call | flops 3355443200 | bytes 13000000 | tf_op jit(solution)/shard_map/project/pallas_call | solution.py:123
  154.7 2.3 broadcast_in_dim.7
  157.0 4.4 %all-to-all-start.2 = ((bf16[16,64,640]{2,1,0:T(8,128)(2,1)}), bf16[16,64,640]{2,1,0:T(8,128)(2,1)S(1)}, u32[]{:S(2)}, u32[]{:S(2)}) async-start(bf16[16,64,640]{2,1,0:T(8,128)(2,1)} %bitcast.25), calls=%async_computation.2 | async-start | bytes 2621440 | tf_op jit(solution)/shard_map/all_to_all | solution.py:381
  163.8 15.7 %all-to-all-done.2 = bf16[16,64,640]{2,1,0:T(8,128)(2,1)S(1)} async-done(((bf16[16,64,640]{2,1,0:T(8,128)(2,1)}), bf16[16,64,640]{2,1,0:T(8,128)(2,1)S(1)}, u32[]{:S(2)}, u32[]{:S(2)}) %all-to-all-start.2) | async-done | bytes 1310752 | tf_op jit(solution)/shard_map/all_to_all | solution.py:381
  180.6 21.2 %attend.1 = bf16[8,2,32,1152]{3,2,1,0:T(8,128)(2,1)} custom-call(s32[8]{0:T(128)} %copy-done.7, s32[8]{0:T(128)} %get-tuple-element.13.local_ref, s32[8]{0:T(128)} %broadcast_xor_fusion.reach_ref, s32[2]{0:T(128)} %pad_add_fusion.place_ref, bf16[8,2,64,640]{3,2,1,0:T(8,128)(2,1)} %bitcast.95, bf16[8,4,256,256]{3,2,1,0:T(8,128)(2,1)} %all-to-all-done.3.page_ref, ...), custom_call_target="tpu_custom_call" | custom-call | flops 7650410496 | bytes 8000000 | tf_op jit(solution)/shard_map/attend/pallas_call | solution.py:268
  201.8 3.6 %all-to-all-start.4 = ((bf16[16,32,1152]{2,1,0:T(8,128)(2,1)}), bf16[16,32,1152]{2,1,0:T(8,128)(2,1)S(1)}, u32[]{:S(2)}, u32[]{:S(2)}) async-start(bf16[16,32,1152]{2,1,0:T(8,128)(2,1)} %bitcast.97), calls=%async_computation.4 | async-start | bytes 2359296 | tf_op jit(solution)/shard_map/all_to_all | solution.py:381
  205.4 16.7 %all-to-all-done.4 = bf16[16,32,1152]{2,1,0:T(8,128)(2,1)S(1)} async-done(((bf16[16,32,1152]{2,1,0:T(8,128)(2,1)}), bf16[16,32,1152]{2,1,0:T(8,128)(2,1)S(1)}, u32[]{:S(2)}, u32[]{:S(2)}) %all-to-all-start.4) | async-done | bytes 1179680 | tf_op jit(solution)/shard_map/all_to_all | solution.py:381
  223.2 10.3 %output_part.1 = bf16[256,5120]{1,0:T(8,128)(2,1)} custom-call(s32[2]{0:T(128)} %pad_add_fusion.place_ref, bf16[8,2,32,1152]{3,2,1,0:T(8,128)(2,1)} %bitcast.91, bf16[512,5120]{1,0:T(8,128)(2,1)} %own_ref.1, bf16[512,5120]{1,0:T(8,128)(2,1)} %all-gather.5.cloned.1.call-done.other_ref), custom_call_target="tpu_custom_call" | custom-call | flops 2684354560 | bytes 14000000 | tf_op jit(solution)/shard_map/output_part/pallas_call | solution.py:350
  233.5 38.0 %all_to_all.30 = bf16[8,32,5120]{2,1,0:T(8,128)(2,1)S(1)} all-to-all(bf16[8,32,5120]{2,1,0:T(8,128)(2,1)} %bitcast.90), channel_id=1, replica_groups={{0,3,4,7,8,11,12,15},{1,2,5,6,9,10,13,14},{16,19,20,23,24,27,28,31},{17..., dimensions={0} | all-to-all | bytes 5242880 | tf_op jit(solution)/shard_map/all_to_all | solution.py:381
  (96 shorter events, 28.6 us)
Async XLA Ops:
  6.5 132.8 %all-gather.3.cloned.1.call-start = ((), (), s32[]{:S(2)}) async-start(), calls=%async_computation.6 | async-start | bytes 5570560 | tf_op jit(solution)/shard_map/all_gather | solution.py:407
  7.3 10.1 %copy-start.9 = (s32[32]{0:T(128)S(1)}, s32[32]{0:T(128)}, u32[]{:S(2)}) copy-start(s32[32]{0:T(128)} %param.18) | copy-start | bytes 388
  7.3 19.0 %copy-start.8 = (bf16[320,4,128]{2,1,0:T(4,128)(2,1)S(1)}, bf16[320,4,128]{2,1,0:T(4,128)(2,1)}, u32[]{:S(2)}) copy-start(bf16[320,4,128]{2,1,0:T(4,128)(2,1)} %param.22) | copy-start | bytes 983044
  9.5 16.8 %all-to-all-start = ((bf16[16,32,320]{2,1,0:T(8,128)(2,1)}), bf16[16,32,320]{2,1,0:T(8,128)(2,1)S(1)}, u32[]{:S(2)}, u32[]{:S(2)}) async-start(bf16[16,32,320]{2,1,0:T(8,128)(2,1)} %bitcast.88), calls=%async_computation | async-start | bytes 786432 | tf_op jit(solution)/shard_map/all_to_all | solution.py:381
  27.4 11.7 %all-to-all-start.1 = ((f32[16,32,128]{2,1,0:T(8,128)}), f32[16,32,128]{2,1,0:T(8,128)S(1)}, u32[]{:S(2)}, u32[]{:S(2)}) async-start(f32[16,32,128]{2,1,0:T(8,128)} %bitcast.13), calls=%async_computation.1 | async-start | bytes 524288 | tf_op jit(solution)/shard_map/all_to_all | solution.py:381
  30.9 174.5 %all-gather.5.cloned.1.call-start = ((), (), s32[]{:S(2)}) async-start(), calls=%async_computation.7 | async-start | bytes 5898240 | tf_op jit(solution)/shard_map/all_gather | solution.py:455
  31.0 32.2 %copy-start.10 = (s32[128]{0:T(128)S(1)}, s32[128]{0:T(128)}, u32[]{:S(2)}) copy-start(s32[128]{0:T(128)} %param.16) | copy-start | bytes 1540
  40.3 22.0 %collective-permute-start.13 = (bf16[64,5120]{1,0:T(8,128)(2,1)S(1)}, bf16[64,5120]{1,0:T(8,128)(2,1)S(1)}, u32[]{:S(2)}, u32[]{:S(2)}) collective-permute-start(bf16[64,5120]{1,0:T(8,128)(2,1)S(1)} %constant_dynamic-slice_fusion), channel_id=1, source_target_pairs={{0,1},{1,0},{2,3},{3,2},{4,5},{5,4},{6,7},{7,6},{8,9},{9,8},{10,11... | collective-permute-start | bytes 1966088 | tf_op jit(solution)/shard_map/ppermute | solution.py:456
  67.9 86.8 %all-to-all-start.3 = ((bf16[8,4,256,256]{3,2,1,0:T(8,128)(2,1)}), bf16[8,4,256,256]{3,2,1,0:T(8,128)(2,1)}, u32[]{:S(2)}, u32[]{:S(2)}) async-start(bf16[8,4,256,256]{3,2,1,0:T(8,128)(2,1)} %bitcast.89), calls=%async_computation.3 | async-start | bytes 8388608 | tf_op jit(solution)/shard_map/all_to_all | solution.py:381
  77.6 33.9 %collective-permute-start.2 = (bf16[32,128]{1,0:T(8,128)(2,1)S(1)}, bf16[32,128]{1,0:T(8,128)(2,1)S(1)}, u32[]{:S(2)}, u32[]{:S(2)}) collective-permute-start(bf16[32,128]{1,0:T(8,128)(2,1)S(1)} %reduce_sum.81), channel_id=1, source_target_pairs={{0,3},{1,0},{2,1},{3,2},{4,7},{5,4},{6,5},{7,6},{8,11},{9,8},{10,9... | collective-permute-start | bytes 24584 | tf_op jit(solution)/shard_map/ppermute | solution.py:434
  80.0 31.4 %collective-permute-start.1 = (bf16[32,128]{1,0:T(8,128)(2,1)S(1)}, bf16[32,128]{1,0:T(8,128)(2,1)S(1)}, u32[]{:S(2)}, u32[]{:S(2)}) collective-permute-start(bf16[32,128]{1,0:T(8,128)(2,1)S(1)} %reduce_sum.81), channel_id=1, source_target_pairs={{0,2},{1,3},{2,0},{3,1},{4,6},{5,7},{6,4},{7,5},{8,10},{9,11},{10,... | collective-permute-start | bytes 24584 | tf_op jit(solution)/shard_map/ppermute | solution.py:434
  81.6 31.7 %collective-permute-start = (bf16[32,128]{1,0:T(8,128)(2,1)S(1)}, bf16[32,128]{1,0:T(8,128)(2,1)S(1)}, u32[]{:S(2)}, u32[]{:S(2)}) collective-permute-start(bf16[32,128]{1,0:T(8,128)(2,1)S(1)} %reduce_sum.81), channel_id=1, source_target_pairs={{0,1},{1,2},{2,3},{3,0},{4,5},{5,6},{6,7},{7,4},{8,9},{9,10},{10,1... | collective-permute-start | bytes 24584 | tf_op jit(solution)/shard_map/ppermute | solution.py:434
  82.5 51.8 %collective-permute-start.6 = (bf16[272,256]{1,0:T(8,128)(2,1)S(1)}, bf16[272,256]{1,0:T(8,128)(2,1)S(1)}, u32[]{:S(2)}, u32[]{:S(2)}) collective-permute-start(bf16[272,256]{1,0:T(8,128)(2,1)S(1)} %get-tuple-element.19), channel_id=1, source_target_pairs={{0,16},{16,0},{32,48},{48,32},{64,80},{80,64},{96,112},{112,96},{1... | collective-permute-start | bytes 417800 | tf_op jit(solution)/shard_map/ppermute | solution.py:449
  90.9 45.3 %collective-permute-start.7 = (bf16[272,256]{1,0:T(8,128)(2,1)S(1)}, bf16[272,256]{1,0:T(8,128)(2,1)S(1)}, u32[]{:S(2)}, u32[]{:S(2)}) collective-permute-start(bf16[272,256]{1,0:T(8,128)(2,1)S(1)} %get-tuple-element.20), channel_id=1, source_target_pairs={{0,32},{16,48},{32,0},{48,16},{64,96},{80,112},{96,64},{112,80},{1... | collective-permute-start | bytes 417800 | tf_op jit(solution)/shard_map/ppermute | solution.py:449
  113.3 4.1 %collective-permute-start.5 = (bf16[4,32,128]{2,1,0:T(8,128)(2,1)S(1)}, bf16[4,32,128]{2,1,0:T(8,128)(2,1)S(1)}, u32[]{:S(2)}, u32[]{:S(2)}) collective-permute-start(bf16[4,32,128]{2,1,0:T(8,128)(2,1)S(1)} %get-tuple-element.26), channel_id=1, source_target_pairs={{0,12},{1,13},{2,14},{3,15},{4,0},{5,1},{6,2},{7,3},{8,4},{9,5},{1... | collective-permute-start | bytes 98312 | tf_op jit(solution)/shard_map/ppermute | solution.py:436
  115.8 12.0 %collective-permute-start.4 = (bf16[4,32,128]{2,1,0:T(8,128)(2,1)S(1)}, bf16[4,32,128]{2,1,0:T(8,128)(2,1)S(1)}, u32[]{:S(2)}, u32[]{:S(2)}) collective-permute-start(bf16[4,32,128]{2,1,0:T(8,128)(2,1)S(1)} %get-tuple-element.26), channel_id=1, source_target_pairs={{0,8},{1,9},{2,10},{3,11},{4,12},{5,13},{6,14},{7,15},{8,0},{9,1},... | collective-permute-start | bytes 98312 | tf_op jit(solution)/shard_map/ppermute | solution.py:436
  116.3 14.0 %collective-permute-start.3 = (bf16[4,32,128]{2,1,0:T(8,128)(2,1)S(1)}, bf16[4,32,128]{2,1,0:T(8,128)(2,1)S(1)}, u32[]{:S(2)}, u32[]{:S(2)}) collective-permute-start(bf16[4,32,128]{2,1,0:T(8,128)(2,1)S(1)} %get-tuple-element.26), channel_id=1, source_target_pairs={{0,4},{1,5},{2,6},{3,7},{4,8},{5,9},{6,10},{7,11},{8,12},{9,13},{1... | collective-permute-start | bytes 98312 | tf_op jit(solution)/shard_map/ppermute | solution.py:436
  117.4 19.2 %collective-permute-start.8 = (bf16[272,256]{1,0:T(8,128)(2,1)S(1)}, bf16[272,256]{1,0:T(8,128)(2,1)S(1)}, u32[]{:S(2)}, u32[]{:S(2)}) collective-permute-start(bf16[272,256]{1,0:T(8,128)(2,1)S(1)} %get-tuple-element.21), channel_id=1, source_target_pairs={{0,48},{16,32},{32,16},{48,0},{64,112},{80,96},{96,80},{112,64},{1... | collective-permute-start | bytes 417800 | tf_op jit(solution)/shard_map/ppermute | solution.py:449
  127.8 8.9 %collective-permute-start.9 = (bf16[272,256]{1,0:T(8,128)(2,1)S(1)}, bf16[272,256]{1,0:T(8,128)(2,1)S(1)}, u32[]{:S(2)}, u32[]{:S(2)}) collective-permute-start(bf16[272,256]{1,0:T(8,128)(2,1)S(1)} %get-tuple-element.22), channel_id=1, source_target_pairs={{0,64},{16,80},{32,96},{48,112},{64,0},{80,16},{96,32},{112,48},{1... | collective-permute-start | bytes 417800 | tf_op jit(solution)/shard_map/ppermute | solution.py:449
  130.3 9.0 %collective-permute-start.10 = (bf16[272,256]{1,0:T(8,128)(2,1)S(1)}, bf16[272,256]{1,0:T(8,128)(2,1)S(1)}, u32[]{:S(2)}, u32[]{:S(2)}) collective-permute-start(bf16[272,256]{1,0:T(8,128)(2,1)S(1)} %get-tuple-element.24), channel_id=1, source_target_pairs={{0,80},{16,64},{32,112},{48,96},{64,16},{80,0},{96,48},{112,32},{1... | collective-permute-start | bytes 417800 | tf_op jit(solution)/shard_map/ppermute | solution.py:449
  134.3 27.1 %collective-permute-start.11 = (bf16[272,256]{1,0:T(8,128)(2,1)S(1)}, bf16[272,256]{1,0:T(8,128)(2,1)S(1)}, u32[]{:S(2)}, u32[]{:S(2)}) collective-permute-start(bf16[272,256]{1,0:T(8,128)(2,1)S(1)} %get-tuple-element.23), channel_id=1, source_target_pairs={{0,96},{16,112},{32,64},{48,80},{64,32},{80,48},{96,0},{112,16},{1... | collective-permute-start | bytes 417800 | tf_op jit(solution)/shard_map/ppermute | solution.py:449
  136.1 25.3 %collective-permute-start.12 = (bf16[272,256]{1,0:T(8,128)(2,1)S(1)}, bf16[272,256]{1,0:T(8,128)(2,1)S(1)}, u32[]{:S(2)}, u32[]{:S(2)}) collective-permute-start(bf16[272,256]{1,0:T(8,128)(2,1)S(1)} %get-tuple-element.17), channel_id=1, source_target_pairs={{0,112},{16,96},{32,80},{48,64},{64,48},{80,32},{96,16},{112,0},{1... | collective-permute-start | bytes 417800 | tf_op jit(solution)/shard_map/ppermute | solution.py:449
  157.0 22.5 %all-to-all-start.2 = ((bf16[16,64,640]{2,1,0:T(8,128)(2,1)}), bf16[16,64,640]{2,1,0:T(8,128)(2,1)S(1)}, u32[]{:S(2)}, u32[]{:S(2)}) async-start(bf16[16,64,640]{2,1,0:T(8,128)(2,1)} %bitcast.25), calls=%async_computation.2 | async-start | bytes 2621440 | tf_op jit(solution)/shard_map/all_to_all | solution.py:381
  201.8 20.3 %all-to-all-start.4 = ((bf16[16,32,1152]{2,1,0:T(8,128)(2,1)}), bf16[16,32,1152]{2,1,0:T(8,128)(2,1)S(1)}, u32[]{:S(2)}, u32[]{:S(2)}) async-start(bf16[16,32,1152]{2,1,0:T(8,128)(2,1)} %bitcast.97), calls=%async_computation.4 | async-start | bytes 2359296 | tf_op jit(solution)/shard_map/all_to_all | solution.py:381
  (8 other events, 41.9 us)
Sparse Core Ops, SparseCore 0:
  9.5 69.0 all-gather.2
  80.3 37.2 all-gather.4

commit v3 on v2

--- a/solution.py
+++ b/solution.py
@@ -111,14 +111,18 @@
             )
             for head in range(OWN_HEADS):
                 lanes = slice(head * HEAD_SIZE, (head + 1) * HEAD_SIZE)
-                out_ref[rows, lanes] = norm_rotate(
+                turned = norm_rotate(
                     query[:, lanes], gain_ref[...], cos_ref[rows, :], sin_ref[rows, :]
                 ).astype(jnp.bfloat16)
-        out_ref[:, OWN_WIDTH:] = keyval_sum[...].astype(jnp.bfloat16)
+                out_ref[slot, 0, :, lanes] = turned
+                out_ref[slot, 1, :, lanes] = turned
+            keyval = keyval_sum[rows, :].astype(jnp.bfloat16)
+            out_ref[slot, 0, :, OWN_WIDTH:] = keyval
+            out_ref[slot, 1, :, OWN_WIDTH:] = keyval
 
 
 def project(tasks, spots, tokens, query_weight, keyval_weight, low_rank, up_maps, cosine, sine, gain):
-    tile = 512
+    tile = 1280
     whole = lambda *shape: pl.BlockSpec(shape, lambda k, t, s: (0,) * len(shape))
     return pl.pallas_call(
         project_kernel,
@@ -135,13 +139,13 @@
                 whole(ROWS, HEAD_SIZE),
                 whole(1, HEAD_SIZE),
             ],
-            out_specs=whole(ROWS, SENT_WIDTH),
+            out_specs=whole(GROUPS, 2, SLOT_ROWS, SENT_WIDTH),
             scratch_shapes=[
                 pltpu.VMEM((ROWS, OWN_WIDTH), jnp.float32),
                 pltpu.VMEM((ROWS, HEAD_SIZE), jnp.float32),
             ],
         ),
-        out_shape=jax.ShapeDtypeStruct((ROWS, SENT_WIDTH), jnp.bfloat16),
+        out_shape=jax.ShapeDtypeStruct((GROUPS, 2, SLOT_ROWS, SENT_WIDTH), jnp.bfloat16),
         compiler_params=pltpu.CompilerParams(vmem_limit_bytes=60 * 2**20),
         cost_estimate=pl.CostEstimate(
             flops=2 * ROWS * MODEL_WIDTH * SENT_WIDTH, bytes_accessed=13_000_000, transcendentals=0
@@ -377,6 +381,10 @@
     return [(shard, (shard + 4 * distance) % SHARDS) for shard in range(SHARDS)]
 
 
+def across_groups(bits):
+    return [(group, group ^ bits) for group in range(GROUPS)]
+
+
 def swap(block, axes, groups=None):
     return lax.all_to_all(
         block, axes, split_axis=0, concat_axis=0, tiled=True, axis_index_groups=groups
@@ -406,6 +414,22 @@
 
     part_rows = lax.all_gather(tokens, "ad", axis=0, tiled=True)
 
+    slot_suffix = generated_cache.reshape(GROUPS, SLOT_SAMPLES * 16, 2 * HEAD_SIZE)
+    slot_lengths = suffix_lengths.reshape(GROUPS, SLOT_SAMPLES, 1).astype(jnp.bfloat16)
+    slot_suffix = jnp.concatenate(
+        [slot_suffix, jnp.broadcast_to(slot_lengths, (GROUPS, SLOT_SAMPLES, 2 * HEAD_SIZE))], axis=1
+    )
+    by_core = slot_suffix.reshape((GROUPS // 2, 2) + slot_suffix.shape[1:])
+    kept = lax.dynamic_index_in_dim(by_core, group % 2, 1, keepdims=True)
+    given = lax.dynamic_index_in_dim(by_core, 1 - group % 2, 1, keepdims=True)
+    given = lax.ppermute(given, "grp", across_groups(1))
+    both = jnp.concatenate([kept, given], axis=1)
+    suffix = []
+    for k in range(GROUPS // 2):
+        block = lax.dynamic_index_in_dim(both, (group // 2) ^ k, 0, keepdims=False)
+        suffix.append(lax.ppermute(block, "grp", across_groups(2 * k)) if k else block)
+    suffix = jnp.concatenate(suffix, axis=0)
+
     owners = jnp.arange(GROUPS, dtype=jnp.int32)
     local_of_slot = lax.dynamic_index_in_dim(local_table, group, 1, keepdims=False)
     prompts = owners * OWNED + local_of_slot
@@ -422,14 +446,12 @@
         jnp.float32
     )
     rank_part = jnp.sum(rank_all * chosen[:, None, :, None], axis=2)
+    rank_part, suffix = lax.optimization_barrier((rank_part, suffix))
     rank_rows = jnp.sum(swap(rank_part.reshape(SHARDS, own_rows, ADAPTER_RANK), "ad"), axis=0)
     rank_rows = rank_rows.astype(jnp.bfloat16)
 
-    rank_rows, page_source, suffix_source, weight_source = lax.optimization_barrier(
-        (rank_rows, prompt_cache, generated_cache, output_weight)
-    )
-
-    arrived = swap(jnp.swapaxes(page_source, 0, 1), "ad", ROLE_GROUPS)
+    rank_rows, head_pages = lax.optimization_barrier((rank_rows, jnp.swapaxes(prompt_cache, 0, 1)))
+    arrived = swap(head_pages, "ad", ROLE_GROUPS)
 
     ring = [rank_rows] + [lax.ppermute(rank_rows, "ad", along_x(k)) for k in (1, 2, 3)]
     ring = jnp.stack(ring)
@@ -437,19 +459,7 @@
     every = jnp.arange(SHARDS, dtype=jnp.int32)
     spots = ((shard // 4 - every // 4) % 4) * 4 + (shard % 4 - every % 4) % 4
 
-    slot_suffix = suffix_source.reshape(GROUPS, SLOT_SAMPLES * 16, 2 * HEAD_SIZE)
-    slot_lengths = suffix_lengths.reshape(GROUPS, SLOT_SAMPLES, 1).astype(jnp.bfloat16)
-    slot_suffix = jnp.concatenate(
-        [slot_suffix, jnp.broadcast_to(slot_lengths, (GROUPS, SLOT_SAMPLES, 2 * HEAD_SIZE))], axis=1
-    )
-    suffix = []
-    for k in range(GROUPS):
-        block = lax.dynamic_index_in_dim(slot_suffix, group ^ k, 0, keepdims=False)
-        if k:
-            block = lax.ppermute(block, "grp", [(g, g ^ k) for g in range(GROUPS)])
-        suffix.append(block)
-    suffix = jnp.stack(suffix)
-
+    part_rows, weight_source = lax.optimization_barrier((part_rows, output_weight))
     slice_rows = OWN_WIDTH // GROUPS
     weight_slice = lax.dynamic_slice_in_dim(weight_source, group * slice_rows, slice_rows, 0)
     other_weight = lax.all_gather(
@@ -472,11 +482,7 @@
         query_norm_gain.reshape(1, HEAD_SIZE),
     )
     received = swap(
-        jnp.broadcast_to(
-            sent.reshape(GROUPS, 1, SLOT_ROWS, SENT_WIDTH), (GROUPS, 2, SLOT_ROWS, SENT_WIDTH)
-        ).reshape(2 * GROUPS, SLOT_ROWS, SENT_WIDTH),
-        ("grp", "ad"),
-        HEAD_GROUPS,
+        sent.reshape(2 * GROUPS, SLOT_ROWS, SENT_WIDTH), ("grp", "ad"), HEAD_GROUPS
     ).reshape(GROUPS, 2, SLOT_ROWS, SENT_WIDTH)
 
     local = lax.dynamic_index_in_dim(local_table, group, 0, keepdims=False)

time: 281 us -> 336 us (1.20)
  waiting for transfers between devices: 95.1 us -> 158 us
  starting transfers between devices: 61.3 us -> 40.3 us
  blocking collectives: 38 us -> 58.3 us
  local copies, waits for them, and re-layouts: 14.2 us -> 9.61 us
    all_gather x1, waiting for transfers between devices: 0.02 us -> 61.7 us  [shards(): part_rows = lax.all_gather(tokens, 'ad', axis=0, tiled=True)]
    all_to_all x5 -> x4, waiting for transfers between devices: 49 us -> 21.7 us  [swap(): lax.all_to_all(block, axes, split_axis=0, concat_axis=0, tiled=True, axis...]
    ppermute x7 -> x4, starting transfers between devices: 28.1 us -> 5.04 us  [the longest x3 3.42 us: shards(): lax.ppermute(block, 'grp', across_groups(2 * k))]
    all_to_all x1 -> x2, blocking collectives: 38 us -> 58.3 us  [swap(): lax.all_to_all(block, axes, split_axis=0, concat_axis=0, tiled=True, axis...]
    ppermute x3, waiting for transfers between devices: 21.2 us -> 39.4 us  [shards(): lax.ppermute(rank_rows, 'ad', along_x(k))]
    ppermute x7 -> x4, waiting for transfers between devices: 2.66 us -> 17.5 us  [the longest x3 17.5 us: shards(): lax.ppermute(block, 'grp', across_groups(2 * k))]
    ppermute x1, waiting for transfers between devices: 21 us -> 14.4 us  [shards(): lax.ppermute(weight_slice, 'ad', PARTNERS)]
    optimization_barrier x1 -> x0, local copies, waits for them, and re-layouts: 4.65 us -> none  [shards(): lax.optimization_barrier((rank_rows, prompt_cache, generated_cache, outpu...]
  transfers between devices with their start and end apart: 21 -> 17, of which waited for: 9 -> 11; matrix products, arithmetic and copies ran while one was open for 7% -> 5% of each run, Pallas kernels for 13% -> 10%
where the time goes in v3:
time: 336 us; the launch traced here: 335 us
  waiting for transfers between devices  158 us (47%)
  blocking collectives  58.3 us (17%)
  Pallas kernels  44.4 us (13%)
  starting transfers between devices  40.3 us (12%)
  between operations  13.7 us (4%)
  local copies, waits for them, and re-layouts  9.61 us (3%)
  other arithmetic  9.44 us (3%)
    all_gather x1, waiting for transfers between devices, shards(): part_rows = lax.all_gather(tokens, 'ad', axis=0, tiled=True)  61.7 us
    all_to_all x2, blocking collectives, swap(): lax.all_to_all(block, axes, split_axis=0, concat_axis=0, tiled=True, axis...  58.3 us
    ppermute x3, waiting for transfers between devices, shards(): lax.ppermute(rank_rows, 'ad', along_x(k))  39.4 us
    all_to_all x4, starting transfers between devices, swap(): lax.all_to_all(block, axes, split_axis=0, concat_axis=0, tiled=True, axis...  27.3 us
    all_to_all x4, waiting for transfers between devices, swap(): lax.all_to_all(block, axes, split_axis=0, concat_axis=0, tiled=True, axis...  21.7 us
    pallas_call x1, Pallas kernels, attend(): pl.pallas_call(attend_kernel, grid_spec=pltpu.PrefetchScalarGridSpec(num_...  21.2 us
    ppermute x3, waiting for transfers between devices, shards(): lax.ppermute(block, 'grp', across_groups(2 * k))  17.5 us
    ppermute x1, waiting for transfers between devices, shards(): lax.ppermute(weight_slice, 'ad', PARTNERS)  14.4 us
  transfers between devices with their start and end apart: 17, of which 11 were waited for; matrix products, arithmetic and copies ran while one was open for 5% of the time, Pallas kernels for 10%

profile of v3, /device:TPU:1, one launch (start us, length us, event | category | flops | bytes accessed | tf_op | source)
XLA Modules:
  0.0 335.4 jit_solution(14670277477206809652)
XLA Ops:
  7.3 61.7 %all-gather.3.cloned.1.call-done.tokens_ref = bf16[512,5120]{1,0:T(8,128)(2,1)} async-done(((bf16[32,5120]{1,0:T(8,128)(2,1)}), bf16[512,5120]{1,0:T(8,128)(2,1)}) %all-gather.3.cloned.1.call-update) | async-done | bytes 5242896 | tf_op jit(solution)/shard_map/all_gather | solution.py:415
  71.4 14.4 %collective-permute-done.10 = bf16[64,5120]{1,0:T(8,128)(2,1)S(1)} collective-permute-done((bf16[64,5120]{1,0:T(8,128)(2,1)S(1)}, bf16[64,5120]{1,0:T(8,128)(2,1)S(1)}, u32[]{:S(2)}, u32[]{:S(2)}) %collective-permute-start.10) | collective-permute-done | bytes 655392 | tf_op jit(solution)/shard_map/ppermute | solution.py:466
  87.0 1.6 collective-permute-start
  89.9 5.0 %all-to-all-start = ((bf16[16,32,320]{2,1,0:T(8,128)(2,1)}), bf16[16,32,320]{2,1,0:T(8,128)(2,1)S(1)}, u32[]{:S(2)}, u32[]{:S(2)}) async-start(bf16[16,32,320]{2,1,0:T(8,128)(2,1)} %bitcast.67), calls=%async_computation | async-start | bytes 786432 | tf_op jit(solution)/shard_map/all_to_all | solution.py:389
  95.5 2.7 collective-permute-start.3
  99.0 4.9 %all-to-all-done = bf16[16,32,320]{2,1,0:T(8,128)(2,1)S(1)} async-done(((bf16[16,32,320]{2,1,0:T(8,128)(2,1)}), bf16[16,32,320]{2,1,0:T(8,128)(2,1)S(1)}, u32[]{:S(2)}, u32[]{:S(2)}) %all-to-all-start) | async-done | bytes 327712 | tf_op jit(solution)/shard_map/all_to_all | solution.py:389
  105.0 11.1 %collective-permute-done.3 = bf16[2,272,256]{2,1,0:T(8,128)(2,1)S(1)} collective-permute-done((bf16[2,272,256]{2,1,0:T(8,128)(2,1)S(1)}, bf16[2,272,256]{2,1,0:T(8,128)(2,1)S(1)}, u32[]{:S(2)}, u32[]{:S(2)}) %collective-permute-start.3) | collective-permute-done | bytes 278560 | tf_op jit(solution)/shard_map/ppermute | solution.py:430
  116.2 6.4 %collective-permute-done.1 = bf16[2,272,256]{2,1,0:T(8,128)(2,1)S(1)} collective-permute-done((bf16[2,272,256]{2,1,0:T(8,128)(2,1)S(1)}, bf16[2,272,256]{2,1,0:T(8,128)(2,1)S(1)}, u32[]{:S(2)}, u32[]{:S(2)}) %collective-permute-start.1) | collective-permute-done | bytes 278560 | tf_op jit(solution)/shard_map/ppermute | solution.py:430
  122.7 6.7 %all-to-all-start.1 = ((f32[16,32,128]{2,1,0:T(8,128)}), f32[16,32,128]{2,1,0:T(8,128)S(1)}, u32[]{:S(2)}, u32[]{:S(2)}) async-start(f32[16,32,128]{2,1,0:T(8,128)} %bitcast.18), calls=%async_computation.1 | async-start | bytes 524288 | tf_op jit(solution)/shard_map/all_to_all | solution.py:389
  129.5 4.6 %copy.52 = bf16[4,8,256,256]{3,2,0,1:T(8,128)(2,1)} copy(bf16[4,8,256,256]{3,2,1,0:T(8,128)(2,1)} %param.14) | data formatting | bytes 8388608 | tf_op args[1]
  134.1 2.9 all-to-all-done.1
  137.1 4.6 %all-to-all-start.3 = ((bf16[8,4,256,256]{3,2,1,0:T(8,128)(2,1)}), bf16[8,4,256,256]{3,2,1,0:T(8,128)(2,1)}, u32[]{:S(2)}, u32[]{:S(2)}) async-start(bf16[8,4,256,256]{3,2,1,0:T(8,128)(2,1)} %bitcast.68), calls=%async_computation.3 | async-start | bytes 8388608 | tf_op jit(solution)/shard_map/all_to_all | solution.py:389
  144.1 2.5 collective-permute-start.6
  147.2 36.1 %collective-permute-done.6 = bf16[32,128]{1,0:T(8,128)(2,1)S(1)} collective-permute-done((bf16[32,128]{1,0:T(8,128)(2,1)S(1)}, bf16[32,128]{1,0:T(8,128)(2,1)S(1)}, u32[]{:S(2)}, u32[]{:S(2)}) %collective-permute-start.6) | collective-permute-done | bytes 8224 | tf_op jit(solution)/shard_map/ppermute | solution.py:456
  183.3 3.3 collective-permute-done.4
  186.6 2.3 collective-permute-start.9
  190.7 2.7 collective-permute-done.8
  194.4 13.0 %project.1 = bf16[8,2,64,640]{3,2,1,0:T(8,128)(2,1)} custom-call(s32[8]{0:T(128)} %copy-done.5, s32[16]{0:T(128)} %fusion.17.spot_ref, bf16[512,5120]{1,0:T(8,128)(2,1)} %all-gather.3.cloned.1.call-done.tokens_ref, bf16[5120,512]{1,0:T(8,128)(2,1)} %query_ref.1, bf16[128,5120]{1,0:T(8,128)(2,1)} %bitcast.72, bf16[16,32,128]{2,1,0:T(8,128)(2,1)} %bitcast.76, ...), custom_call_target="tpu_custom_call" | custom-call | flops 3355443200 | bytes 13000000 | tf_op jit(solution)/shard_map/project/pallas_call | solution.py:127
  207.4 11.0 %all-to-all-start.2 = ((bf16[16,64,640]{2,1,0:T(8,128)(2,1)}), bf16[16,64,640]{2,1,0:T(8,128)(2,1)S(1)}, u32[]{:S(2)}, u32[]{:S(2)}) async-start(bf16[16,64,640]{2,1,0:T(8,128)(2,1)} %bitcast.70), calls=%async_computation.2 | async-start | bytes 2621440 | tf_op jit(solution)/shard_map/all_to_all | solution.py:389
  222.6 13.9 %all-to-all-done.2 = bf16[16,64,640]{2,1,0:T(8,128)(2,1)S(1)} async-done(((bf16[16,64,640]{2,1,0:T(8,128)(2,1)}), bf16[16,64,640]{2,1,0:T(8,128)(2,1)S(1)}, u32[]{:S(2)}, u32[]{:S(2)}) %all-to-all-start.2) | async-done | bytes 1310752 | tf_op jit(solution)/shard_map/all_to_all | solution.py:389
  237.6 21.2 %attend.1 = bf16[8,2,32,1152]{3,2,1,0:T(8,128)(2,1)} custom-call(s32[8]{0:T(128)} %copy-done.7, s32[8]{0:T(128)} %get-tuple-element.17.local_ref, s32[8]{0:T(128)} %broadcast_xor_fusion.reach_ref, s32[2]{0:T(128)} %pad_add_fusion.place_ref, bf16[8,2,64,640]{3,2,1,0:T(8,128)(2,1)} %bitcast.73, bf16[8,4,256,256]{3,2,1,0:T(8,128)(2,1)} %all-to-all-done.3.page_ref, ...), custom_call_target="tpu_custom_call" | custom-call | flops 7650410496 | bytes 8000000 | tf_op jit(solution)/shard_map/attend/pallas_call | solution.py:272
  258.8 21.3 %all_to_all.30 = bf16[16,32,1152]{2,1,0:T(8,128)(2,1)} all-to-all(bf16[16,32,1152]{2,1,0:T(8,128)(2,1)} %bitcast.74), channel_id=1, replica_groups={{0,1,16,17,32,33,48,49,64,65,80,81,96,97,112,113},{2,3,18,19,34,35,50,5..., dimensions={0} | all-to-all | bytes 2359296 | tf_op jit(solution)/shard_map/all_to_all | solution.py:389
  280.1 10.3 %output_part.1 = bf16[256,5120]{1,0:T(8,128)(2,1)} custom-call(s32[2]{0:T(128)} %pad_add_fusion.place_ref, bf16[8,2,32,1152]{3,2,1,0:T(8,128)(2,1)} %bitcast.71, bf16[512,5120]{1,0:T(8,128)(2,1)} %own_ref.1, bf16[512,5120]{1,0:T(8,128)(2,1)} %all-gather.5.cloned.1.call-done.other_ref), custom_call_target="tpu_custom_call" | custom-call | flops 2684354560 | bytes 14000000 | tf_op jit(solution)/shard_map/output_part/pallas_call | solution.py:354
  290.4 37.0 %all_to_all.31 = bf16[8,32,5120]{2,1,0:T(8,128)(2,1)S(1)} all-to-all(bf16[8,32,5120]{2,1,0:T(8,128)(2,1)} %bitcast.69), channel_id=1, replica_groups={{0,3,4,7,8,11,12,15},{1,2,5,6,9,10,13,14},{16,19,20,23,24,27,28,31},{17..., dimensions={0} | all-to-all | bytes 5242880 | tf_op jit(solution)/shard_map/all_to_all | solution.py:389
  (82 shorter events, 20.4 us)
Async XLA Ops:
  6.5 80.2 %copy-start.9 = (s32[128]{0:T(128)S(1)}, s32[128]{0:T(128)}, u32[]{:S(2)}) copy-start(s32[128]{0:T(128)} %param.16) | copy-start | bytes 1540
  6.5 62.5 %all-gather.3.cloned.1.call-start = ((), (), s32[]{:S(2)}) async-start(), calls=%async_computation.6 | async-start | bytes 5570560 | tf_op jit(solution)/shard_map/all_gather | solution.py:415
  7.3 79.7 %copy-start.3 = (bf16[128,16,256]{2,1,0:T(8,128)(2,1)S(1)}, bf16[128,16,256]{2,1,0:T(8,128)(2,1)}, u32[]{:S(2)}) copy-start(bf16[128,16,256]{2,1,0:T(8,128)(2,1)} %param.15) | copy-start | bytes 3145732
  7.3 272.8 %all-gather.5.cloned.1.call-start = ((), (), s32[]{:S(2)}) async-start(), calls=%async_computation.7 | async-start | bytes 5898240 | tf_op jit(solution)/shard_map/all_gather | solution.py:465
  70.1 15.7 %collective-permute-start.10 = (bf16[64,5120]{1,0:T(8,128)(2,1)S(1)}, bf16[64,5120]{1,0:T(8,128)(2,1)S(1)}, u32[]{:S(2)}, u32[]{:S(2)}) collective-permute-start(bf16[64,5120]{1,0:T(8,128)(2,1)S(1)} %constant_dynamic-slice_fusion), channel_id=1, source_target_pairs={{0,1},{1,0},{2,3},{3,2},{4,5},{5,4},{6,7},{7,6},{8,9},{9,8},{10,11... | collective-permute-start | bytes 1966088 | tf_op jit(solution)/shard_map/ppermute | solution.py:466
  87.0 7.8 %copy-start.6 = (s32[32,2]{0,1:T(2,128)S(1)}, s32[32,2]{0,1:T(2,128)}, u32[]{:S(2)}) copy-start(s32[32,2]{0,1:T(2,128)} %param.17) | copy-start | bytes 772
  87.0 8.2 %copy-start.10 = (s32[32]{0:T(128)S(1)}, s32[32]{0:T(128)}, u32[]{:S(2)}) copy-start(s32[32]{0:T(128)} %param.18) | copy-start | bytes 388
  87.0 8.3 %collective-permute-start = (bf16[4,1,272,256]{3,2,1,0:T(8,128)(2,1)S(1)}, bf16[4,1,272,256]{3,2,1,0:T(8,128)(2,1)S(1)}, u32[]{:S(2)}, u32[]{:S(2)}) collective-permute-start(bf16[4,1,272,256]{3,2,1,0:T(8,128)(2,1)S(1)} %get-tuple-element.25), channel_id=1, source_target_pairs={{0,16},{16,0},{32,48},{48,32},{64,80},{80,64},{96,112},{112,96},{1... | collective-permute-start | bytes 1671176 | tf_op jit(solution)/shard_map/ppermute | solution.py:425
  89.9 14.1 %all-to-all-start = ((bf16[16,32,320]{2,1,0:T(8,128)(2,1)}), bf16[16,32,320]{2,1,0:T(8,128)(2,1)S(1)}, u32[]{:S(2)}, u32[]{:S(2)}) async-start(bf16[16,32,320]{2,1,0:T(8,128)(2,1)} %bitcast.67), calls=%async_computation | async-start | bytes 786432 | tf_op jit(solution)/shard_map/all_to_all | solution.py:389
  95.4 3.6 %copy-start.5 = (s32[8]{0:T(128)}, s32[8]{0:T(128)S(1)}, u32[]{:S(2)}) copy-start(s32[8]{0:T(128)S(1)} %select_reduce_fusion.1.task_ref) | copy-start | bytes 100
  95.4 8.5 %copy-start.8 = (bf16[320,4,128]{2,1,0:T(4,128)(2,1)S(1)}, bf16[320,4,128]{2,1,0:T(4,128)(2,1)}, u32[]{:S(2)}) copy-start(bf16[320,4,128]{2,1,0:T(4,128)(2,1)} %param.22) | copy-start | bytes 983044
  95.5 20.6 %collective-permute-start.3 = (bf16[2,272,256]{2,1,0:T(8,128)(2,1)S(1)}, bf16[2,272,256]{2,1,0:T(8,128)(2,1)S(1)}, u32[]{:S(2)}, u32[]{:S(2)}) collective-permute-start(bf16[2,272,256]{2,1,0:T(8,128)(2,1)S(1)} %get-tuple-element.24), channel_id=1, source_target_pairs={{0,96},{16,112},{32,64},{48,80},{64,32},{80,48},{96,0},{112,16},{1... | collective-permute-start | bytes 835592 | tf_op jit(solution)/shard_map/ppermute | solution.py:430
  98.3 17.9 %collective-permute-start.2 = (bf16[2,272,256]{2,1,0:T(8,128)(2,1)S(1)}, bf16[2,272,256]{2,1,0:T(8,128)(2,1)S(1)}, u32[]{:S(2)}, u32[]{:S(2)}) collective-permute-start(bf16[2,272,256]{2,1,0:T(8,128)(2,1)S(1)} %get-tuple-element.23), channel_id=1, source_target_pairs={{0,64},{16,80},{32,96},{48,112},{64,0},{80,16},{96,32},{112,48},{1... | collective-permute-start | bytes 835592 | tf_op jit(solution)/shard_map/ppermute | solution.py:430
  98.7 23.9 %collective-permute-start.1 = (bf16[2,272,256]{2,1,0:T(8,128)(2,1)S(1)}, bf16[2,272,256]{2,1,0:T(8,128)(2,1)S(1)}, u32[]{:S(2)}, u32[]{:S(2)}) collective-permute-start(bf16[2,272,256]{2,1,0:T(8,128)(2,1)S(1)} %get-tuple-element.22), channel_id=1, source_target_pairs={{0,32},{16,48},{32,0},{48,16},{64,96},{80,112},{96,64},{112,80},{1... | collective-permute-start | bytes 835592 | tf_op jit(solution)/shard_map/ppermute | solution.py:430
  122.7 97.6 %copy-start.2 = (bf16[8,272,256]{2,1,0:T(8,128)(2,1)}, bf16[8,272,256]{2,1,0:T(8,128)(2,1)S(1)}, u32[]{:S(2)}) copy-start(bf16[8,272,256]{2,1,0:T(8,128)(2,1)S(1)} %pad_maximum_fusion.suffix_ref) | copy-start | bytes 3342340
  122.7 14.3 %all-to-all-start.1 = ((f32[16,32,128]{2,1,0:T(8,128)}), f32[16,32,128]{2,1,0:T(8,128)S(1)}, u32[]{:S(2)}, u32[]{:S(2)}) async-start(f32[16,32,128]{2,1,0:T(8,128)} %bitcast.18), calls=%async_computation.1 | async-start | bytes 524288 | tf_op jit(solution)/shard_map/all_to_all | solution.py:389
  137.1 70.4 %all-to-all-start.3 = ((bf16[8,4,256,256]{3,2,1,0:T(8,128)(2,1)}), bf16[8,4,256,256]{3,2,1,0:T(8,128)(2,1)}, u32[]{:S(2)}, u32[]{:S(2)}) async-start(bf16[8,4,256,256]{3,2,1,0:T(8,128)(2,1)} %bitcast.68), calls=%async_computation.3 | async-start | bytes 8388608 | tf_op jit(solution)/shard_map/all_to_all | solution.py:389
  144.1 39.2 %collective-permute-start.6 = (bf16[32,128]{1,0:T(8,128)(2,1)S(1)}, bf16[32,128]{1,0:T(8,128)(2,1)S(1)}, u32[]{:S(2)}, u32[]{:S(2)}) collective-permute-start(bf16[32,128]{1,0:T(8,128)(2,1)S(1)} %reduce_sum.81), channel_id=1, source_target_pairs={{0,3},{1,0},{2,1},{3,2},{4,7},{5,4},{6,5},{7,6},{8,11},{9,8},{10,9... | collective-permute-start | bytes 24584 | tf_op jit(solution)/shard_map/ppermute | solution.py:456
  146.6 36.7 %collective-permute-start.5 = (bf16[32,128]{1,0:T(8,128)(2,1)S(1)}, bf16[32,128]{1,0:T(8,128)(2,1)S(1)}, u32[]{:S(2)}, u32[]{:S(2)}) collective-permute-start(bf16[32,128]{1,0:T(8,128)(2,1)S(1)} %reduce_sum.81), channel_id=1, source_target_pairs={{0,2},{1,3},{2,0},{3,1},{4,6},{5,7},{6,4},{7,5},{8,10},{9,11},{10,... | collective-permute-start | bytes 24584 | tf_op jit(solution)/shard_map/ppermute | solution.py:456
  146.6 40.0 %collective-permute-start.4 = (bf16[32,128]{1,0:T(8,128)(2,1)S(1)}, bf16[32,128]{1,0:T(8,128)(2,1)S(1)}, u32[]{:S(2)}, u32[]{:S(2)}) collective-permute-start(bf16[32,128]{1,0:T(8,128)(2,1)S(1)} %reduce_sum.81), channel_id=1, source_target_pairs={{0,1},{1,2},{2,3},{3,0},{4,5},{5,6},{6,7},{7,4},{8,9},{9,10},{10,1... | collective-permute-start | bytes 24584 | tf_op jit(solution)/shard_map/ppermute | solution.py:456
  186.6 4.2 %collective-permute-start.9 = (bf16[4,32,128]{2,1,0:T(8,128)(2,1)S(1)}, bf16[4,32,128]{2,1,0:T(8,128)(2,1)S(1)}, u32[]{:S(2)}, u32[]{:S(2)}) collective-permute-start(bf16[4,32,128]{2,1,0:T(8,128)(2,1)S(1)} %get-tuple-element.28), channel_id=1, source_target_pairs={{0,12},{1,13},{2,14},{3,15},{4,0},{5,1},{6,2},{7,3},{8,4},{9,5},{1... | collective-permute-start | bytes 98312 | tf_op jit(solution)/shard_map/ppermute | solution.py:458
  188.9 4.5 %collective-permute-start.8 = (bf16[4,32,128]{2,1,0:T(8,128)(2,1)S(1)}, bf16[4,32,128]{2,1,0:T(8,128)(2,1)S(1)}, u32[]{:S(2)}, u32[]{:S(2)}) collective-permute-start(bf16[4,32,128]{2,1,0:T(8,128)(2,1)S(1)} %get-tuple-element.28), channel_id=1, source_target_pairs={{0,8},{1,9},{2,10},{3,11},{4,12},{5,13},{6,14},{7,15},{8,0},{9,1},... | collective-permute-start | bytes 98312 | tf_op jit(solution)/shard_map/ppermute | solution.py:458
  189.5 4.3 %collective-permute-start.7 = (bf16[4,32,128]{2,1,0:T(8,128)(2,1)S(1)}, bf16[4,32,128]{2,1,0:T(8,128)(2,1)S(1)}, u32[]{:S(2)}, u32[]{:S(2)}) collective-permute-start(bf16[4,32,128]{2,1,0:T(8,128)(2,1)S(1)} %get-tuple-element.28), channel_id=1, source_target_pairs={{0,4},{1,5},{2,6},{3,7},{4,8},{5,9},{6,10},{7,11},{8,12},{9,13},{1... | collective-permute-start | bytes 98312 | tf_op jit(solution)/shard_map/ppermute | solution.py:458
  207.4 29.1 %all-to-all-start.2 = ((bf16[16,64,640]{2,1,0:T(8,128)(2,1)}), bf16[16,64,640]{2,1,0:T(8,128)(2,1)S(1)}, u32[]{:S(2)}, u32[]{:S(2)}) async-start(bf16[16,64,640]{2,1,0:T(8,128)(2,1)} %bitcast.70), calls=%async_computation.2 | async-start | bytes 2621440 | tf_op jit(solution)/shard_map/all_to_all | solution.py:389
  (4 other events, 6.6 us)
Sparse Core Ops, SparseCore 0:
  9.5 59.4 all-gather.2
  86.8 48.0 all-gather.4

commit v4 on v3

--- a/solution.py
+++ b/solution.py
@@ -26,6 +26,7 @@
 OWN_WIDTH = OWN_HEADS * HEAD_SIZE
 HEAD_FAN = 2 * OWN_HEADS
 SENT_WIDTH = OWN_WIDTH + HEAD_SIZE
+TILE_HEADS = 4
 BACK_WIDTH = HEAD_FAN * HEAD_SIZE + HEAD_SIZE
 
 theta_base = 1000000.0
@@ -114,15 +115,12 @@
                 turned = norm_rotate(
                     query[:, lanes], gain_ref[...], cos_ref[rows, :], sin_ref[rows, :]
                 ).astype(jnp.bfloat16)
-                out_ref[slot, 0, :, lanes] = turned
-                out_ref[slot, 1, :, lanes] = turned
-            keyval = keyval_sum[rows, :].astype(jnp.bfloat16)
-            out_ref[slot, 0, :, OWN_WIDTH:] = keyval
-            out_ref[slot, 1, :, OWN_WIDTH:] = keyval
+                out_ref[slot, :, lanes] = turned
+            out_ref[slot, :, OWN_WIDTH:] = keyval_sum[rows, :].astype(jnp.bfloat16)
 
 
 def project(tasks, spots, tokens, query_weight, keyval_weight, low_rank, up_maps, cosine, sine, gain):
-    tile = 1280
+    tile = 2560
     whole = lambda *shape: pl.BlockSpec(shape, lambda k, t, s: (0,) * len(shape))
     return pl.pallas_call(
         project_kernel,
@@ -139,16 +137,16 @@
                 whole(ROWS, HEAD_SIZE),
                 whole(1, HEAD_SIZE),
             ],
-            out_specs=whole(GROUPS, 2, SLOT_ROWS, SENT_WIDTH),
+            out_specs=whole(GROUPS, SLOT_ROWS, SENT_WIDTH),
             scratch_shapes=[
                 pltpu.VMEM((ROWS, OWN_WIDTH), jnp.float32),
                 pltpu.VMEM((ROWS, HEAD_SIZE), jnp.float32),
             ],
         ),
-        out_shape=jax.ShapeDtypeStruct((GROUPS, 2, SLOT_ROWS, SENT_WIDTH), jnp.bfloat16),
+        out_shape=jax.ShapeDtypeStruct((GROUPS, SLOT_ROWS, SENT_WIDTH), jnp.bfloat16),
         compiler_params=pltpu.CompilerParams(vmem_limit_bytes=60 * 2**20),
         cost_estimate=pl.CostEstimate(
-            flops=2 * ROWS * MODEL_WIDTH * SENT_WIDTH, bytes_accessed=13_000_000, transcendentals=0
+            flops=20 * ROWS * MODEL_WIDTH * SENT_WIDTH, bytes_accessed=13_000_000, transcendentals=0
         ),
         name="project",
     )(tasks, spots, tokens, query_weight, keyval_weight, low_rank, up_maps, cosine, sine, gain)
@@ -159,7 +157,8 @@
     local_ref,
     reach_ref,
     place_ref,
-    sent_ref,
+    own_ref,
+    other_ref,
     page_ref,
     suffix_ref,
     cos_ref,
@@ -175,8 +174,10 @@
     values = jnp.concatenate(
         [jnp.ones((span, HEAD_SIZE), jnp.bfloat16), pages[:, HEAD_SIZE:]], axis=1
     )
-    low_part = sent_ref[0, 0, :, OWN_WIDTH:].astype(jnp.float32)
-    high_part = sent_ref[0, 1, :, OWN_WIDTH:].astype(jnp.float32)
+    first_sent = jnp.where(half == 0, own_ref[0], other_ref[0])
+    second_sent = jnp.where(half == 0, other_ref[0], own_ref[0])
+    low_part = first_sent[:, OWN_WIDTH:].astype(jnp.float32)
+    high_part = second_sent[:, OWN_WIDTH:].astype(jnp.float32)
     lane = lax.broadcasted_iota(jnp.int32, (SLOT_ROWS, HEAD_SIZE), 1)
     low_lanes = lane < HEAD_SIZE // 2
     new_keys = jnp.where(low_lanes, low_part, pltpu.roll(high_part, HEAD_SIZE // 2, 1))
@@ -216,44 +217,53 @@
     bias = jnp.concatenate(
         [jnp.where(suffix_seen, 0.0, masked_low), jnp.where(new_seen, 0.0, masked_low)], axis=1
     )
-    pair_bias = jnp.concatenate([bias, bias], axis=0)
+    bias = jnp.concatenate([bias] * TILE_HEADS, axis=0)
     logs = jnp.zeros((SLOT_ROWS, HEAD_SIZE), jnp.float32)
-    for first in range(0, HEAD_FAN, 2):
-        source, start = divmod(first, OWN_HEADS)
-        start = start * HEAD_SIZE
-        query = jnp.concatenate(
-            [
-                sent_ref[0, source, :, start : start + HEAD_SIZE],
-                sent_ref[0, source, :, start + HEAD_SIZE : start + 2 * HEAD_SIZE],
-            ],
-            axis=0,
-        )
-        prefix_score = dot_nt(query, keys)
-        extra_score = dot_nt(query, extra_keys) + pair_bias
+
+    def finish(first, total, peak):
+        nonlocal logs
+        denominator = total[:, :HEAD_SIZE]
+        attended = (total[:, HEAD_SIZE:] / denominator).astype(jnp.bfloat16)
+        log_sum = peak + jnp.log2(denominator)
+        for index in range(TILE_HEADS):
+            head = first + index
+            rows = slice(index * SLOT_ROWS, (index + 1) * SLOT_ROWS)
+            top = attended[rows][:HALF_ROWS]
+            low = attended[rows][HALF_ROWS:]
+            lanes = slice(head * HEAD_SIZE, (head + 1) * HEAD_SIZE)
+            out_ref[0, 0, :, lanes] = jnp.where(flip == 0, top, low)
+            out_ref[0, 1, :, lanes] = jnp.where(flip == 0, low, top)
+            logs = jnp.where(lane == head, log_sum[rows], logs)
+
+    def query_of(first):
+        query = []
+        for head in range(first, first + TILE_HEADS):
+            source, start = divmod(head, OWN_HEADS)
+            sent = second_sent if source else first_sent
+            query.append(sent[:, start * HEAD_SIZE : (start + 1) * HEAD_SIZE])
+        return jnp.concatenate(query, axis=0)
+
+
+    def scores(first):
+        query = query_of(first)
+        return dot_nt(query, keys), dot_nt(query, extra_keys) + bias
+
+    tiles = list(range(0, HEAD_FAN, TILE_HEADS))
+    ready = scores(tiles[0])
+    for number, first in enumerate(tiles):
+        prefix_score, extra_score = ready
+        if number + 1 < len(tiles):
+            ready = scores(tiles[number + 1])
         peak = jnp.maximum(
             jnp.max(prefix_score, axis=-1, keepdims=True),
             jnp.max(extra_score, axis=-1, keepdims=True),
         )
-        scaled_peak = peak * exponent_scale
-        prefix_weight = jnp.exp2(prefix_score * exponent_scale - scaled_peak).astype(jnp.bfloat16)
-        extra_weight = jnp.exp2(extra_score * exponent_scale - scaled_peak).astype(jnp.bfloat16)
+        prefix_weight = jnp.exp2(prefix_score - peak).astype(jnp.bfloat16)
+        extra_weight = jnp.exp2(extra_score - peak).astype(jnp.bfloat16)
         total = jnp.dot(prefix_weight, values, preferred_element_type=jnp.float32) + jnp.dot(
             extra_weight, extra_values, preferred_element_type=jnp.float32
         )
-        denominator = total[:, :HEAD_SIZE]
-        attended = total[:, HEAD_SIZE:] / denominator
-        log_sum = scaled_peak + jnp.log2(denominator)
-        for index in range(2):
-            head = first + index
-            rows = slice(index * SLOT_ROWS, (index + 1) * SLOT_ROWS)
-            top = attended[index * SLOT_ROWS : index * SLOT_ROWS + HALF_ROWS].astype(jnp.bfloat16)
-            low = attended[index * SLOT_ROWS + HALF_ROWS : (index + 1) * SLOT_ROWS].astype(
-                jnp.bfloat16
-            )
-            lanes = slice(head * HEAD_SIZE, (head + 1) * HEAD_SIZE)
-            out_ref[0, 0, :, lanes] = jnp.where(flip == 0, top, low)
-            out_ref[0, 1, :, lanes] = jnp.where(flip == 0, low, top)
-            logs = jnp.where(lane == head, log_sum[rows], logs)
+        finish(first, total, peak)
     high_term = logs.astype(jnp.bfloat16).astype(jnp.float32)
     rest = logs - high_term
     mid_term = rest.astype(jnp.bfloat16).astype(jnp.float32)
@@ -267,7 +277,7 @@
     out_ref[0, 1, :, HEAD_FAN * HEAD_SIZE :] = jnp.where(flip == 0, low, top)
 
 
-def attend(order, local, reach, place, sent, pages, suffix, cosine, sine, gain):
+def attend(order, local, reach, place, own, other, pages, suffix, cosine, sine, gain):
     block = PROMPT_TOKENS // SHARDS
     return pl.pallas_call(
         attend_kernel,
@@ -275,7 +285,8 @@
             num_scalar_prefetch=4,
             grid=(GROUPS,),
             in_specs=[
-                pl.BlockSpec((1, 2, SLOT_ROWS, SENT_WIDTH), lambda i, o, l, r, p: (o[i], 0, 0, 0)),
+                pl.BlockSpec((1, SLOT_ROWS, SENT_WIDTH), lambda i, o, l, r, p: (r[i], 0, 0)),
+                pl.BlockSpec((1, SLOT_ROWS, SENT_WIDTH), lambda i, o, l, r, p: (r[i], 0, 0)),
                 pl.BlockSpec(
                     (GROUPS, 1, block, 2 * HEAD_SIZE), lambda i, o, l, r, p: (0, l[i], 0, 0)
                 ),
@@ -293,12 +304,12 @@
         out_shape=jax.ShapeDtypeStruct((GROUPS, 2, HALF_ROWS, BACK_WIDTH), jnp.bfloat16),
         compiler_params=pltpu.CompilerParams(vmem_limit_bytes=60 * 2**20),
         cost_estimate=pl.CostEstimate(
-            flops=2 * GROUPS * 512 * 2432 * 384,
+            flops=20 * GROUPS * 512 * 2432 * 384,
             bytes_accessed=8_000_000,
             transcendentals=GROUPS * 512 * 2432,
         ),
         name="attend",
-    )(order, local, reach, place, sent, pages, suffix, cosine, sine, gain)
+    )(order, local, reach, place, own, other, pages, suffix, cosine, sine, gain)
 
 
 def output_kernel(place_ref, back_ref, own_ref, other_ref, out_ref, mixed):
@@ -349,7 +360,7 @@
 
 
 def output_part(place, back, own_weight, other_weight):
-    tile = 1024
+    tile = 2560
     rows = GROUPS * HALF_ROWS
     return pl.pallas_call(
         output_kernel,
@@ -383,6 +394,19 @@
 
 def across_groups(bits):
     return [(group, group ^ bits) for group in range(GROUPS)]
+
+
+def exchange_groups(blocks, group):
+    by_core = blocks.reshape((GROUPS // 2, 2) + blocks.shape[1:])
+    kept = lax.dynamic_index_in_dim(by_core, group % 2, 1, keepdims=True)
+    given = lax.dynamic_index_in_dim(by_core, 1 - group % 2, 1, keepdims=True)
+    given = lax.ppermute(given, "grp", across_groups(1))
+    both = jnp.concatenate([kept, given], axis=1)
+    arrived = []
+    for k in range(GROUPS // 2):
+        block = lax.dynamic_index_in_dim(both, (group // 2) ^ k, 0, keepdims=False)
+        arrived.append(lax.ppermute(block, "grp", across_groups(2 * k)) if k else block)
+    return jnp.concatenate(arrived, axis=0)
 
 
 def swap(block, axes, groups=None):
@@ -419,16 +443,7 @@
     slot_suffix = jnp.concatenate(
         [slot_suffix, jnp.broadcast_to(slot_lengths, (GROUPS, SLOT_SAMPLES, 2 * HEAD_SIZE))], axis=1
     )
-    by_core = slot_suffix.reshape((GROUPS // 2, 2) + slot_suffix.shape[1:])
-    kept = lax.dynamic_index_in_dim(by_core, group % 2, 1, keepdims=True)
-    given = lax.dynamic_index_in_dim(by_core, 1 - group % 2, 1, keepdims=True)
-    given = lax.ppermute(given, "grp", across_groups(1))
-    both = jnp.concatenate([kept, given], axis=1)
-    suffix = []
-    for k in range(GROUPS // 2):
-        block = lax.dynamic_index_in_dim(both, (group // 2) ^ k, 0, keepdims=False)
-        suffix.append(lax.ppermute(block, "grp", across_groups(2 * k)) if k else block)
-    suffix = jnp.concatenate(suffix, axis=0)
+    suffix = exchange_groups(slot_suffix, group)
 
     owners = jnp.arange(GROUPS, dtype=jnp.int32)
     local_of_slot = lax.dynamic_index_in_dim(local_table, group, 1, keepdims=False)
@@ -446,25 +461,25 @@
         jnp.float32
     )
     rank_part = jnp.sum(rank_all * chosen[:, None, :, None], axis=2)
-    rank_part, suffix = lax.optimization_barrier((rank_part, suffix))
     rank_rows = jnp.sum(swap(rank_part.reshape(SHARDS, own_rows, ADAPTER_RANK), "ad"), axis=0)
     rank_rows = rank_rows.astype(jnp.bfloat16)
 
-    rank_rows, head_pages = lax.optimization_barrier((rank_rows, jnp.swapaxes(prompt_cache, 0, 1)))
-    arrived = swap(head_pages, "ad", ROLE_GROUPS)
-
     ring = [rank_rows] + [lax.ppermute(rank_rows, "ad", along_x(k)) for k in (1, 2, 3)]
     ring = jnp.stack(ring)
+
     low_rank = jnp.stack([ring] + [lax.ppermute(ring, "ad", along_y(k)) for k in (1, 2, 3)])
     every = jnp.arange(SHARDS, dtype=jnp.int32)
     spots = ((shard // 4 - every // 4) % 4) * 4 + (shard % 4 - every % 4) % 4
 
-    part_rows, weight_source = lax.optimization_barrier((part_rows, output_weight))
     slice_rows = OWN_WIDTH // GROUPS
-    weight_slice = lax.dynamic_slice_in_dim(weight_source, group * slice_rows, slice_rows, 0)
-    other_weight = lax.all_gather(
-        lax.ppermute(weight_slice, "ad", PARTNERS), "grp", axis=0, tiled=True
-    )
+    weight_slice = lax.dynamic_slice_in_dim(output_weight, group * slice_rows, slice_rows, 0)
+    low_rank, head_pages, weight_slice = lax.optimization_barrier(
+        (low_rank, jnp.swapaxes(prompt_cache, 0, 1), weight_slice)
+    )
+    arrived = swap(head_pages, "ad", ROLE_GROUPS)
+    weight_slice = lax.ppermute(weight_slice, "ad", PARTNERS)
+    part_rows, weight_slice = lax.optimization_barrier((part_rows, weight_slice))
+    other_weight = lax.all_gather(weight_slice, "grp", axis=0, tiled=True)
 
     steps = jnp.arange(DECODE_STEPS, dtype=jnp.int32)
     position = (PROMPT_TOKENS + suffix_lengths[:, None] + steps[None, :]).astype(jnp.float32)
@@ -479,11 +494,10 @@
         adapter_up_maps,
         cosine,
         sine,
-        query_norm_gain.reshape(1, HEAD_SIZE),
-    )
-    received = swap(
-        sent.reshape(2 * GROUPS, SLOT_ROWS, SENT_WIDTH), ("grp", "ad"), HEAD_GROUPS
-    ).reshape(GROUPS, 2, SLOT_ROWS, SENT_WIDTH)
+        query_norm_gain.reshape(1, HEAD_SIZE) * exponent_scale,
+    )
+    own_sent = exchange_groups(sent, group)
+    other_sent = lax.ppermute(own_sent, "ad", PARTNERS)
 
     local = lax.dynamic_index_in_dim(local_table, group, 0, keepdims=False)
     rank_key = local * GROUPS + owners
@@ -501,7 +515,8 @@
         local_sorted,
         order ^ group,
         place,
-        received,
+        own_sent,
+        other_sent,
         arrived,
         suffix,
         far_cosine,

time: 336 us -> 238 us (0.71)
  waiting for transfers between devices: 158 us -> 60.6 us
  starting transfers between devices: 40.3 us -> 33.4 us
  blocking collectives: 58.3 us -> 63.7 us
  Pallas kernels: 44.4 us -> 39.7 us
  other arithmetic: 9.44 us -> 13.6 us
    all_gather x1, waiting for transfers between devices: 61.7 us -> 0.01 us  [shards(): part_rows = lax.all_gather(tokens, 'ad', axis=0, tiled=True)]
    ppermute x3, waiting for transfers between devices: 39.4 us -> 3.69 us  [shards(): lax.ppermute(rank_rows, 'ad', along_x(k))]
    ppermute x5 -> x10, waiting for transfers between devices: 31.9 us -> 43.7 us  [the longest x1 15.8 us: shards(): weight_slice = lax.ppermute(weight_slice, 'ad', PARTNERS)]
    all_to_all x4 -> x3, starting transfers between devices: 27.3 us -> 16.1 us  [swap(): lax.all_to_all(block, axes, split_axis=0, concat_axis=0, tiled=True, axis...]
    all_to_all x4 -> x3, waiting for transfers between devices: 21.7 us -> 12.4 us  [swap(): lax.all_to_all(block, axes, split_axis=0, concat_axis=0, tiled=True, axis...]
    ppermute x5 -> x10, starting transfers between devices: 6.31 us -> 13 us  [the longest x6 9.41 us: exchange_groups(): lax.ppermute(block, 'grp', across_groups(2 * k))]
    all_to_all x2, blocking collectives: 58.3 us -> 63.7 us  [swap(): lax.all_to_all(block, axes, split_axis=0, concat_axis=0, tiled=True, axis...]
  transfers between devices with their start and end apart: 17 -> 21, of which waited for: 11 -> 11; matrix products, arithmetic and copies ran while one was open for 5% -> 10% of each run, Pallas kernels for 10% -> 13%
where the time goes in v4:
time: 238 us; the launch traced here: 237 us
  blocking collectives  63.7 us (27%)
  waiting for transfers between devices  60.6 us (25%)
  Pallas kernels  39.7 us (17%)
  starting transfers between devices  33.4 us (14%)
  between operations  13.7 us (6%)
  other arithmetic  13.6 us (6%)
  local copies, waits for them, and re-layouts  10.8 us (5%)
    all_to_all x2, blocking collectives, swap(): lax.all_to_all(block, axes, split_axis=0, concat_axis=0, tiled=True, axis...  63.7 us
    pallas_call x1, Pallas kernels, attend(): pl.pallas_call(attend_kernel, grid_spec=pltpu.PrefetchScalarGridSpec(num_...  18.4 us
    all_to_all x3, starting transfers between devices, swap(): lax.all_to_all(block, axes, split_axis=0, concat_axis=0, tiled=True, axis...  16.1 us
    ppermute x1, waiting for transfers between devices, shards(): weight_slice = lax.ppermute(weight_slice, 'ad', PARTNERS)  15.8 us
    ppermute x6, waiting for transfers between devices, exchange_groups(): lax.ppermute(block, 'grp', across_groups(2 * k))  15.1 us
    pallas_call x1, Pallas kernels, project(): pl.pallas_call(project_kernel, grid_spec=pltpu.PrefetchScalarGridSpec(num...  12.8 us
    ppermute x1, waiting for transfers between devices, shards(): other_sent = lax.ppermute(own_sent, 'ad', PARTNERS)  12.8 us
    all_to_all x3, waiting for transfers between devices, swap(): lax.all_to_all(block, axes, split_axis=0, concat_axis=0, tiled=True, axis...  12.4 us
  transfers between devices with their start and end apart: 21, of which 11 were waited for; matrix products, arithmetic and copies ran while one was open for 10% of the time, Pallas kernels for 13%

profile of v4, /device:TPU:1, one launch (start us, length us, event | category | flops | bytes accessed | tf_op | source)
XLA Modules:
  0.0 236.6 jit_solution(771261471374515284)
XLA Ops:
  9.5 7.6 %all-to-all-start = ((bf16[16,32,320]{2,1,0:T(8,128)(2,1)}), bf16[16,32,320]{2,1,0:T(8,128)(2,1)S(1)}, u32[]{:S(2)}, u32[]{:S(2)}) async-start(bf16[16,32,320]{2,1,0:T(8,128)(2,1)} %bitcast.75), calls=%async_computation | async-start | bytes 786432 | tf_op jit(solution)/shard_map/all_to_all | solution.py:413
  21.0 5.2 %all-to-all-done = bf16[16,32,320]{2,1,0:T(8,128)(2,1)S(1)} async-done(((bf16[16,32,320]{2,1,0:T(8,128)(2,1)}), bf16[16,32,320]{2,1,0:T(8,128)(2,1)S(1)}, u32[]{:S(2)}, u32[]{:S(2)}) %all-to-all-start) | async-done | bytes 327712 | tf_op jit(solution)/shard_map/all_to_all | solution.py:413
  27.4 3.5 %all-to-all-start.1 = ((f32[16,32,128]{2,1,0:T(8,128)}), f32[16,32,128]{2,1,0:T(8,128)S(1)}, u32[]{:S(2)}, u32[]{:S(2)}) async-start(f32[16,32,128]{2,1,0:T(8,128)} %bitcast.11), calls=%async_computation.1 | async-start | bytes 524288 | tf_op jit(solution)/shard_map/all_to_all | solution.py:413
  32.1 7.1 %all-to-all-done.1 = f32[16,32,128]{2,1,0:T(8,128)S(1)} async-done(((f32[16,32,128]{2,1,0:T(8,128)}), f32[16,32,128]{2,1,0:T(8,128)S(1)}, u32[]{:S(2)}, u32[]{:S(2)}) %all-to-all-start.1) | async-done | bytes 262176 | tf_op jit(solution)/shard_map/all_to_all | solution.py:413
  39.6 2.4 %collective-permute-start.1 = (bf16[32,128]{1,0:T(8,128)(2,1)S(1)}, bf16[32,128]{1,0:T(8,128)(2,1)S(1)}, u32[]{:S(2)}, u32[]{:S(2)}) collective-permute-start(bf16[32,128]{1,0:T(8,128)(2,1)S(1)} %reduce_sum.81), channel_id=1, source_target_pairs={{0,2},{1,3},{2,0},{3,1},{4,6},{5,7},{6,4},{7,5},{8,10},{9,11},{10,... | collective-permute-start | bytes 24584 | tf_op jit(solution)/shard_map/ppermute | solution.py:467
  42.0 1.6 collective-permute-done.1
  43.6 2.1 collective-permute-done
  47.5 4.6 %copy.52 = bf16[4,8,256,256]{3,2,0,1:T(8,128)(2,1)} copy(bf16[4,8,256,256]{3,2,1,0:T(8,128)(2,1)} %param.14) | data formatting | bytes 8388608 | tf_op args[1]
  56.7 2.9 %collective-permute-start.15 = (bf16[2,272,256]{2,1,0:T(8,128)(2,1)}, bf16[2,272,256]{2,1,0:T(8,128)(2,1)S(1)}, u32[]{:S(2)}, u32[]{:S(2)}) collective-permute-start(bf16[2,272,256]{2,1,0:T(8,128)(2,1)} %get-tuple-element.22), channel_id=1, source_target_pairs={{0,96},{16,112},{32,64},{48,80},{64,32},{80,48},{96,0},{112,16},{1... | collective-permute-start | bytes 835592 | tf_op jit(solution)/shard_map/ppermute | solution.py:408
  59.6 5.0 %all-to-all-start.2 = ((bf16[8,4,256,256]{3,2,1,0:T(8,128)(2,1)}), bf16[8,4,256,256]{3,2,1,0:T(8,128)(2,1)}, u32[]{:S(2)}, u32[]{:S(2)}) async-start(bf16[8,4,256,256]{3,2,1,0:T(8,128)(2,1)} %bitcast.76), calls=%async_computation.2 | async-start | bytes 8388608 | tf_op jit(solution)/shard_map/all_to_all | solution.py:413
  64.7 15.8 %collective-permute-done.6 = bf16[64,5120]{1,0:T(8,128)(2,1)S(1)} collective-permute-done((bf16[64,5120]{1,0:T(8,128)(2,1)S(1)}, bf16[64,5120]{1,0:T(8,128)(2,1)S(1)}, u32[]{:S(2)}, u32[]{:S(2)}) %collective-permute-start.6) | collective-permute-done | bytes 655392 | tf_op jit(solution)/shard_map/ppermute | solution.py:480
  80.5 12.8 %project.1 = bf16[8,64,640]{2,1,0:T(8,128)(2,1)} custom-call(s32[8]{0:T(128)} %copy-done.7, s32[16]{0:T(128)} %fusion.27.spot_ref, bf16[512,5120]{1,0:T(8,128)(2,1)} %all-gather.3.cloned.1.call-done.tokens_ref, bf16[5120,512]{1,0:T(8,128)(2,1)} %query_ref.1, bf16[128,5120]{1,0:T(8,128)(2,1)} %bitcast.94, bf16[16,32,128]{2,1,0:T(8,128)(2,1)} %bitcast.84, ...), custom_call_target="tpu_custom_call" | custom-call | flops 33554432000 | bytes 13000000 | tf_op jit(solution)/shard_map/project/pallas_call | solution.py:125
  94.6 2.1 collective-permute-start.7
  97.2 2.9 %collective-permute-start.14 = (bf16[2,272,256]{2,1,0:T(8,128)(2,1)S(1)}, bf16[2,272,256]{2,1,0:T(8,128)(2,1)S(1)}, u32[]{:S(2)}, u32[]{:S(2)}) collective-permute-start(bf16[2,272,256]{2,1,0:T(8,128)(2,1)S(1)} %copy-done.5), channel_id=1, source_target_pairs={{0,64},{16,80},{32,96},{48,112},{64,0},{80,16},{96,32},{112,48},{1... | collective-permute-start | bytes 835592 | tf_op jit(solution)/shard_map/ppermute | solution.py:408
  101.7 2.4 %collective-permute-start.9 = (bf16[2,64,640]{2,1,0:T(8,128)(2,1)S(1)}, bf16[2,64,640]{2,1,0:T(8,128)(2,1)}, u32[]{:S(2)}, u32[]{:S(2)}) collective-permute-start(bf16[2,64,640]{2,1,0:T(8,128)(2,1)S(1)} %get-tuple-element.27), channel_id=1, source_target_pairs={{0,64},{16,80},{32,96},{48,112},{64,0},{80,16},{96,32},{112,48},{1... | collective-permute-start | bytes 491528 | tf_op jit(solution)/shard_map/ppermute | solution.py:408
  105.1 2.0 collective-permute-done.14
  107.1 6.3 %collective-permute-done.13 = bf16[2,272,256]{2,1,0:T(8,128)(2,1)S(1)} collective-permute-done((bf16[2,272,256]{2,1,0:T(8,128)(2,1)S(1)}, bf16[2,272,256]{2,1,0:T(8,128)(2,1)S(1)}, u32[]{:S(2)}, u32[]{:S(2)}) %collective-permute-start.13) | collective-permute-done | bytes 278560 | tf_op jit(solution)/shard_map/ppermute | solution.py:408
  113.5 3.0 %collective-permute-done.9 = bf16[2,64,640]{2,1,0:T(8,128)(2,1)} collective-permute-done((bf16[2,64,640]{2,1,0:T(8,128)(2,1)S(1)}, bf16[2,64,640]{2,1,0:T(8,128)(2,1)}, u32[]{:S(2)}, u32[]{:S(2)}) %collective-permute-start.9) | collective-permute-done | bytes 163872 | tf_op jit(solution)/shard_map/ppermute | solution.py:408
  116.6 3.8 %collective-permute-done.8 = bf16[2,64,640]{2,1,0:T(8,128)(2,1)} collective-permute-done((bf16[2,64,640]{2,1,0:T(8,128)(2,1)S(1)}, bf16[2,64,640]{2,1,0:T(8,128)(2,1)}, u32[]{:S(2)}, u32[]{:S(2)}) %collective-permute-start.8) | collective-permute-done | bytes 163872 | tf_op jit(solution)/shard_map/ppermute | solution.py:408
  124.4 12.8 %collective-permute-done.11.other_ref = bf16[8,64,640]{2,1,0:T(8,128)(2,1)S(1)} collective-permute-done((bf16[8,64,640]{2,1,0:T(8,128)(2,1)S(1)}, bf16[8,64,640]{2,1,0:T(8,128)(2,1)S(1)}, u32[]{:S(2)}, u32[]{:S(2)}) %collective-permute-start.11) | collective-permute-done | bytes 655392 | tf_op jit(solution)/shard_map/ppermute | solution.py:500
  138.1 18.4 %attend.1 = bf16[8,2,32,1152]{3,2,1,0:T(8,128)(2,1)} custom-call(s32[8]{0:T(128)} %copy-done.8, s32[8]{0:T(128)} %get-tuple-element.15.local_ref, s32[8]{0:T(128)} %broadcast_xor_fusion.reach_ref, s32[2]{0:T(128)} %pad_add_fusion.place_ref, bf16[8,64,640]{2,1,0:T(8,128)(2,1)} %copy-done.3, bf16[8,64,640]{2,1,0:T(8,128)(2,1)} %copy-done.9, ...), custom_call_target="tpu_custom_call" | custom-call | flops 76504104960 | bytes 8000000 | tf_op jit(solution)/shard_map/attend/pallas_call | solution.py:282
  156.4 23.4 %all_to_all.25 = bf16[16,32,1152]{2,1,0:T(8,128)(2,1)} all-to-all(bf16[16,32,1152]{2,1,0:T(8,128)(2,1)} %bitcast.79), channel_id=1, replica_groups={{0,1,16,17,32,33,48,49,64,65,80,81,96,97,112,113},{2,3,18,19,34,35,50,5..., dimensions={0} | all-to-all | bytes 2359296 | tf_op jit(solution)/shard_map/all_to_all | solution.py:413
  179.9 8.5 %output_part.1 = bf16[256,5120]{1,0:T(8,128)(2,1)} custom-call(s32[2]{0:T(128)} %pad_add_fusion.place_ref, bf16[8,2,32,1152]{3,2,1,0:T(8,128)(2,1)} %bitcast.78, bf16[512,5120]{1,0:T(8,128)(2,1)} %own_ref.1, bf16[512,5120]{1,0:T(8,128)(2,1)} %all-gather.5.cloned.1.call-done.other_ref), custom_call_target="tpu_custom_call" | custom-call | flops 2684354560 | bytes 14000000 | tf_op jit(solution)/shard_map/output_part/pallas_call | solution.py:365
  188.3 40.3 %all_to_all.26 = bf16[8,32,5120]{2,1,0:T(8,128)(2,1)S(1)} all-to-all(bf16[8,32,5120]{2,1,0:T(8,128)(2,1)} %bitcast.77), channel_id=1, replica_groups={{0,3,4,7,8,11,12,15},{1,2,5,6,9,10,13,14},{16,19,20,23,24,27,28,31},{17..., dimensions={0} | all-to-all | bytes 5242880 | tf_op jit(solution)/shard_map/all_to_all | solution.py:413
  (100 shorter events, 26.4 us)
Async XLA Ops:
  6.5 74.0 %all-gather.3.cloned.1.call-start = ((), (), s32[]{:S(2)}) async-start(), calls=%async_computation.5 | async-start | bytes 5570560 | tf_op jit(solution)/shard_map/all_gather | solution.py:439
  7.3 10.1 %copy-start.1 = (bf16[128,16,256]{2,1,0:T(8,128)(2,1)S(1)}, bf16[128,16,256]{2,1,0:T(8,128)(2,1)}, u32[]{:S(2)}) copy-start(bf16[128,16,256]{2,1,0:T(8,128)(2,1)} %param.15) | copy-start | bytes 3145732
  9.5 16.8 %all-to-all-start = ((bf16[16,32,320]{2,1,0:T(8,128)(2,1)}), bf16[16,32,320]{2,1,0:T(8,128)(2,1)S(1)}, u32[]{:S(2)}, u32[]{:S(2)}) async-start(bf16[16,32,320]{2,1,0:T(8,128)(2,1)} %bitcast.75), calls=%async_computation | async-start | bytes 786432 | tf_op jit(solution)/shard_map/all_to_all | solution.py:413
  18.3 37.5 %collective-permute-start.12 = (bf16[4,1,272,256]{3,2,1,0:T(8,128)(2,1)}, bf16[4,1,272,256]{3,2,1,0:T(8,128)(2,1)S(1)}, u32[]{:S(2)}, u32[]{:S(2)}) collective-permute-start(bf16[4,1,272,256]{3,2,1,0:T(8,128)(2,1)} %get-tuple-element.23), channel_id=1, source_target_pairs={{0,16},{16,0},{32,48},{48,32},{64,80},{80,64},{96,112},{112,96},{1... | collective-permute-start | bytes 1671176 | tf_op jit(solution)/shard_map/ppermute | solution.py:403
  27.4 11.8 %all-to-all-start.1 = ((f32[16,32,128]{2,1,0:T(8,128)}), f32[16,32,128]{2,1,0:T(8,128)S(1)}, u32[]{:S(2)}, u32[]{:S(2)}) async-start(f32[16,32,128]{2,1,0:T(8,128)} %bitcast.11), calls=%async_computation.1 | async-start | bytes 524288 | tf_op jit(solution)/shard_map/all_to_all | solution.py:413
  39.3 2.8 %collective-permute-start.2 = (bf16[32,128]{1,0:T(8,128)(2,1)S(1)}, bf16[32,128]{1,0:T(8,128)(2,1)S(1)}, u32[]{:S(2)}, u32[]{:S(2)}) collective-permute-start(bf16[32,128]{1,0:T(8,128)(2,1)S(1)} %reduce_sum.81), channel_id=1, source_target_pairs={{0,3},{1,0},{2,1},{3,2},{4,7},{5,4},{6,5},{7,6},{8,11},{9,8},{10,9... | collective-permute-start | bytes 24584 | tf_op jit(solution)/shard_map/ppermute | solution.py:467
  39.6 4.0 %collective-permute-start.1 = (bf16[32,128]{1,0:T(8,128)(2,1)S(1)}, bf16[32,128]{1,0:T(8,128)(2,1)S(1)}, u32[]{:S(2)}, u32[]{:S(2)}) collective-permute-start(bf16[32,128]{1,0:T(8,128)(2,1)S(1)} %reduce_sum.81), channel_id=1, source_target_pairs={{0,2},{1,3},{2,0},{3,1},{4,6},{5,7},{6,4},{7,5},{8,10},{9,11},{10,... | collective-permute-start | bytes 24584 | tf_op jit(solution)/shard_map/ppermute | solution.py:467
  42.0 3.7 %collective-permute-start = (bf16[32,128]{1,0:T(8,128)(2,1)S(1)}, bf16[32,128]{1,0:T(8,128)(2,1)S(1)}, u32[]{:S(2)}, u32[]{:S(2)}) collective-permute-start(bf16[32,128]{1,0:T(8,128)(2,1)S(1)} %reduce_sum.81), channel_id=1, source_target_pairs={{0,1},{1,2},{2,3},{3,0},{4,5},{5,6},{6,7},{7,4},{8,9},{9,10},{10,1... | collective-permute-start | bytes 24584 | tf_op jit(solution)/shard_map/ppermute | solution.py:467
  45.7 6.4 %collective-permute-start.5 = (bf16[4,32,128]{2,1,0:T(8,128)(2,1)S(1)}, bf16[4,32,128]{2,1,0:T(8,128)(2,1)S(1)}, u32[]{:S(2)}, u32[]{:S(2)}) collective-permute-start(bf16[4,32,128]{2,1,0:T(8,128)(2,1)S(1)} %get-tuple-element.32), channel_id=1, source_target_pairs={{0,12},{1,13},{2,14},{3,15},{4,0},{5,1},{6,2},{7,3},{8,4},{9,5},{1... | collective-permute-start | bytes 98312 | tf_op jit(solution)/shard_map/ppermute | solution.py:470
  46.3 5.8 %collective-permute-start.4 = (bf16[4,32,128]{2,1,0:T(8,128)(2,1)S(1)}, bf16[4,32,128]{2,1,0:T(8,128)(2,1)S(1)}, u32[]{:S(2)}, u32[]{:S(2)}) collective-permute-start(bf16[4,32,128]{2,1,0:T(8,128)(2,1)S(1)} %get-tuple-element.32), channel_id=1, source_target_pairs={{0,8},{1,9},{2,10},{3,11},{4,12},{5,13},{6,14},{7,15},{8,0},{9,1},... | collective-permute-start | bytes 98312 | tf_op jit(solution)/shard_map/ppermute | solution.py:470
  46.5 5.7 %collective-permute-start.3 = (bf16[4,32,128]{2,1,0:T(8,128)(2,1)S(1)}, bf16[4,32,128]{2,1,0:T(8,128)(2,1)S(1)}, u32[]{:S(2)}, u32[]{:S(2)}) collective-permute-start(bf16[4,32,128]{2,1,0:T(8,128)(2,1)S(1)} %get-tuple-element.32), channel_id=1, source_target_pairs={{0,4},{1,5},{2,6},{3,7},{4,8},{5,9},{6,10},{7,11},{8,12},{9,13},{1... | collective-permute-start | bytes 98312 | tf_op jit(solution)/shard_map/ppermute | solution.py:470
  52.9 27.6 %collective-permute-start.6 = (bf16[64,5120]{1,0:T(8,128)(2,1)S(1)}, bf16[64,5120]{1,0:T(8,128)(2,1)S(1)}, u32[]{:S(2)}, u32[]{:S(2)}) collective-permute-start(bf16[64,5120]{1,0:T(8,128)(2,1)S(1)} %constant_dynamic-slice_fusion.2), channel_id=1, source_target_pairs={{0,1},{1,0},{2,3},{3,2},{4,5},{5,4},{6,7},{7,6},{8,9},{9,8},{10,11... | collective-permute-start | bytes 1966088 | tf_op jit(solution)/shard_map/ppermute | solution.py:480
  54.2 42.5 %copy-start.8 = (s32[8]{0:T(128)}, s32[8]{0:T(128)S(1)}, u32[]{:S(2)}) copy-start(s32[8]{0:T(128)S(1)} %get-tuple-element.16.order_ref) | copy-start | bytes 100
  56.7 47.4 %collective-permute-start.15 = (bf16[2,272,256]{2,1,0:T(8,128)(2,1)}, bf16[2,272,256]{2,1,0:T(8,128)(2,1)S(1)}, u32[]{:S(2)}, u32[]{:S(2)}) collective-permute-start(bf16[2,272,256]{2,1,0:T(8,128)(2,1)} %get-tuple-element.22), channel_id=1, source_target_pairs={{0,96},{16,112},{32,64},{48,80},{64,32},{80,48},{96,0},{112,16},{1... | collective-permute-start | bytes 835592 | tf_op jit(solution)/shard_map/ppermute | solution.py:408
  59.6 64.8 %all-to-all-start.2 = ((bf16[8,4,256,256]{3,2,1,0:T(8,128)(2,1)}), bf16[8,4,256,256]{3,2,1,0:T(8,128)(2,1)}, u32[]{:S(2)}, u32[]{:S(2)}) async-start(bf16[8,4,256,256]{3,2,1,0:T(8,128)(2,1)} %bitcast.76), calls=%async_computation.2 | async-start | bytes 8388608 | tf_op jit(solution)/shard_map/all_to_all | solution.py:413
  64.6 115.2 %all-gather.5.cloned.1.call-start = ((), (), s32[]{:S(2)}) async-start(), calls=%async_computation.6 | async-start | bytes 5898240 | tf_op jit(solution)/shard_map/all_gather | solution.py:482
  80.5 12.9 %copy-start.2 = (bf16[64,5120]{1,0:T(8,128)(2,1)}, bf16[64,5120]{1,0:T(8,128)(2,1)S(1)}, u32[]{:S(2)}) copy-start(bf16[64,5120]{1,0:T(8,128)(2,1)S(1)} %collective-permute-done.6) | copy-start | bytes 1966084
  94.6 5.9 %collective-permute-start.7 = (bf16[4,1,64,640]{3,2,1,0:T(8,128)(2,1)S(1)}, bf16[4,1,64,640]{3,2,1,0:T(8,128)(2,1)S(1)}, u32[]{:S(2)}, u32[]{:S(2)}) collective-permute-start(bf16[4,1,64,640]{3,2,1,0:T(8,128)(2,1)S(1)} %get-tuple-element.29), channel_id=1, source_target_pairs={{0,16},{16,0},{32,48},{48,32},{64,80},{80,64},{96,112},{112,96},{1... | collective-permute-start | bytes 983048 | tf_op jit(solution)/shard_map/ppermute | solution.py:403
  97.2 9.9 %collective-permute-start.14 = (bf16[2,272,256]{2,1,0:T(8,128)(2,1)S(1)}, bf16[2,272,256]{2,1,0:T(8,128)(2,1)S(1)}, u32[]{:S(2)}, u32[]{:S(2)}) collective-permute-start(bf16[2,272,256]{2,1,0:T(8,128)(2,1)S(1)} %copy-done.5), channel_id=1, source_target_pairs={{0,64},{16,80},{32,96},{48,112},{64,0},{80,16},{96,32},{112,48},{1... | collective-permute-start | bytes 835592 | tf_op jit(solution)/shard_map/ppermute | solution.py:408
  100.1 13.3 %collective-permute-start.13 = (bf16[2,272,256]{2,1,0:T(8,128)(2,1)S(1)}, bf16[2,272,256]{2,1,0:T(8,128)(2,1)S(1)}, u32[]{:S(2)}, u32[]{:S(2)}) collective-permute-start(bf16[2,272,256]{2,1,0:T(8,128)(2,1)S(1)} %copy-done.4), channel_id=1, source_target_pairs={{0,32},{16,48},{32,0},{48,16},{64,96},{80,112},{96,64},{112,80},{1... | collective-permute-start | bytes 835592 | tf_op jit(solution)/shard_map/ppermute | solution.py:408
  101.2 12.3 %collective-permute-start.10 = (bf16[2,64,640]{2,1,0:T(8,128)(2,1)}, bf16[2,64,640]{2,1,0:T(8,128)(2,1)}, u32[]{:S(2)}, u32[]{:S(2)}) collective-permute-start(bf16[2,64,640]{2,1,0:T(8,128)(2,1)} %get-tuple-element.28), channel_id=1, source_target_pairs={{0,96},{16,112},{32,64},{48,80},{64,32},{80,48},{96,0},{112,16},{1... | collective-permute-start | bytes 491528 | tf_op jit(solution)/shard_map/ppermute | solution.py:408
  101.7 14.9 %collective-permute-start.9 = (bf16[2,64,640]{2,1,0:T(8,128)(2,1)S(1)}, bf16[2,64,640]{2,1,0:T(8,128)(2,1)}, u32[]{:S(2)}, u32[]{:S(2)}) collective-permute-start(bf16[2,64,640]{2,1,0:T(8,128)(2,1)S(1)} %get-tuple-element.27), channel_id=1, source_target_pairs={{0,64},{16,80},{32,96},{48,112},{64,0},{80,16},{96,32},{112,48},{1... | collective-permute-start | bytes 491528 | tf_op jit(solution)/shard_map/ppermute | solution.py:408
  104.1 16.3 %collective-permute-start.8 = (bf16[2,64,640]{2,1,0:T(8,128)(2,1)S(1)}, bf16[2,64,640]{2,1,0:T(8,128)(2,1)}, u32[]{:S(2)}, u32[]{:S(2)}) collective-permute-start(bf16[2,64,640]{2,1,0:T(8,128)(2,1)S(1)} %get-tuple-element.26), channel_id=1, source_target_pairs={{0,32},{16,48},{32,0},{48,16},{64,96},{80,112},{96,64},{112,80},{1... | collective-permute-start | bytes 491528 | tf_op jit(solution)/shard_map/ppermute | solution.py:408
  121.6 15.6 %collective-permute-start.11 = (bf16[8,64,640]{2,1,0:T(8,128)(2,1)S(1)}, bf16[8,64,640]{2,1,0:T(8,128)(2,1)S(1)}, u32[]{:S(2)}, u32[]{:S(2)}) collective-permute-start(bf16[8,64,640]{2,1,0:T(8,128)(2,1)S(1)} %pad_maximum_fusion.1.own_ref), channel_id=1, source_target_pairs={{0,1},{1,0},{2,3},{3,2},{4,5},{5,4},{6,7},{7,6},{8,9},{9,8},{10,11... | collective-permute-start | bytes 1966088 | tf_op jit(solution)/shard_map/ppermute | solution.py:500
  (11 other events, 55.9 us)
Sparse Core Ops, SparseCore 0:
  9.5 69.2 all-gather.2
  113.6 38.9 all-gather.4

commit v5 on v4

--- a/solution.py
+++ b/solution.py
@@ -406,7 +406,7 @@
     for k in range(GROUPS // 2):
         block = lax.dynamic_index_in_dim(both, (group // 2) ^ k, 0, keepdims=False)
         arrived.append(lax.ppermute(block, "grp", across_groups(2 * k)) if k else block)
-    return jnp.concatenate(arrived, axis=0)
+    return arrived
 
 
 def swap(block, axes, groups=None):
@@ -443,7 +443,7 @@
     slot_suffix = jnp.concatenate(
         [slot_suffix, jnp.broadcast_to(slot_lengths, (GROUPS, SLOT_SAMPLES, 2 * HEAD_SIZE))], axis=1
     )
-    suffix = exchange_groups(slot_suffix, group)
+    suffix = jnp.concatenate(exchange_groups(slot_suffix, group), axis=0)
 
     owners = jnp.arange(GROUPS, dtype=jnp.int32)
     local_of_slot = lax.dynamic_index_in_dim(local_table, group, 1, keepdims=False)
@@ -497,7 +497,8 @@
         query_norm_gain.reshape(1, HEAD_SIZE) * exponent_scale,
     )
     own_sent = exchange_groups(sent, group)
-    other_sent = lax.ppermute(own_sent, "ad", PARTNERS)
+    other_sent = jnp.concatenate([lax.ppermute(part, "ad", PARTNERS) for part in own_sent], axis=0)
+    own_sent = jnp.concatenate(own_sent, axis=0)
 
     local = lax.dynamic_index_in_dim(local_table, group, 0, keepdims=False)
     rank_key = local * GROUPS + owners

time: 238 us -> 220 us (0.924)
  waiting for transfers between devices: 60.6 us -> 44.2 us
    ppermute x6, waiting for transfers between devices: 15.1 us -> 6.14 us  [exchange_groups(): lax.ppermute(block, 'grp', across_groups(2 * k))]
    ppermute x1 -> x4, waiting for transfers between devices: 12.8 us -> 7.92 us  [shards(): lax.ppermute(part, 'ad', PARTNERS)]
    unnamed x29 -> x21, local copies, waits for them, and re-layouts: 5.55 us -> 4.69 us
  transfers between devices with their start and end apart: 21 -> 24, of which waited for: 11 -> 13; matrix products, arithmetic and copies ran while one was open for 10% -> 11% of each run, Pallas kernels for 13% -> 14%
where the time goes in v5:
time: 220 us; the launch traced here: 218 us
  blocking collectives  63 us (29%)
  waiting for transfers between devices  44.2 us (20%)
  Pallas kernels  39.8 us (18%)
  starting transfers between devices  32.8 us (15%)
  other arithmetic  13.9 us (6%)
  between operations  13.6 us (6%)
  local copies, waits for them, and re-layouts  9.89 us (4%)
    all_to_all x2, blocking collectives, swap(): lax.all_to_all(block, axes, split_axis=0, concat_axis=0, tiled=True, axis...  63 us
    pallas_call x1, Pallas kernels, attend(): pl.pallas_call(attend_kernel, grid_spec=pltpu.PrefetchScalarGridSpec(num_...  18.4 us
    all_to_all x3, starting transfers between devices, swap(): lax.all_to_all(block, axes, split_axis=0, concat_axis=0, tiled=True, axis...  15.9 us
    ppermute x1, waiting for transfers between devices, shards(): weight_slice = lax.ppermute(weight_slice, 'ad', PARTNERS)  14.4 us
    pallas_call x1, Pallas kernels, project(): pl.pallas_call(project_kernel, grid_spec=pltpu.PrefetchScalarGridSpec(num...  12.9 us
    all_to_all x3, waiting for transfers between devices, swap(): lax.all_to_all(block, axes, split_axis=0, concat_axis=0, tiled=True, axis...  11 us
    pallas_call x1, Pallas kernels, output_part(): pl.pallas_call(output_kernel, grid_spec=pltpu.PrefetchScalarGridSpec(num_...  8.49 us
    ppermute x4, waiting for transfers between devices, shards(): lax.ppermute(part, 'ad', PARTNERS)  7.92 us
  transfers between devices with their start and end apart: 24, of which 13 were waited for; matrix products, arithmetic and copies ran while one was open for 11% of the time, Pallas kernels for 14%

profile of v5, /device:TPU:1, one launch (start us, length us, event | category | flops | bytes accessed | tf_op | source)
XLA Modules:
  0.0 218.4 jit_solution(15889906654570861796)
XLA Ops:
  7.3 1.4 reshape.151
  9.5 7.6 %all-to-all-start = ((bf16[16,32,320]{2,1,0:T(8,128)(2,1)}), bf16[16,32,320]{2,1,0:T(8,128)(2,1)S(1)}, u32[]{:S(2)}, u32[]{:S(2)}) async-start(bf16[16,32,320]{2,1,0:T(8,128)(2,1)} %bitcast.75), calls=%async_computation | async-start | bytes 786432 | tf_op jit(solution)/shard_map/all_to_all | solution.py:413
  22.4 3.9 %all-to-all-done = bf16[16,32,320]{2,1,0:T(8,128)(2,1)S(1)} async-done(((bf16[16,32,320]{2,1,0:T(8,128)(2,1)}), bf16[16,32,320]{2,1,0:T(8,128)(2,1)S(1)}, u32[]{:S(2)}, u32[]{:S(2)}) %all-to-all-start) | async-done | bytes 327712 | tf_op jit(solution)/shard_map/all_to_all | solution.py:413
  26.3 1.1 fusion
  27.4 3.5 %all-to-all-start.1 = ((f32[16,32,128]{2,1,0:T(8,128)}), f32[16,32,128]{2,1,0:T(8,128)S(1)}, u32[]{:S(2)}, u32[]{:S(2)}) async-start(f32[16,32,128]{2,1,0:T(8,128)} %bitcast.11), calls=%async_computation.1 | async-start | bytes 524288 | tf_op jit(solution)/shard_map/all_to_all | solution.py:413
  32.1 7.1 %all-to-all-done.1 = f32[16,32,128]{2,1,0:T(8,128)S(1)} async-done(((f32[16,32,128]{2,1,0:T(8,128)}), f32[16,32,128]{2,1,0:T(8,128)S(1)}, u32[]{:S(2)}, u32[]{:S(2)}) %all-to-all-start.1) | async-done | bytes 262176 | tf_op jit(solution)/shard_map/all_to_all | solution.py:413
  39.6 2.3 %collective-permute-start.1 = (bf16[32,128]{1,0:T(8,128)(2,1)S(1)}, bf16[32,128]{1,0:T(8,128)(2,1)S(1)}, u32[]{:S(2)}, u32[]{:S(2)}) collective-permute-start(bf16[32,128]{1,0:T(8,128)(2,1)S(1)} %reduce_sum.81), channel_id=1, source_target_pairs={{0,2},{1,3},{2,0},{3,1},{4,6},{5,7},{6,4},{7,5},{8,10},{9,11},{10,... | collective-permute-start | bytes 24584 | tf_op jit(solution)/shard_map/ppermute | solution.py:467
  43.6 2.0 collective-permute-done
  47.2 4.6 %copy.52 = bf16[4,8,256,256]{3,2,0,1:T(8,128)(2,1)} copy(bf16[4,8,256,256]{3,2,1,0:T(8,128)(2,1)} %param.14) | data formatting | bytes 8388608 | tf_op args[1]
  53.5 1.2 fusion.7
  54.8 3.0 %collective-permute-start.18 = (bf16[2,272,256]{2,1,0:T(8,128)(2,1)S(1)}, bf16[2,272,256]{2,1,0:T(8,128)(2,1)S(1)}, u32[]{:S(2)}, u32[]{:S(2)}) collective-permute-start(bf16[2,272,256]{2,1,0:T(8,128)(2,1)S(1)} %get-tuple-element.22), channel_id=1, source_target_pairs={{0,96},{16,112},{32,64},{48,80},{64,32},{80,48},{96,0},{112,16},{1... | collective-permute-start | bytes 835592 | tf_op jit(solution)/shard_map/ppermute | solution.py:408
  59.7 4.8 %all-to-all-start.2 = ((bf16[8,4,256,256]{3,2,1,0:T(8,128)(2,1)}), bf16[8,4,256,256]{3,2,1,0:T(8,128)(2,1)}, u32[]{:S(2)}, u32[]{:S(2)}) async-start(bf16[8,4,256,256]{3,2,1,0:T(8,128)(2,1)} %bitcast.76), calls=%async_computation.2 | async-start | bytes 8388608 | tf_op jit(solution)/shard_map/all_to_all | solution.py:413
  66.0 14.4 %collective-permute-done.6 = bf16[64,5120]{1,0:T(8,128)(2,1)S(1)} collective-permute-done((bf16[64,5120]{1,0:T(8,128)(2,1)S(1)}, bf16[64,5120]{1,0:T(8,128)(2,1)S(1)}, u32[]{:S(2)}, u32[]{:S(2)}) %collective-permute-start.6) | collective-permute-done | bytes 655392 | tf_op jit(solution)/shard_map/ppermute | solution.py:480
  80.4 12.9 %project.1 = bf16[8,64,640]{2,1,0:T(8,128)(2,1)} custom-call(s32[8]{0:T(128)} %copy-done.4, s32[16]{0:T(128)} %fusion.27.spot_ref, bf16[512,5120]{1,0:T(8,128)(2,1)} %all-gather.3.cloned.1.call-done.tokens_ref, bf16[5120,512]{1,0:T(8,128)(2,1)} %query_ref.1, bf16[128,5120]{1,0:T(8,128)(2,1)} %bitcast.94, bf16[16,32,128]{2,1,0:T(8,128)(2,1)} %bitcast.84, ...), custom_call_target="tpu_custom_call" | custom-call | flops 33554432000 | bytes 13000000 | tf_op jit(solution)/shard_map/project/pallas_call | solution.py:125
  94.5 2.1 collective-permute-start.7
  97.9 2.7 %collective-permute-start.10 = (bf16[2,64,640]{2,1,0:T(8,128)(2,1)S(1)}, bf16[2,64,640]{2,1,0:T(8,128)(2,1)S(1)}, u32[]{:S(2)}, u32[]{:S(2)}) collective-permute-start(bf16[2,64,640]{2,1,0:T(8,128)(2,1)S(1)} %get-tuple-element.28), channel_id=1, source_target_pairs={{0,96},{16,112},{32,64},{48,80},{64,32},{80,48},{96,0},{112,16},{1... | collective-permute-start | bytes 491528 | tf_op jit(solution)/shard_map/ppermute | solution.py:408
  102.9 4.9 %collective-permute-done.10 = bf16[2,64,640]{2,1,0:T(8,128)(2,1)S(1)} collective-permute-done((bf16[2,64,640]{2,1,0:T(8,128)(2,1)S(1)}, bf16[2,64,640]{2,1,0:T(8,128)(2,1)S(1)}, u32[]{:S(2)}, u32[]{:S(2)}) %collective-permute-start.10) | collective-permute-done | bytes 163872 | tf_op jit(solution)/shard_map/ppermute | solution.py:408
  112.5 3.5 %collective-permute-done.13 = bf16[2,64,640]{2,1,0:T(8,128)(2,1)S(1)} collective-permute-done((bf16[2,64,640]{2,1,0:T(8,128)(2,1)S(1)}, bf16[2,64,640]{2,1,0:T(8,128)(2,1)S(1)}, u32[]{:S(2)}, u32[]{:S(2)}) %collective-permute-start.13) | collective-permute-done | bytes 163872 | tf_op jit(solution)/shard_map/ppermute | solution.py:500
  116.0 3.5 %collective-permute-done.12 = bf16[2,64,640]{2,1,0:T(8,128)(2,1)S(1)} collective-permute-done((bf16[2,64,640]{2,1,0:T(8,128)(2,1)S(1)}, bf16[2,64,640]{2,1,0:T(8,128)(2,1)S(1)}, u32[]{:S(2)}, u32[]{:S(2)}) %collective-permute-start.12) | collective-permute-done | bytes 163872 | tf_op jit(solution)/shard_map/ppermute | solution.py:500
  120.5 18.4 %attend.1 = bf16[8,2,32,1152]{3,2,1,0:T(8,128)(2,1)} custom-call(s32[8]{0:T(128)} %copy-done.5, s32[8]{0:T(128)} %get-tuple-element.15.local_ref, s32[8]{0:T(128)} %broadcast_xor_fusion.reach_ref, s32[2]{0:T(128)} %pad_add_fusion.place_ref, bf16[8,64,640]{2,1,0:T(8,128)(2,1)} %pad_maximum_fusion.1.own_ref, bf16[8,64,640]{2,1,0:T(8,128)(2,1)} %pad_maximum_fusion.2.other_ref, ...), custom_call_target="tpu_custom_call" | custom-call | flops 76504104960 | bytes 8000000 | tf_op jit(solution)/shard_map/attend/pallas_call | solution.py:282
  138.9 24.8 %all_to_all.25 = bf16[16,32,1152]{2,1,0:T(8,128)(2,1)} all-to-all(bf16[16,32,1152]{2,1,0:T(8,128)(2,1)} %bitcast.79), channel_id=1, replica_groups={{0,1,16,17,32,33,48,49,64,65,80,81,96,97,112,113},{2,3,18,19,34,35,50,5..., dimensions={0} | all-to-all | bytes 2359296 | tf_op jit(solution)/shard_map/all_to_all | solution.py:413
  163.6 8.5 %output_part.1 = bf16[256,5120]{1,0:T(8,128)(2,1)} custom-call(s32[2]{0:T(128)} %pad_add_fusion.place_ref, bf16[8,2,32,1152]{3,2,1,0:T(8,128)(2,1)} %bitcast.78, bf16[512,5120]{1,0:T(8,128)(2,1)} %own_ref.1, bf16[512,5120]{1,0:T(8,128)(2,1)} %all-gather.5.cloned.1.call-done.other_ref), custom_call_target="tpu_custom_call" | custom-call | flops 2684354560 | bytes 14000000 | tf_op jit(solution)/shard_map/output_part/pallas_call | solution.py:365
  172.1 38.2 %all_to_all.26 = bf16[8,32,5120]{2,1,0:T(8,128)(2,1)S(1)} all-to-all(bf16[8,32,5120]{2,1,0:T(8,128)(2,1)} %bitcast.77), channel_id=1, replica_groups={{0,3,4,7,8,11,12,15},{1,2,5,6,9,10,13,14},{16,19,20,23,24,27,28,31},{17..., dimensions={0} | all-to-all | bytes 5242880 | tf_op jit(solution)/shard_map/all_to_all | solution.py:413
  210.3 1.2 reduce_sum.82
  (99 shorter events, 26.9 us)
Async XLA Ops:
  6.5 73.9 %all-gather.3.cloned.1.call-start = ((), (), s32[]{:S(2)}) async-start(), calls=%async_computation.5 | async-start | bytes 5570560 | tf_op jit(solution)/shard_map/all_gather | solution.py:439
  9.5 16.8 %all-to-all-start = ((bf16[16,32,320]{2,1,0:T(8,128)(2,1)}), bf16[16,32,320]{2,1,0:T(8,128)(2,1)S(1)}, u32[]{:S(2)}, u32[]{:S(2)}) async-start(bf16[16,32,320]{2,1,0:T(8,128)(2,1)} %bitcast.75), calls=%async_computation | async-start | bytes 786432 | tf_op jit(solution)/shard_map/all_to_all | solution.py:413
  18.3 35.3 %collective-permute-start.15 = (bf16[4,1,272,256]{3,2,1,0:T(8,128)(2,1)}, bf16[4,1,272,256]{3,2,1,0:T(8,128)(2,1)}, u32[]{:S(2)}, u32[]{:S(2)}) collective-permute-start(bf16[4,1,272,256]{3,2,1,0:T(8,128)(2,1)} %get-tuple-element.23), channel_id=1, source_target_pairs={{0,16},{16,0},{32,48},{48,32},{64,80},{80,64},{96,112},{112,96},{1... | collective-permute-start | bytes 1671176 | tf_op jit(solution)/shard_map/ppermute | solution.py:403
  27.4 11.8 %all-to-all-start.1 = ((f32[16,32,128]{2,1,0:T(8,128)}), f32[16,32,128]{2,1,0:T(8,128)S(1)}, u32[]{:S(2)}, u32[]{:S(2)}) async-start(f32[16,32,128]{2,1,0:T(8,128)} %bitcast.11), calls=%async_computation.1 | async-start | bytes 524288 | tf_op jit(solution)/shard_map/all_to_all | solution.py:413
  39.3 3.7 %collective-permute-start.2 = (bf16[32,128]{1,0:T(8,128)(2,1)S(1)}, bf16[32,128]{1,0:T(8,128)(2,1)S(1)}, u32[]{:S(2)}, u32[]{:S(2)}) collective-permute-start(bf16[32,128]{1,0:T(8,128)(2,1)S(1)} %reduce_sum.81), channel_id=1, source_target_pairs={{0,3},{1,0},{2,1},{3,2},{4,7},{5,4},{6,5},{7,6},{8,11},{9,8},{10,9... | collective-permute-start | bytes 24584 | tf_op jit(solution)/shard_map/ppermute | solution.py:467
  39.6 4.0 %collective-permute-start.1 = (bf16[32,128]{1,0:T(8,128)(2,1)S(1)}, bf16[32,128]{1,0:T(8,128)(2,1)S(1)}, u32[]{:S(2)}, u32[]{:S(2)}) collective-permute-start(bf16[32,128]{1,0:T(8,128)(2,1)S(1)} %reduce_sum.81), channel_id=1, source_target_pairs={{0,2},{1,3},{2,0},{3,1},{4,6},{5,7},{6,4},{7,5},{8,10},{9,11},{10,... | collective-permute-start | bytes 24584 | tf_op jit(solution)/shard_map/ppermute | solution.py:467
  41.9 3.7 %collective-permute-start = (bf16[32,128]{1,0:T(8,128)(2,1)S(1)}, bf16[32,128]{1,0:T(8,128)(2,1)S(1)}, u32[]{:S(2)}, u32[]{:S(2)}) collective-permute-start(bf16[32,128]{1,0:T(8,128)(2,1)S(1)} %reduce_sum.81), channel_id=1, source_target_pairs={{0,1},{1,2},{2,3},{3,0},{4,5},{5,6},{6,7},{7,4},{8,9},{9,10},{10,1... | collective-permute-start | bytes 24584 | tf_op jit(solution)/shard_map/ppermute | solution.py:467
  45.7 6.2 %collective-permute-start.5 = (bf16[4,32,128]{2,1,0:T(8,128)(2,1)S(1)}, bf16[4,32,128]{2,1,0:T(8,128)(2,1)S(1)}, u32[]{:S(2)}, u32[]{:S(2)}) collective-permute-start(bf16[4,32,128]{2,1,0:T(8,128)(2,1)S(1)} %get-tuple-element.32), channel_id=1, source_target_pairs={{0,12},{1,13},{2,14},{3,15},{4,0},{5,1},{6,2},{7,3},{8,4},{9,5},{1... | collective-permute-start | bytes 98312 | tf_op jit(solution)/shard_map/ppermute | solution.py:470
  46.3 5.6 %collective-permute-start.4 = (bf16[4,32,128]{2,1,0:T(8,128)(2,1)S(1)}, bf16[4,32,128]{2,1,0:T(8,128)(2,1)S(1)}, u32[]{:S(2)}, u32[]{:S(2)}) collective-permute-start(bf16[4,32,128]{2,1,0:T(8,128)(2,1)S(1)} %get-tuple-element.32), channel_id=1, source_target_pairs={{0,8},{1,9},{2,10},{3,11},{4,12},{5,13},{6,14},{7,15},{8,0},{9,1},... | collective-permute-start | bytes 98312 | tf_op jit(solution)/shard_map/ppermute | solution.py:470
  46.5 5.7 %collective-permute-start.3 = (bf16[4,32,128]{2,1,0:T(8,128)(2,1)S(1)}, bf16[4,32,128]{2,1,0:T(8,128)(2,1)S(1)}, u32[]{:S(2)}, u32[]{:S(2)}) collective-permute-start(bf16[4,32,128]{2,1,0:T(8,128)(2,1)S(1)} %get-tuple-element.32), channel_id=1, source_target_pairs={{0,4},{1,5},{2,6},{3,7},{4,8},{5,9},{6,10},{7,11},{8,12},{9,13},{1... | collective-permute-start | bytes 98312 | tf_op jit(solution)/shard_map/ppermute | solution.py:470
  52.9 27.5 %collective-permute-start.6 = (bf16[64,5120]{1,0:T(8,128)(2,1)S(1)}, bf16[64,5120]{1,0:T(8,128)(2,1)S(1)}, u32[]{:S(2)}, u32[]{:S(2)}) collective-permute-start(bf16[64,5120]{1,0:T(8,128)(2,1)S(1)} %constant_dynamic-slice_fusion.2), channel_id=1, source_target_pairs={{0,1},{1,0},{2,3},{3,2},{4,5},{5,4},{6,7},{7,6},{8,9},{9,8},{10,11... | collective-permute-start | bytes 1966088 | tf_op jit(solution)/shard_map/ppermute | solution.py:480
  54.8 9.8 %collective-permute-start.18 = (bf16[2,272,256]{2,1,0:T(8,128)(2,1)S(1)}, bf16[2,272,256]{2,1,0:T(8,128)(2,1)S(1)}, u32[]{:S(2)}, u32[]{:S(2)}) collective-permute-start(bf16[2,272,256]{2,1,0:T(8,128)(2,1)S(1)} %get-tuple-element.22), channel_id=1, source_target_pairs={{0,96},{16,112},{32,64},{48,80},{64,32},{80,48},{96,0},{112,16},{1... | collective-permute-start | bytes 835592 | tf_op jit(solution)/shard_map/ppermute | solution.py:408
  57.8 6.9 %collective-permute-start.17 = (bf16[2,272,256]{2,1,0:T(8,128)(2,1)S(1)}, bf16[2,272,256]{2,1,0:T(8,128)(2,1)S(1)}, u32[]{:S(2)}, u32[]{:S(2)}) collective-permute-start(bf16[2,272,256]{2,1,0:T(8,128)(2,1)S(1)} %get-tuple-element.21), channel_id=1, source_target_pairs={{0,64},{16,80},{32,96},{48,112},{64,0},{80,16},{96,32},{112,48},{1... | collective-permute-start | bytes 835592 | tf_op jit(solution)/shard_map/ppermute | solution.py:408
  57.9 8.0 %collective-permute-start.16 = (bf16[2,272,256]{2,1,0:T(8,128)(2,1)S(1)}, bf16[2,272,256]{2,1,0:T(8,128)(2,1)S(1)}, u32[]{:S(2)}, u32[]{:S(2)}) collective-permute-start(bf16[2,272,256]{2,1,0:T(8,128)(2,1)S(1)} %get-tuple-element.20), channel_id=1, source_target_pairs={{0,32},{16,48},{32,0},{48,16},{64,96},{80,112},{96,64},{112,80},{1... | collective-permute-start | bytes 835592 | tf_op jit(solution)/shard_map/ppermute | solution.py:408
  59.7 60.8 %all-to-all-start.2 = ((bf16[8,4,256,256]{3,2,1,0:T(8,128)(2,1)}), bf16[8,4,256,256]{3,2,1,0:T(8,128)(2,1)}, u32[]{:S(2)}, u32[]{:S(2)}) async-start(bf16[8,4,256,256]{3,2,1,0:T(8,128)(2,1)} %bitcast.76), calls=%async_computation.2 | async-start | bytes 8388608 | tf_op jit(solution)/shard_map/all_to_all | solution.py:413
  64.5 99.1 %all-gather.5.cloned.1.call-start = ((), (), s32[]{:S(2)}) async-start(), calls=%async_computation.6 | async-start | bytes 5898240 | tf_op jit(solution)/shard_map/all_gather | solution.py:482
  94.5 3.4 %collective-permute-start.7 = (bf16[4,1,64,640]{3,2,1,0:T(8,128)(2,1)S(1)}, bf16[4,1,64,640]{3,2,1,0:T(8,128)(2,1)S(1)}, u32[]{:S(2)}, u32[]{:S(2)}) collective-permute-start(bf16[4,1,64,640]{3,2,1,0:T(8,128)(2,1)S(1)} %get-tuple-element.29), channel_id=1, source_target_pairs={{0,16},{16,0},{32,48},{48,32},{64,80},{80,64},{96,112},{112,96},{1... | collective-permute-start | bytes 983048 | tf_op jit(solution)/shard_map/ppermute | solution.py:403
  97.9 9.8 %collective-permute-start.10 = (bf16[2,64,640]{2,1,0:T(8,128)(2,1)S(1)}, bf16[2,64,640]{2,1,0:T(8,128)(2,1)S(1)}, u32[]{:S(2)}, u32[]{:S(2)}) collective-permute-start(bf16[2,64,640]{2,1,0:T(8,128)(2,1)S(1)} %get-tuple-element.28), channel_id=1, source_target_pairs={{0,96},{16,112},{32,64},{48,80},{64,32},{80,48},{96,0},{112,16},{1... | collective-permute-start | bytes 491528 | tf_op jit(solution)/shard_map/ppermute | solution.py:408
  100.7 7.5 %collective-permute-start.9 = (bf16[2,64,640]{2,1,0:T(8,128)(2,1)S(1)}, bf16[2,64,640]{2,1,0:T(8,128)(2,1)S(1)}, u32[]{:S(2)}, u32[]{:S(2)}) collective-permute-start(bf16[2,64,640]{2,1,0:T(8,128)(2,1)S(1)} %get-tuple-element.27), channel_id=1, source_target_pairs={{0,64},{16,80},{32,96},{48,112},{64,0},{80,16},{96,32},{112,48},{1... | collective-permute-start | bytes 491528 | tf_op jit(solution)/shard_map/ppermute | solution.py:408
  101.1 8.2 %collective-permute-start.8 = (bf16[2,64,640]{2,1,0:T(8,128)(2,1)S(1)}, bf16[2,64,640]{2,1,0:T(8,128)(2,1)S(1)}, u32[]{:S(2)}, u32[]{:S(2)}) collective-permute-start(bf16[2,64,640]{2,1,0:T(8,128)(2,1)S(1)} %get-tuple-element.26), channel_id=1, source_target_pairs={{0,32},{16,48},{32,0},{48,16},{64,96},{80,112},{96,64},{112,80},{1... | collective-permute-start | bytes 491528 | tf_op jit(solution)/shard_map/ppermute | solution.py:408
  102.4 9.3 %collective-permute-start.11 = (bf16[2,64,640]{2,1,0:T(8,128)(2,1)S(1)}, bf16[2,64,640]{2,1,0:T(8,128)(2,1)S(1)}, u32[]{:S(2)}, u32[]{:S(2)}) collective-permute-start(bf16[2,64,640]{2,1,0:T(8,128)(2,1)S(1)} %get-tuple-element.25), channel_id=1, source_target_pairs={{0,1},{1,0},{2,3},{3,2},{4,5},{5,4},{6,7},{7,6},{8,9},{9,8},{10,11... | collective-permute-start | bytes 491528 | tf_op jit(solution)/shard_map/ppermute | solution.py:500
  107.8 4.8 %collective-permute-start.14 = (bf16[2,64,640]{2,1,0:T(8,128)(2,1)S(1)}, bf16[2,64,640]{2,1,0:T(8,128)(2,1)S(1)}, u32[]{:S(2)}, u32[]{:S(2)}) collective-permute-start(bf16[2,64,640]{2,1,0:T(8,128)(2,1)S(1)} %collective-permute-done.10), channel_id=1, source_target_pairs={{0,1},{1,0},{2,3},{3,2},{4,5},{5,4},{6,7},{7,6},{8,9},{9,8},{10,11... | collective-permute-start | bytes 491528 | tf_op jit(solution)/shard_map/ppermute | solution.py:500
  108.2 7.8 %collective-permute-start.13 = (bf16[2,64,640]{2,1,0:T(8,128)(2,1)S(1)}, bf16[2,64,640]{2,1,0:T(8,128)(2,1)S(1)}, u32[]{:S(2)}, u32[]{:S(2)}) collective-permute-start(bf16[2,64,640]{2,1,0:T(8,128)(2,1)S(1)} %collective-permute-done.9), channel_id=1, source_target_pairs={{0,1},{1,0},{2,3},{3,2},{4,5},{5,4},{6,7},{7,6},{8,9},{9,8},{10,11... | collective-permute-start | bytes 491528 | tf_op jit(solution)/shard_map/ppermute | solution.py:500
  109.2 10.3 %collective-permute-start.12 = (bf16[2,64,640]{2,1,0:T(8,128)(2,1)S(1)}, bf16[2,64,640]{2,1,0:T(8,128)(2,1)S(1)}, u32[]{:S(2)}, u32[]{:S(2)}) collective-permute-start(bf16[2,64,640]{2,1,0:T(8,128)(2,1)S(1)} %collective-permute-done.8), channel_id=1, source_target_pairs={{0,1},{1,0},{2,3},{3,2},{4,5},{5,4},{6,7},{7,6},{8,9},{9,8},{10,11... | collective-permute-start | bytes 491528 | tf_op jit(solution)/shard_map/ppermute | solution.py:500
  (10 other events, 96.0 us)
Sparse Core Ops, SparseCore 0:
  9.5 69.1 all-gather.2
  96.9 37.5 all-gather.4

commit v6 on v5

--- a/solution.py
+++ b/solution.py
@@ -39,6 +39,7 @@
     [group * SHARDS + 2 * head + half for group in range(GROUPS) for half in range(2)]
     for head in range(KEY_VALUE_HEADS)
 ]
+ACROSS = [(shard, shard // 4 * 4 + 3 - shard % 4) for shard in range(SHARDS)]
 PARTNERS = [(shard, shard ^ 1) for shard in range(SHARDS)]
 
 
@@ -312,76 +313,131 @@
     )(order, local, reach, place, own, other, pages, suffix, cosine, sine, gain)
 
 
-def output_kernel(place_ref, back_ref, own_ref, other_ref, out_ref, mixed):
+def combine(place_ref, back_ref, mixed_ref):
     half = place_ref[0]
     rows = GROUPS * HALF_ROWS
-
+    slots = [
+        (place_ref[1] + index // 2) % 4 * 2 + (place_ref[2] ^ (index % 2))
+        for index in range(GROUPS)
+    ]
+
+    def part_of(source, lanes):
+        parts = [back_ref[slot, source, :, lanes] for slot in slots]
+        return jnp.concatenate(parts, axis=0).astype(jnp.float32)
+
+    def log_of(source):
+        packed = part_of(source, slice(HEAD_FAN * HEAD_SIZE, BACK_WIDTH))
+        return (
+            packed
+            + pltpu.roll(packed, HEAD_SIZE - HEAD_FAN, 1)
+            + pltpu.roll(packed, HEAD_SIZE - 2 * HEAD_FAN, 1)
+        )
+
+    first_log = log_of(0)
+    second_log = log_of(1)
+    peak = jnp.maximum(first_log, second_log)
+    first_part = jnp.exp2(first_log - peak)
+    second_part = jnp.exp2(second_log - peak)
+    both = first_part + second_part
+    first_part = first_part / both
+    second_part = second_part / both
+
+    def attended(head):
+        lanes = slice(head * HEAD_SIZE, (head + 1) * HEAD_SIZE)
+        return (
+            part_of(0, lanes) * first_part[:, head : head + 1]
+            + part_of(1, lanes) * second_part[:, head : head + 1]
+        ).astype(jnp.bfloat16)
+
+    for head in range(OWN_HEADS):
+        low = attended(head)
+        high = attended(head + OWN_HEADS)
+        lanes = slice(head * HEAD_SIZE, (head + 1) * HEAD_SIZE)
+        mixed_ref[:, lanes] = jnp.where(half == 0, low, high)
+        lanes = slice((head + OWN_HEADS) * HEAD_SIZE, (head + OWN_HEADS + 1) * HEAD_SIZE)
+        mixed_ref[:, lanes] = jnp.where(half == 0, high, low)
+
+
+def times_weights(mixed_ref, own_ref, other_ref):
+    return (
+        jnp.dot(mixed_ref[:, :OWN_WIDTH], own_ref[...], preferred_element_type=jnp.float32)
+        + jnp.dot(mixed_ref[:, OWN_WIDTH:], other_ref[...], preferred_element_type=jnp.float32)
+    ).astype(jnp.bfloat16)
+
+
+def left_kernel(place_ref, back_ref, own_ref, other_ref, mixed_ref, *out_refs):
     @pl.when(pl.program_id(0) == 0)
     def _():
-        lane = lax.broadcasted_iota(jnp.int32, (rows, HEAD_SIZE), 1)
-
-        def log_of(source):
-            packed = back_ref[:, source, :, HEAD_FAN * HEAD_SIZE :]
-            packed = packed.reshape(rows, HEAD_SIZE).astype(jnp.float32)
-            return (
-                packed
-                + pltpu.roll(packed, HEAD_SIZE - HEAD_FAN, 1)
-                + pltpu.roll(packed, HEAD_SIZE - 2 * HEAD_FAN, 1)
-            )
-
-        first_log = log_of(0)
-        second_log = log_of(1)
-        peak = jnp.maximum(first_log, second_log)
-        first_part = jnp.exp2(first_log - peak)
-        second_part = jnp.exp2(second_log - peak)
-        both = first_part + second_part
-        first_part = first_part / both
-        second_part = second_part / both
-
-        def attended(head):
-            lanes = slice(head * HEAD_SIZE, (head + 1) * HEAD_SIZE)
-            first = back_ref[:, 0, :, lanes].reshape(rows, HEAD_SIZE).astype(jnp.float32)
-            second = back_ref[:, 1, :, lanes].reshape(rows, HEAD_SIZE).astype(jnp.float32)
-            return (
-                first * first_part[:, head : head + 1] + second * second_part[:, head : head + 1]
-            ).astype(jnp.bfloat16)
-
-        for head in range(OWN_HEADS):
-            low = attended(head)
-            high = attended(head + OWN_HEADS)
-            lanes = slice(head * HEAD_SIZE, (head + 1) * HEAD_SIZE)
-            mixed[0, :, lanes] = jnp.where(half == 0, low, high)
-            mixed[1, :, lanes] = jnp.where(half == 0, high, low)
-
-    out_ref[...] = (
-        jnp.dot(mixed[0], own_ref[...], preferred_element_type=jnp.float32)
-        + jnp.dot(mixed[1], other_ref[...], preferred_element_type=jnp.float32)
-    ).astype(jnp.bfloat16)
-
-
-def output_part(place, back, own_weight, other_weight):
-    tile = 2560
+        combine(place_ref, back_ref, mixed_ref)
+
+    product = times_weights(mixed_ref, own_ref, other_ref)
+    for index, out_ref in enumerate(out_refs):
+        out_ref[...] = product[2 * index * HALF_ROWS : 2 * (index + 1) * HALF_ROWS]
+
+
+def right_kernel(mixed_ref, own_ref, other_ref, kept_ref, given_ref):
+    product = times_weights(mixed_ref, own_ref, other_ref)
+    for index in range(4):
+        rows = slice(index * HALF_ROWS, (index + 1) * HALF_ROWS)
+        start = 2 * index * HALF_ROWS
+        kept_ref[rows, :] = product[start : start + HALF_ROWS]
+        given_ref[rows, :] = product[start + HALF_ROWS : start + 2 * HALF_ROWS]
+
+
+OUT_TILE = 1280
+SIDE = MODEL_WIDTH // 2
+OUT_COST = pl.CostEstimate(
+    flops=8 * GROUPS * HALF_ROWS * SIDE * 1024, bytes_accessed=8_000_000, transcendentals=0
+)
+
+
+def left_product(place, back, own_weight, other_weight):
     rows = GROUPS * HALF_ROWS
     return pl.pallas_call(
-        output_kernel,
+        left_kernel,
         grid_spec=pltpu.PrefetchScalarGridSpec(
             num_scalar_prefetch=1,
-            grid=(MODEL_WIDTH // tile,),
+            grid=(SIDE // OUT_TILE,),
             in_specs=[
                 pl.BlockSpec((GROUPS, 2, HALF_ROWS, BACK_WIDTH), lambda n, p: (0, 0, 0, 0)),
-                pl.BlockSpec((OWN_WIDTH, tile), lambda n, p: (0, n)),
-                pl.BlockSpec((OWN_WIDTH, tile), lambda n, p: (0, n)),
+                pl.BlockSpec((OWN_WIDTH, OUT_TILE), lambda n, p: (0, n)),
+                pl.BlockSpec((OWN_WIDTH, OUT_TILE), lambda n, p: (0, n)),
             ],
-            out_specs=pl.BlockSpec((rows, tile), lambda n, p: (0, n)),
-            scratch_shapes=[pltpu.VMEM((2, rows, OWN_WIDTH), jnp.bfloat16)],
+            out_specs=[pl.BlockSpec((rows, 2 * OWN_WIDTH), lambda n, p: (0, 0))]
+            + [pl.BlockSpec((rows // 4, OUT_TILE), lambda n, p: (0, n))] * 4,
         ),
-        out_shape=jax.ShapeDtypeStruct((rows, MODEL_WIDTH), jnp.bfloat16),
+        out_shape=[jax.ShapeDtypeStruct((rows, 2 * OWN_WIDTH), jnp.bfloat16)]
+        + [jax.ShapeDtypeStruct((rows // 4, SIDE), jnp.bfloat16)] * 4,
         compiler_params=pltpu.CompilerParams(vmem_limit_bytes=60 * 2**20),
-        cost_estimate=pl.CostEstimate(
-            flops=2 * rows * MODEL_WIDTH * 1024, bytes_accessed=14_000_000, transcendentals=0
-        ),
-        name="output_part",
+        cost_estimate=OUT_COST,
+        name="left_product",
     )(place, back, own_weight, other_weight)
+
+
+def right_product(mixed, own_weight, other_weight):
+    rows = GROUPS * HALF_ROWS
+    skip = SIDE // OUT_TILE
+    return pl.pallas_call(
+        right_kernel,
+        grid=(SIDE // OUT_TILE,),
+        in_specs=[
+            pl.BlockSpec((rows, 2 * OWN_WIDTH), lambda n: (0, 0)),
+            pl.BlockSpec((OWN_WIDTH, OUT_TILE), lambda n: (0, n + skip)),
+            pl.BlockSpec((OWN_WIDTH, OUT_TILE), lambda n: (0, n + skip)),
+        ],
+        out_specs=[pl.BlockSpec((rows // 2, OUT_TILE), lambda n: (0, n))] * 2,
+        out_shape=[jax.ShapeDtypeStruct((rows // 2, SIDE), jnp.bfloat16)] * 2,
+        compiler_params=pltpu.CompilerParams(vmem_limit_bytes=60 * 2**20),
+        cost_estimate=OUT_COST,
+        name="right_product",
+    )(mixed, own_weight, other_weight)
+
+
+def total_of(parts):
+    total = parts[0].astype(jnp.float32)
+    for part in parts[1:]:
+        total = total + part.astype(jnp.float32)
+    return total
 
 
 def along_x(distance):
@@ -527,9 +583,20 @@
     back = swap(
         partial.reshape(2 * GROUPS, HALF_ROWS, BACK_WIDTH), ("grp", "ad"), HEAD_GROUPS
     ).reshape(GROUPS, 2, HALF_ROWS, BACK_WIDTH)
-    product = output_part(place, back, output_weight, other_weight)
-    blocks = swap(product.reshape(GROUPS, HALF_ROWS, MODEL_WIDTH), "ad", ROLE_GROUPS)
-    return jnp.sum(blocks.astype(jnp.float32), axis=0).astype(jnp.bfloat16)
+    place = jnp.stack([half, shard // 4, head % 2]).astype(jnp.int32)
+    mixed, *by_y = left_product(place, back, output_weight, other_weight)
+    by_y = by_y[:1] + [lax.ppermute(by_y[k], "ad", along_y(k)) for k in (1, 2, 3)]
+    kept, given = right_product(mixed, output_weight, other_weight)
+    given = lax.ppermute(given, "ad", ACROSS)
+    left = total_of(by_y)
+    left_given = lax.ppermute(left[HALF_ROWS:].astype(jnp.bfloat16), "ad", ACROSS)
+    right = total_of([kept, given]).reshape(4, HALF_ROWS, SIDE)
+    right_parts = [right[0]] + [
+        lax.ppermute(right[k].astype(jnp.bfloat16), "ad", along_y(k)) for k in (1, 2, 3)
+    ]
+    left = left[:HALF_ROWS] + left_given.astype(jnp.float32)
+    right = total_of(right_parts)
+    return jnp.concatenate([left.astype(jnp.bfloat16), right.astype(jnp.bfloat16)], axis=1)
 
 
 def solution(mesh):

time: 220 us -> 216 us (0.982)
  blocking collectives: 63 us -> 0 us
  waiting for transfers between devices: 44.2 us -> 80.6 us
  starting transfers between devices: 32.8 us -> 52.2 us
    all_to_all x2 -> x0, blocking collectives: 63 us -> none  [swap(): lax.all_to_all(block, axes, split_axis=0, concat_axis=0, tiled=True, axis...]
    ppermute x0 -> x8, waiting for transfers between devices: none -> 20.2 us  [the longest x3 10.1 us: shards(): lax.ppermute(by_y[k], 'ad', along_y(k))]
    all_to_all x3 -> x4, waiting for transfers between devices: 11 us -> 27 us  [swap(): lax.all_to_all(block, axes, split_axis=0, concat_axis=0, tiled=True, axis...]
    ppermute x0 -> x8, starting transfers between devices: none -> 12.2 us  [the longest x3 3.4 us: shards(): lax.ppermute(by_y[k], 'ad', along_y(k))]
    all_to_all x3 -> x4, starting transfers between devices: 15.9 us -> 23 us  [swap(): lax.all_to_all(block, axes, split_axis=0, concat_axis=0, tiled=True, axis...]
    pallas_call x1 -> x2, Pallas kernels: 8.49 us -> 10.6 us  [the longest x1 6.1 us: left_product(): pl.pallas_call(left_kernel, grid_spec=pltpu.PrefetchScalarGridSpec(num_sc...]
    unnamed x21 -> x27, local copies, waits for them, and re-layouts: 4.69 us -> 5.7 us
  transfers between devices with their start and end apart: 24 -> 33, of which waited for: 13 -> 20; matrix products, arithmetic and copies ran while one was open for 11% -> 12% of each run, Pallas kernels for 14% -> 17%
where the time goes in v6:
time: 216 us; the launch traced here: 215 us
  waiting for transfers between devices  80.6 us (37%)
  starting transfers between devices  52.2 us (24%)
  Pallas kernels  41.8 us (19%)
  other arithmetic  14.6 us (7%)
  between operations  13.7 us (6%)
  local copies, waits for them, and re-layouts  10.9 us (5%)
    all_to_all x4, waiting for transfers between devices, swap(): lax.all_to_all(block, axes, split_axis=0, concat_axis=0, tiled=True, axis...  27 us
    all_to_all x4, starting transfers between devices, swap(): lax.all_to_all(block, axes, split_axis=0, concat_axis=0, tiled=True, axis...  23 us
    pallas_call x1, Pallas kernels, attend(): pl.pallas_call(attend_kernel, grid_spec=pltpu.PrefetchScalarGridSpec(num_...  18.4 us
    ppermute x1, waiting for transfers between devices, shards(): weight_slice = lax.ppermute(weight_slice, 'ad', PARTNERS)  14.4 us
    pallas_call x1, Pallas kernels, project(): pl.pallas_call(project_kernel, grid_spec=pltpu.PrefetchScalarGridSpec(num...  12.9 us
    ppermute x3, waiting for transfers between devices, shards(): lax.ppermute(by_y[k], 'ad', along_y(k))  10.1 us
    ppermute x3, waiting for transfers between devices, shards(): lax.ppermute(right[k].astype(jnp.bfloat16), 'ad', along_y(k))  8.53 us
    ppermute x4, waiting for transfers between devices, shards(): lax.ppermute(part, 'ad', PARTNERS)  7.93 us
  transfers between devices with their start and end apart: 33, of which 20 were waited for; matrix products, arithmetic and copies ran while one was open for 12% of the time, Pallas kernels for 17%

profile of v6, /device:TPU:1, one launch (start us, length us, event | category | flops | bytes accessed | tf_op | source)
XLA Modules:
  0.0 214.9 jit_solution(14176585348534111112)
XLA Ops:
  9.5 7.6 %all-to-all-start = ((bf16[16,32,320]{2,1,0:T(8,128)(2,1)}), bf16[16,32,320]{2,1,0:T(8,128)(2,1)S(1)}, u32[]{:S(2)}, u32[]{:S(2)}) async-start(bf16[16,32,320]{2,1,0:T(8,128)(2,1)} %bitcast.76), calls=%async_computation | async-start | bytes 786432 | tf_op jit(solution)/shard_map/all_to_all | solution.py:469
  22.4 3.9 %all-to-all-done = bf16[16,32,320]{2,1,0:T(8,128)(2,1)S(1)} async-done(((bf16[16,32,320]{2,1,0:T(8,128)(2,1)}), bf16[16,32,320]{2,1,0:T(8,128)(2,1)S(1)}, u32[]{:S(2)}, u32[]{:S(2)}) %all-to-all-start) | async-done | bytes 327712 | tf_op jit(solution)/shard_map/all_to_all | solution.py:469
  27.4 3.5 %all-to-all-start.1 = ((f32[16,32,128]{2,1,0:T(8,128)}), f32[16,32,128]{2,1,0:T(8,128)S(1)}, u32[]{:S(2)}, u32[]{:S(2)}) async-start(f32[16,32,128]{2,1,0:T(8,128)} %bitcast.13), calls=%async_computation.1 | async-start | bytes 524288 | tf_op jit(solution)/shard_map/all_to_all | solution.py:469
  32.1 7.1 %all-to-all-done.1 = f32[16,32,128]{2,1,0:T(8,128)S(1)} async-done(((f32[16,32,128]{2,1,0:T(8,128)}), f32[16,32,128]{2,1,0:T(8,128)S(1)}, u32[]{:S(2)}, u32[]{:S(2)}) %all-to-all-start.1) | async-done | bytes 262176 | tf_op jit(solution)/shard_map/all_to_all | solution.py:469
  47.2 4.6 %copy.52 = bf16[4,8,256,256]{3,2,0,1:T(8,128)(2,1)} copy(bf16[4,8,256,256]{3,2,1,0:T(8,128)(2,1)} %param.14) | data formatting | bytes 8388608 | tf_op args[1]
  54.8 3.1 %collective-permute-start.18 = (bf16[2,272,256]{2,1,0:T(8,128)(2,1)S(1)}, bf16[2,272,256]{2,1,0:T(8,128)(2,1)S(1)}, u32[]{:S(2)}, u32[]{:S(2)}) collective-permute-start(bf16[2,272,256]{2,1,0:T(8,128)(2,1)S(1)} %get-tuple-element.38), channel_id=1, source_target_pairs={{0,96},{16,112},{32,64},{48,80},{64,32},{80,48},{96,0},{112,16},{1... | collective-permute-start | bytes 835592 | tf_op jit(solution)/shard_map/ppermute | solution.py:464
  59.7 4.7 %all-to-all-start.2 = ((bf16[8,4,256,256]{3,2,1,0:T(8,128)(2,1)}), bf16[8,4,256,256]{3,2,1,0:T(8,128)(2,1)}, u32[]{:S(2)}, u32[]{:S(2)}) async-start(bf16[8,4,256,256]{3,2,1,0:T(8,128)(2,1)} %bitcast.77), calls=%async_computation.2 | async-start | bytes 8388608 | tf_op jit(solution)/shard_map/all_to_all | solution.py:469
  66.1 14.4 %collective-permute-done.6 = bf16[64,5120]{1,0:T(8,128)(2,1)S(1)} collective-permute-done((bf16[64,5120]{1,0:T(8,128)(2,1)S(1)}, bf16[64,5120]{1,0:T(8,128)(2,1)S(1)}, u32[]{:S(2)}, u32[]{:S(2)}) %collective-permute-start.6) | collective-permute-done | bytes 655392 | tf_op jit(solution)/shard_map/ppermute | solution.py:536
  80.5 12.9 %project.1 = bf16[8,64,640]{2,1,0:T(8,128)(2,1)} custom-call(s32[8]{0:T(128)} %copy-done.7, s32[16]{0:T(128)} %fusion.31.spot_ref, bf16[512,5120]{1,0:T(8,128)(2,1)} %all-gather.3.cloned.1.call-done.tokens_ref, bf16[5120,512]{1,0:T(8,128)(2,1)} %query_ref.1, bf16[128,5120]{1,0:T(8,128)(2,1)} %bitcast.94, bf16[16,32,128]{2,1,0:T(8,128)(2,1)} %bitcast.84, ...), custom_call_target="tpu_custom_call" | custom-call | flops 33554432000 | bytes 13000000 | tf_op jit(solution)/shard_map/project/pallas_call | solution.py:126
  98.0 2.7 %collective-permute-start.10 = (bf16[2,64,640]{2,1,0:T(8,128)(2,1)S(1)}, bf16[2,64,640]{2,1,0:T(8,128)(2,1)S(1)}, u32[]{:S(2)}, u32[]{:S(2)}) collective-permute-start(bf16[2,64,640]{2,1,0:T(8,128)(2,1)S(1)} %get-tuple-element.47), channel_id=1, source_target_pairs={{0,96},{16,112},{32,64},{48,80},{64,32},{80,48},{96,0},{112,16},{1... | collective-permute-start | bytes 491528 | tf_op jit(solution)/shard_map/ppermute | solution.py:464
  102.9 4.9 %collective-permute-done.10 = bf16[2,64,640]{2,1,0:T(8,128)(2,1)S(1)} collective-permute-done((bf16[2,64,640]{2,1,0:T(8,128)(2,1)S(1)}, bf16[2,64,640]{2,1,0:T(8,128)(2,1)S(1)}, u32[]{:S(2)}, u32[]{:S(2)}) %collective-permute-start.10) | collective-permute-done | bytes 163872 | tf_op jit(solution)/shard_map/ppermute | solution.py:464
  112.6 3.5 %collective-permute-done.13 = bf16[2,64,640]{2,1,0:T(8,128)(2,1)S(1)} collective-permute-done((bf16[2,64,640]{2,1,0:T(8,128)(2,1)S(1)}, bf16[2,64,640]{2,1,0:T(8,128)(2,1)S(1)}, u32[]{:S(2)}, u32[]{:S(2)}) %collective-permute-start.13) | collective-permute-done | bytes 163872 | tf_op jit(solution)/shard_map/ppermute | solution.py:556
  116.1 3.5 %collective-permute-done.12 = bf16[2,64,640]{2,1,0:T(8,128)(2,1)S(1)} collective-permute-done((bf16[2,64,640]{2,1,0:T(8,128)(2,1)S(1)}, bf16[2,64,640]{2,1,0:T(8,128)(2,1)S(1)}, u32[]{:S(2)}, u32[]{:S(2)}) %collective-permute-start.12) | collective-permute-done | bytes 163872 | tf_op jit(solution)/shard_map/ppermute | solution.py:556
  120.5 18.4 %attend.1 = bf16[8,2,32,1152]{3,2,1,0:T(8,128)(2,1)} custom-call(s32[8]{0:T(128)} %copy-done.8, s32[8]{0:T(128)} %get-tuple-element.29.local_ref, s32[8]{0:T(128)} %broadcast_xor_fusion.reach_ref, s32[2]{0:T(128)} %pad_add_fusion.1.place_ref, bf16[8,64,640]{2,1,0:T(8,128)(2,1)} %pad_maximum_fusion.1.own_ref, ...), custom_call_target="tpu_custom_call" | custom-call | flops 76504104960 | bytes 8000000 | tf_op jit(solution)/shard_map/attend/pallas_call | solution.py:283
  138.9 7.1 %all-to-all-start.3 = ((bf16[16,32,1152]{2,1,0:T(8,128)(2,1)}), bf16[16,32,1152]{2,1,0:T(8,128)(2,1)S(1)}, u32[]{:S(2)}, u32[]{:S(2)}) async-start(bf16[16,32,1152]{2,1,0:T(8,128)(2,1)} %bitcast.79), calls=%async_computation.3 | async-start | bytes 2359296 | tf_op jit(solution)/shard_map/all_to_all | solution.py:469
  146.7 16.0 %all-to-all-done.3 = bf16[16,32,1152]{2,1,0:T(8,128)(2,1)S(1)} async-done(((bf16[16,32,1152]{2,1,0:T(8,128)(2,1)}), bf16[16,32,1152]{2,1,0:T(8,128)(2,1)S(1)}, u32[]{:S(2)}, u32[]{:S(2)}) %all-to-all-start.3) | async-done | bytes 1179680 | tf_op jit(solution)/shard_map/all_to_all | solution.py:469
  163.7 6.1 %left_product.1 = (bf16[256,1024]{1,0:T(8,128)(2,1)}, bf16[64,2560]{1,0:T(8,128)(2,1)}, bf16[64,2560]{1,0:T(8,128)(2,1)}, bf16[64,2560]{1,0:T(8,128)(2,1)}, bf16[64,2560]{1,0:T(8,128)(2,1)}) custom-call(s32[3]{0:T(128)} %pad_add_fusion.place_ref, bf16[8,2,32,1152]{3,2,1,0:T(8,128)(2,1)} %bitcast.78, bf16[512,5120]{1,0:T(8,128)(2,1)} %own_ref.3, ...), custom_call_target="tpu_custom_call" | custom-call | flops 5368709120 | bytes 8000000 | tf_op jit(solution)/shard_map/left_product/pallas_call | solution.py:396
  173.2 4.5 %right_product.1 = (bf16[128,2560]{1,0:T(8,128)(2,1)}, bf16[128,2560]{1,0:T(8,128)(2,1)}) custom-call(bf16[256,1024]{1,0:T(8,128)(2,1)} %get-tuple-element.26.mixed_ref, bf16[512,5120]{1,0:T(8,128)(2,1)} %own_ref.3, bf16[512,5120]{1,0:T(8,128)(2,1)} %all-gather.5.cloned.1.call-done.other_ref), custom_call_target="tpu_custom_call" | custom-call | flops 5368709120 | bytes 8000000 | tf_op jit(solution)/shard_map/right_product/pallas_call | solution.py:420
  177.7 2.7 %collective-permute-start.23 = (bf16[128,2560]{1,0:T(8,128)(2,1)}, bf16[128,2560]{1,0:T(8,128)(2,1)S(1)}, u32[]{:S(2)}, u32[]{:S(2)}) collective-permute-start(bf16[128,2560]{1,0:T(8,128)(2,1)} %get-tuple-element.28), channel_id=1, source_target_pairs={{0,3},{1,2},{2,1},{3,0},{4,7},{5,6},{6,5},{7,4},{8,11},{9,10},{10,... | collective-permute-start | bytes 1966088 | tf_op jit(solution)/shard_map/ppermute | solution.py:590
  180.4 6.4 %collective-permute-done.21 = bf16[64,2560]{1,0:T(8,128)(2,1)S(1)} collective-permute-done((bf16[64,2560]{1,0:T(8,128)(2,1)}, bf16[64,2560]{1,0:T(8,128)(2,1)S(1)}, u32[]{:S(2)}, u32[]{:S(2)}) %collective-permute-start.21) | collective-permute-done | bytes 327712 | tf_op jit(solution)/shard_map/ppermute | solution.py:588
  186.8 3.7 %collective-permute-done.19 = bf16[64,2560]{1,0:T(8,128)(2,1)S(1)} collective-permute-done((bf16[64,2560]{1,0:T(8,128)(2,1)}, bf16[64,2560]{1,0:T(8,128)(2,1)S(1)}, u32[]{:S(2)}, u32[]{:S(2)}) %collective-permute-start.19) | collective-permute-done | bytes 327712 | tf_op jit(solution)/shard_map/ppermute | solution.py:588
  190.7 2.8 %collective-permute-start.22 = (bf16[32,2560]{1,0:T(8,128)(2,1)S(1)}, bf16[32,2560]{1,0:T(8,128)(2,1)S(1)}, u32[]{:S(2)}, u32[]{:S(2)}) collective-permute-start(bf16[32,2560]{1,0:T(8,128)(2,1)S(1)} %slice.55), channel_id=1, source_target_pairs={{0,3},{1,2},{2,1},{3,0},{4,7},{5,6},{6,5},{7,4},{8,11},{9,10},{10,... | collective-permute-start | bytes 491528 | tf_op jit(solution)/shard_map/ppermute | solution.py:592
  198.7 3.3 %collective-permute-done.26 = bf16[32,2560]{1,0:T(8,128)(2,1)S(1)} collective-permute-done((bf16[32,2560]{1,0:T(8,128)(2,1)S(1)}, bf16[32,2560]{1,0:T(8,128)(2,1)S(1)}, u32[]{:S(2)}, u32[]{:S(2)}) %collective-permute-start.26) | collective-permute-done | bytes 163872 | tf_op jit(solution)/shard_map/ppermute | solution.py:595
  203.4 3.8 %collective-permute-done.24 = bf16[32,2560]{1,0:T(8,128)(2,1)S(1)} collective-permute-done((bf16[32,2560]{1,0:T(8,128)(2,1)S(1)}, bf16[32,2560]{1,0:T(8,128)(2,1)S(1)}, u32[]{:S(2)}, u32[]{:S(2)}) %collective-permute-start.24) | collective-permute-done | bytes 163872 | tf_op jit(solution)/shard_map/ppermute | solution.py:595
  (129 shorter events, 49.9 us)
Async XLA Ops:
  6.5 74.0 %all-gather.3.cloned.1.call-start = ((), (), s32[]{:S(2)}) async-start(), calls=%async_computation.4 | async-start | bytes 5570560 | tf_op jit(solution)/shard_map/all_gather | solution.py:495
  9.5 16.8 %all-to-all-start = ((bf16[16,32,320]{2,1,0:T(8,128)(2,1)}), bf16[16,32,320]{2,1,0:T(8,128)(2,1)S(1)}, u32[]{:S(2)}, u32[]{:S(2)}) async-start(bf16[16,32,320]{2,1,0:T(8,128)(2,1)} %bitcast.76), calls=%async_computation | async-start | bytes 786432 | tf_op jit(solution)/shard_map/all_to_all | solution.py:469
  18.2 35.3 %collective-permute-start.15 = (bf16[4,1,272,256]{3,2,1,0:T(8,128)(2,1)}, bf16[4,1,272,256]{3,2,1,0:T(8,128)(2,1)}, u32[]{:S(2)}, u32[]{:S(2)}) collective-permute-start(bf16[4,1,272,256]{3,2,1,0:T(8,128)(2,1)} %get-tuple-element.39), channel_id=1, source_target_pairs={{0,16},{16,0},{32,48},{48,32},{64,80},{80,64},{96,112},{112,96},{1... | collective-permute-start | bytes 1671176 | tf_op jit(solution)/shard_map/ppermute | solution.py:459
  27.4 11.8 %all-to-all-start.1 = ((f32[16,32,128]{2,1,0:T(8,128)}), f32[16,32,128]{2,1,0:T(8,128)S(1)}, u32[]{:S(2)}, u32[]{:S(2)}) async-start(f32[16,32,128]{2,1,0:T(8,128)} %bitcast.13), calls=%async_computation.1 | async-start | bytes 524288 | tf_op jit(solution)/shard_map/all_to_all | solution.py:469
  52.9 27.6 %collective-permute-start.6 = (bf16[64,5120]{1,0:T(8,128)(2,1)S(1)}, bf16[64,5120]{1,0:T(8,128)(2,1)S(1)}, u32[]{:S(2)}, u32[]{:S(2)}) collective-permute-start(bf16[64,5120]{1,0:T(8,128)(2,1)S(1)} %constant_dynamic-slice_fusion.2), channel_id=1, source_target_pairs={{0,1},{1,0},{2,3},{3,2},{4,5},{5,4},{6,7},{7,6},{8,9},{9,8},{10,11... | collective-permute-start | bytes 1966088 | tf_op jit(solution)/shard_map/ppermute | solution.py:536
  54.8 9.7 %collective-permute-start.18 = (bf16[2,272,256]{2,1,0:T(8,128)(2,1)S(1)}, bf16[2,272,256]{2,1,0:T(8,128)(2,1)S(1)}, u32[]{:S(2)}, u32[]{:S(2)}) collective-permute-start(bf16[2,272,256]{2,1,0:T(8,128)(2,1)S(1)} %get-tuple-element.38), channel_id=1, source_target_pairs={{0,96},{16,112},{32,64},{48,80},{64,32},{80,48},{96,0},{112,16},{1... | collective-permute-start | bytes 835592 | tf_op jit(solution)/shard_map/ppermute | solution.py:464
  57.9 7.0 %collective-permute-start.17 = (bf16[2,272,256]{2,1,0:T(8,128)(2,1)S(1)}, bf16[2,272,256]{2,1,0:T(8,128)(2,1)S(1)}, u32[]{:S(2)}, u32[]{:S(2)}) collective-permute-start(bf16[2,272,256]{2,1,0:T(8,128)(2,1)S(1)} %get-tuple-element.37), channel_id=1, source_target_pairs={{0,64},{16,80},{32,96},{48,112},{64,0},{80,16},{96,32},{112,48},{1... | collective-permute-start | bytes 835592 | tf_op jit(solution)/shard_map/ppermute | solution.py:464
  57.9 8.0 %collective-permute-start.16 = (bf16[2,272,256]{2,1,0:T(8,128)(2,1)S(1)}, bf16[2,272,256]{2,1,0:T(8,128)(2,1)S(1)}, u32[]{:S(2)}, u32[]{:S(2)}) collective-permute-start(bf16[2,272,256]{2,1,0:T(8,128)(2,1)S(1)} %get-tuple-element.36), channel_id=1, source_target_pairs={{0,32},{16,48},{32,0},{48,16},{64,96},{80,112},{96,64},{112,80},{1... | collective-permute-start | bytes 835592 | tf_op jit(solution)/shard_map/ppermute | solution.py:464
  59.7 60.8 %all-to-all-start.2 = ((bf16[8,4,256,256]{3,2,1,0:T(8,128)(2,1)}), bf16[8,4,256,256]{3,2,1,0:T(8,128)(2,1)}, u32[]{:S(2)}, u32[]{:S(2)}) async-start(bf16[8,4,256,256]{3,2,1,0:T(8,128)(2,1)} %bitcast.77), calls=%async_computation.2 | async-start | bytes 8388608 | tf_op jit(solution)/shard_map/all_to_all | solution.py:469
  64.4 98.2 %all-gather.5.cloned.1.call-start = ((), (), s32[]{:S(2)}) async-start(), calls=%async_computation.5 | async-start | bytes 5898240 | tf_op jit(solution)/shard_map/all_gather | solution.py:538
  98.0 9.8 %collective-permute-start.10 = (bf16[2,64,640]{2,1,0:T(8,128)(2,1)S(1)}, bf16[2,64,640]{2,1,0:T(8,128)(2,1)S(1)}, u32[]{:S(2)}, u32[]{:S(2)}) collective-permute-start(bf16[2,64,640]{2,1,0:T(8,128)(2,1)S(1)} %get-tuple-element.47), channel_id=1, source_target_pairs={{0,96},{16,112},{32,64},{48,80},{64,32},{80,48},{96,0},{112,16},{1... | collective-permute-start | bytes 491528 | tf_op jit(solution)/shard_map/ppermute | solution.py:464
  100.7 7.5 %collective-permute-start.9 = (bf16[2,64,640]{2,1,0:T(8,128)(2,1)S(1)}, bf16[2,64,640]{2,1,0:T(8,128)(2,1)S(1)}, u32[]{:S(2)}, u32[]{:S(2)}) collective-permute-start(bf16[2,64,640]{2,1,0:T(8,128)(2,1)S(1)} %get-tuple-element.46), channel_id=1, source_target_pairs={{0,64},{16,80},{32,96},{48,112},{64,0},{80,16},{96,32},{112,48},{1... | collective-permute-start | bytes 491528 | tf_op jit(solution)/shard_map/ppermute | solution.py:464
  101.1 8.1 %collective-permute-start.8 = (bf16[2,64,640]{2,1,0:T(8,128)(2,1)S(1)}, bf16[2,64,640]{2,1,0:T(8,128)(2,1)S(1)}, u32[]{:S(2)}, u32[]{:S(2)}) collective-permute-start(bf16[2,64,640]{2,1,0:T(8,128)(2,1)S(1)} %get-tuple-element.45), channel_id=1, source_target_pairs={{0,32},{16,48},{32,0},{48,16},{64,96},{80,112},{96,64},{112,80},{1... | collective-permute-start | bytes 491528 | tf_op jit(solution)/shard_map/ppermute | solution.py:464
  102.4 9.3 %collective-permute-start.11 = (bf16[2,64,640]{2,1,0:T(8,128)(2,1)S(1)}, bf16[2,64,640]{2,1,0:T(8,128)(2,1)S(1)}, u32[]{:S(2)}, u32[]{:S(2)}) collective-permute-start(bf16[2,64,640]{2,1,0:T(8,128)(2,1)S(1)} %get-tuple-element.44), channel_id=1, source_target_pairs={{0,1},{1,0},{2,3},{3,2},{4,5},{5,4},{6,7},{7,6},{8,9},{9,8},{10,11... | collective-permute-start | bytes 491528 | tf_op jit(solution)/shard_map/ppermute | solution.py:556
  108.2 7.8 %collective-permute-start.13 = (bf16[2,64,640]{2,1,0:T(8,128)(2,1)S(1)}, bf16[2,64,640]{2,1,0:T(8,128)(2,1)S(1)}, u32[]{:S(2)}, u32[]{:S(2)}) collective-permute-start(bf16[2,64,640]{2,1,0:T(8,128)(2,1)S(1)} %collective-permute-done.9), channel_id=1, source_target_pairs={{0,1},{1,0},{2,3},{3,2},{4,5},{5,4},{6,7},{7,6},{8,9},{9,8},{10,11... | collective-permute-start | bytes 491528 | tf_op jit(solution)/shard_map/ppermute | solution.py:556
  109.3 10.3 %collective-permute-start.12 = (bf16[2,64,640]{2,1,0:T(8,128)(2,1)S(1)}, bf16[2,64,640]{2,1,0:T(8,128)(2,1)S(1)}, u32[]{:S(2)}, u32[]{:S(2)}) collective-permute-start(bf16[2,64,640]{2,1,0:T(8,128)(2,1)S(1)} %collective-permute-done.8), channel_id=1, source_target_pairs={{0,1},{1,0},{2,3},{3,2},{4,5},{5,4},{6,7},{7,6},{8,9},{9,8},{10,11... | collective-permute-start | bytes 491528 | tf_op jit(solution)/shard_map/ppermute | solution.py:556
  138.9 23.8 %all-to-all-start.3 = ((bf16[16,32,1152]{2,1,0:T(8,128)(2,1)}), bf16[16,32,1152]{2,1,0:T(8,128)(2,1)S(1)}, u32[]{:S(2)}, u32[]{:S(2)}) async-start(bf16[16,32,1152]{2,1,0:T(8,128)(2,1)} %bitcast.79), calls=%async_computation.3 | async-start | bytes 2359296 | tf_op jit(solution)/shard_map/all_to_all | solution.py:469
  169.8 17.0 %collective-permute-start.21 = (bf16[64,2560]{1,0:T(8,128)(2,1)}, bf16[64,2560]{1,0:T(8,128)(2,1)S(1)}, u32[]{:S(2)}, u32[]{:S(2)}) collective-permute-start(bf16[64,2560]{1,0:T(8,128)(2,1)} %get-tuple-element.25), channel_id=1, source_target_pairs={{0,12},{1,13},{2,14},{3,15},{4,0},{5,1},{6,2},{7,3},{8,4},{9,5},{1... | collective-permute-start | bytes 983048 | tf_op jit(solution)/shard_map/ppermute | solution.py:588
  172.1 14.7 %collective-permute-start.20 = (bf16[64,2560]{1,0:T(8,128)(2,1)}, bf16[64,2560]{1,0:T(8,128)(2,1)S(1)}, u32[]{:S(2)}, u32[]{:S(2)}) collective-permute-start(bf16[64,2560]{1,0:T(8,128)(2,1)} %get-tuple-element.24), channel_id=1, source_target_pairs={{0,8},{1,9},{2,10},{3,11},{4,12},{5,13},{6,14},{7,15},{8,0},{9,1},... | collective-permute-start | bytes 983048 | tf_op jit(solution)/shard_map/ppermute | solution.py:588
  172.6 17.9 %collective-permute-start.19 = (bf16[64,2560]{1,0:T(8,128)(2,1)}, bf16[64,2560]{1,0:T(8,128)(2,1)S(1)}, u32[]{:S(2)}, u32[]{:S(2)}) collective-permute-start(bf16[64,2560]{1,0:T(8,128)(2,1)} %get-tuple-element.23), channel_id=1, source_target_pairs={{0,4},{1,5},{2,6},{3,7},{4,8},{5,9},{6,10},{7,11},{8,12},{9,13},{1... | collective-permute-start | bytes 983048 | tf_op jit(solution)/shard_map/ppermute | solution.py:588
  177.7 17.4 %collective-permute-start.23 = (bf16[128,2560]{1,0:T(8,128)(2,1)}, bf16[128,2560]{1,0:T(8,128)(2,1)S(1)}, u32[]{:S(2)}, u32[]{:S(2)}) collective-permute-start(bf16[128,2560]{1,0:T(8,128)(2,1)} %get-tuple-element.28), channel_id=1, source_target_pairs={{0,3},{1,2},{2,1},{3,0},{4,7},{5,6},{6,5},{7,4},{8,11},{9,10},{10,... | collective-permute-start | bytes 1966088 | tf_op jit(solution)/shard_map/ppermute | solution.py:590
  190.7 8.0 %collective-permute-start.22 = (bf16[32,2560]{1,0:T(8,128)(2,1)S(1)}, bf16[32,2560]{1,0:T(8,128)(2,1)S(1)}, u32[]{:S(2)}, u32[]{:S(2)}) collective-permute-start(bf16[32,2560]{1,0:T(8,128)(2,1)S(1)} %slice.55), channel_id=1, source_target_pairs={{0,3},{1,2},{2,1},{3,0},{4,7},{5,6},{6,5},{7,4},{8,11},{9,10},{10,... | collective-permute-start | bytes 491528 | tf_op jit(solution)/shard_map/ppermute | solution.py:592
  195.3 6.7 %collective-permute-start.26 = (bf16[32,2560]{1,0:T(8,128)(2,1)S(1)}, bf16[32,2560]{1,0:T(8,128)(2,1)S(1)}, u32[]{:S(2)}, u32[]{:S(2)}) collective-permute-start(bf16[32,2560]{1,0:T(8,128)(2,1)S(1)} %get-tuple-element.42), channel_id=1, source_target_pairs={{0,12},{1,13},{2,14},{3,15},{4,0},{5,1},{6,2},{7,3},{8,4},{9,5},{1... | collective-permute-start | bytes 491528 | tf_op jit(solution)/shard_map/ppermute | solution.py:595
  198.7 8.6 %collective-permute-start.24 = (bf16[32,2560]{1,0:T(8,128)(2,1)S(1)}, bf16[32,2560]{1,0:T(8,128)(2,1)S(1)}, u32[]{:S(2)}, u32[]{:S(2)}) collective-permute-start(bf16[32,2560]{1,0:T(8,128)(2,1)S(1)} %get-tuple-element.41), channel_id=1, source_target_pairs={{0,4},{1,5},{2,6},{3,7},{4,8},{5,9},{6,10},{7,11},{8,12},{9,13},{1... | collective-permute-start | bytes 491528 | tf_op jit(solution)/shard_map/ppermute | solution.py:595
  (22 other events, 161.4 us)
Sparse Core Ops, SparseCore 0:
  9.5 69.3 all-gather.2
  97.0 37.5 all-gather.4

commit v7 on v6

--- a/solution.py
+++ b/solution.py
@@ -23,6 +23,8 @@
 HALF_ROWS = SLOT_ROWS // 2
 ROWS = GROUPS * SLOT_ROWS
 OWN_HEADS = 4
+PIECES = 4
+PIECE = MODEL_WIDTH // PIECES
 OWN_WIDTH = OWN_HEADS * HEAD_SIZE
 HEAD_FAN = 2 * OWN_HEADS
 SENT_WIDTH = OWN_WIDTH + HEAD_SIZE
@@ -87,51 +89,67 @@
     sin_ref,
     gain_ref,
     out_ref,
+    tokens,
+    query_weight,
+    keyval_weight,
     query_sum,
     keyval_sum,
+    sems,
 ):
-    step = pl.program_id(0)
-
-    @pl.when(step == 0)
-    def _():
-        query_sum[...] = jnp.zeros_like(query_sum)
-        keyval_sum[...] = jnp.zeros_like(keyval_sum)
-
-    part = tokens_ref[...]
-    query_sum[...] += jnp.dot(part, query_ref[...], preferred_element_type=jnp.float32)
-    keyval_sum[...] += dot_nt(part, keyval_ref[...])
-
-    @pl.when(step == pl.num_programs(0) - 1)
-    def _():
-        for slot in range(GROUPS):
-            rows = slice(slot * SLOT_ROWS, (slot + 1) * SLOT_ROWS)
-            low_rank = jnp.concatenate(
-                [rank_ref[spot_ref[2 * slot]], rank_ref[spot_ref[2 * slot + 1]]], axis=0
-            )
-            query = query_sum[rows, :] + jnp.dot(
-                low_rank, up_ref[task_ref[slot]], preferred_element_type=jnp.float32
-            )
-            for head in range(OWN_HEADS):
-                lanes = slice(head * HEAD_SIZE, (head + 1) * HEAD_SIZE)
-                turned = norm_rotate(
-                    query[:, lanes], gain_ref[...], cos_ref[rows, :], sin_ref[rows, :]
-                ).astype(jnp.bfloat16)
-                out_ref[slot, :, lanes] = turned
-            out_ref[slot, :, OWN_WIDTH:] = keyval_sum[rows, :].astype(jnp.bfloat16)
+    copies = []
+    for piece in range(PIECES):
+        span = pl.ds(piece * PIECE, PIECE)
+        copies.append(
+            [
+                pltpu.make_async_copy(
+                    tokens_ref.at[:, span], tokens.at[:, span], sems.at[0, piece]
+                ),
+                pltpu.make_async_copy(
+                    query_ref.at[span, :], query_weight.at[span, :], sems.at[1, piece]
+                ),
+                pltpu.make_async_copy(
+                    keyval_ref.at[:, span], keyval_weight.at[:, span], sems.at[2, piece]
+                ),
+            ]
+        )
+        for copy in copies[-1]:
+            copy.start()
+    for piece in range(PIECES):
+        for copy in copies[piece]:
+            copy.wait()
+        span = slice(piece * PIECE, (piece + 1) * PIECE)
+        part = tokens[:, span]
+        query = jnp.dot(part, query_weight[span, :], preferred_element_type=jnp.float32)
+        keyval = dot_nt(part, keyval_weight[:, span])
+        query_sum[...] = query if piece == 0 else query_sum[...] + query
+        keyval_sum[...] = keyval if piece == 0 else keyval_sum[...] + keyval
+
+    for slot in range(GROUPS):
+        rows = slice(slot * SLOT_ROWS, (slot + 1) * SLOT_ROWS)
+        low_rank = jnp.concatenate(
+            [rank_ref[spot_ref[2 * slot]], rank_ref[spot_ref[2 * slot + 1]]], axis=0
+        )
+        query = query_sum[rows, :] + jnp.dot(
+            low_rank, up_ref[task_ref[slot]], preferred_element_type=jnp.float32
+        )
+        for head in range(OWN_HEADS):
+            lanes = slice(head * HEAD_SIZE, (head + 1) * HEAD_SIZE)
+            turned = norm_rotate(
+                query[:, lanes], gain_ref[...], cos_ref[rows, :], sin_ref[rows, :]
+            ).astype(jnp.bfloat16)
+            out_ref[slot, :, lanes] = turned
+        out_ref[slot, :, OWN_WIDTH:] = keyval_sum[rows, :].astype(jnp.bfloat16)
 
 
 def project(tasks, spots, tokens, query_weight, keyval_weight, low_rank, up_maps, cosine, sine, gain):
-    tile = 2560
     whole = lambda *shape: pl.BlockSpec(shape, lambda k, t, s: (0,) * len(shape))
     return pl.pallas_call(
         project_kernel,
         grid_spec=pltpu.PrefetchScalarGridSpec(
             num_scalar_prefetch=2,
-            grid=(MODEL_WIDTH // tile,),
-            in_specs=[
-                pl.BlockSpec((ROWS, tile), lambda k, t, s: (0, k)),
-                pl.BlockSpec((tile, OWN_WIDTH), lambda k, t, s: (k, 0)),
-                pl.BlockSpec((HEAD_SIZE, tile), lambda k, t, s: (0, k)),
+            grid=(1,),
+            in_specs=[pl.BlockSpec(memory_space=pl.ANY)] * 3
+            + [
                 whole(SHARDS, HALF_ROWS, ADAPTER_RANK),
                 whole(ADAPTER_COUNT, ADAPTER_RANK, OWN_WIDTH),
                 whole(ROWS, HEAD_SIZE),
@@ -140,8 +158,12 @@
             ],
             out_specs=whole(GROUPS, SLOT_ROWS, SENT_WIDTH),
             scratch_shapes=[
+                pltpu.VMEM((ROWS, MODEL_WIDTH), jnp.bfloat16),
+                pltpu.VMEM((MODEL_WIDTH, OWN_WIDTH), jnp.bfloat16),
+                pltpu.VMEM((HEAD_SIZE, MODEL_WIDTH), jnp.bfloat16),
                 pltpu.VMEM((ROWS, OWN_WIDTH), jnp.float32),
                 pltpu.VMEM((ROWS, HEAD_SIZE), jnp.float32),
+                pltpu.SemaphoreType.DMA((3, PIECES)),
             ],
         ),
         out_shape=jax.ShapeDtypeStruct((GROUPS, SLOT_ROWS, SENT_WIDTH), jnp.bfloat16),
@@ -384,10 +406,11 @@
         given_ref[rows, :] = product[start + HALF_ROWS : start + 2 * HALF_ROWS]
 
 
-OUT_TILE = 1280
-SIDE = MODEL_WIDTH // 2
+OUT_TILE = 1024
+LEFT = 3 * OUT_TILE
+RIGHT = MODEL_WIDTH - LEFT
 OUT_COST = pl.CostEstimate(
-    flops=8 * GROUPS * HALF_ROWS * SIDE * 1024, bytes_accessed=8_000_000, transcendentals=0
+    flops=4 * GROUPS * HALF_ROWS * MODEL_WIDTH * 1024, bytes_accessed=8_000_000, transcendentals=0
 )
 
 
@@ -397,7 +420,7 @@
         left_kernel,
         grid_spec=pltpu.PrefetchScalarGridSpec(
             num_scalar_prefetch=1,
-            grid=(SIDE // OUT_TILE,),
+            grid=(LEFT // OUT_TILE,),
             in_specs=[
                 pl.BlockSpec((GROUPS, 2, HALF_ROWS, BACK_WIDTH), lambda n, p: (0, 0, 0, 0)),
                 pl.BlockSpec((OWN_WIDTH, OUT_TILE), lambda n, p: (0, n)),
@@ -407,7 +430,7 @@
             + [pl.BlockSpec((rows // 4, OUT_TILE), lambda n, p: (0, n))] * 4,
         ),
         out_shape=[jax.ShapeDtypeStruct((rows, 2 * OWN_WIDTH), jnp.bfloat16)]
-        + [jax.ShapeDtypeStruct((rows // 4, SIDE), jnp.bfloat16)] * 4,
+        + [jax.ShapeDtypeStruct((rows // 4, LEFT), jnp.bfloat16)] * 4,
         compiler_params=pltpu.CompilerParams(vmem_limit_bytes=60 * 2**20),
         cost_estimate=OUT_COST,
         name="left_product",
@@ -416,17 +439,17 @@
 
 def right_product(mixed, own_weight, other_weight):
     rows = GROUPS * HALF_ROWS
-    skip = SIDE // OUT_TILE
+    skip = LEFT // OUT_TILE
     return pl.pallas_call(
         right_kernel,
-        grid=(SIDE // OUT_TILE,),
+        grid=(RIGHT // OUT_TILE,),
         in_specs=[
             pl.BlockSpec((rows, 2 * OWN_WIDTH), lambda n: (0, 0)),
             pl.BlockSpec((OWN_WIDTH, OUT_TILE), lambda n: (0, n + skip)),
             pl.BlockSpec((OWN_WIDTH, OUT_TILE), lambda n: (0, n + skip)),
         ],
         out_specs=[pl.BlockSpec((rows // 2, OUT_TILE), lambda n: (0, n))] * 2,
-        out_shape=[jax.ShapeDtypeStruct((rows // 2, SIDE), jnp.bfloat16)] * 2,
+        out_shape=[jax.ShapeDtypeStruct((rows // 2, RIGHT), jnp.bfloat16)] * 2,
         compiler_params=pltpu.CompilerParams(vmem_limit_bytes=60 * 2**20),
         cost_estimate=OUT_COST,
         name="right_product",
@@ -590,7 +613,7 @@
     given = lax.ppermute(given, "ad", ACROSS)
     left = total_of(by_y)
     left_given = lax.ppermute(left[HALF_ROWS:].astype(jnp.bfloat16), "ad", ACROSS)
-    right = total_of([kept, given]).reshape(4, HALF_ROWS, SIDE)
+    right = total_of([kept, given]).reshape(4, HALF_ROWS, RIGHT)
     right_parts = [right[0]] + [
         lax.ppermute(right[k].astype(jnp.bfloat16), "ad", along_y(k)) for k in (1, 2, 3)
     ]

time: 216 us -> 215 us (level)
    ppermute x3, waiting for transfers between devices: 8.53 us -> 5.02 us  [shards(): lax.ppermute(right[k].astype(jnp.bfloat16), 'ad', along_y(k))]
    ppermute x3, waiting for transfers between devices: 10.1 us -> 13.1 us  [shards(): lax.ppermute(by_y[k], 'ad', along_y(k))]
    ppermute x1, waiting for transfers between devices: 0.01 us -> 2.85 us  [shards(): lax.ppermute(left[HALF_ROWS:].astype(jnp.bfloat16), 'ad', ACROSS)]
  transfers between devices with their start and end apart: 33 -> 33, of which waited for: 20 -> 19; matrix products, arithmetic and copies ran while one was open for 12% -> 12% of each run, Pallas kernels for 17% -> 16%
where the time goes in v7:
time: 215 us; the launch traced here: 214 us
  waiting for transfers between devices  81.1 us (38%)
  starting transfers between devices  50.5 us (23%)
  Pallas kernels  42.2 us (20%)
  other arithmetic  14.5 us (7%)
  between operations  13.7 us (6%)
  local copies, waits for them, and re-layouts  10.9 us (5%)
    all_to_all x4, waiting for transfers between devices, swap(): lax.all_to_all(block, axes, split_axis=0, concat_axis=0, tiled=True, axis...  27 us
    all_to_all x4, starting transfers between devices, swap(): lax.all_to_all(block, axes, split_axis=0, concat_axis=0, tiled=True, axis...  23 us
    pallas_call x1, Pallas kernels, attend(): pl.pallas_call(attend_kernel, grid_spec=pltpu.PrefetchScalarGridSpec(num_...  18.3 us
    ppermute x1, waiting for transfers between devices, shards(): weight_slice = lax.ppermute(weight_slice, 'ad', PARTNERS)  14.4 us
    ppermute x3, waiting for transfers between devices, shards(): lax.ppermute(by_y[k], 'ad', along_y(k))  13.1 us
    pallas_call x1, Pallas kernels, project(): pl.pallas_call(project_kernel, grid_spec=pltpu.PrefetchScalarGridSpec(num...  11.9 us
    ppermute x4, waiting for transfers between devices, shards(): lax.ppermute(part, 'ad', PARTNERS)  7.94 us
    pallas_call x1, Pallas kernels, left_product(): pl.pallas_call(left_kernel, grid_spec=pltpu.PrefetchScalarGridSpec(num_sc...  7.55 us
  transfers between devices with their start and end apart: 33, of which 19 were waited for; matrix products, arithmetic and copies ran while one was open for 12% of the time, Pallas kernels for 16%

profile of v7, /device:TPU:1, one launch (start us, length us, event | category | flops | bytes accessed | tf_op | source)
XLA Modules:
  0.0 214.2 jit_solution(2306824095697243850)
XLA Ops:
  9.5 7.6 %all-to-all-start = ((bf16[16,32,320]{2,1,0:T(8,128)(2,1)}), bf16[16,32,320]{2,1,0:T(8,128)(2,1)S(1)}, u32[]{:S(2)}, u32[]{:S(2)}) async-start(bf16[16,32,320]{2,1,0:T(8,128)(2,1)} %bitcast.76), calls=%async_computation | async-start | bytes 786432 | tf_op jit(solution)/shard_map/all_to_all | solution.py:492
  22.4 3.9 %all-to-all-done = bf16[16,32,320]{2,1,0:T(8,128)(2,1)S(1)} async-done(((bf16[16,32,320]{2,1,0:T(8,128)(2,1)}), bf16[16,32,320]{2,1,0:T(8,128)(2,1)S(1)}, u32[]{:S(2)}, u32[]{:S(2)}) %all-to-all-start) | async-done | bytes 327712 | tf_op jit(solution)/shard_map/all_to_all | solution.py:492
  27.4 3.5 %all-to-all-start.1 = ((f32[16,32,128]{2,1,0:T(8,128)}), f32[16,32,128]{2,1,0:T(8,128)S(1)}, u32[]{:S(2)}, u32[]{:S(2)}) async-start(f32[16,32,128]{2,1,0:T(8,128)} %bitcast.13), calls=%async_computation.1 | async-start | bytes 524288 | tf_op jit(solution)/shard_map/all_to_all | solution.py:492
  32.1 7.1 %all-to-all-done.1 = f32[16,32,128]{2,1,0:T(8,128)S(1)} async-done(((f32[16,32,128]{2,1,0:T(8,128)}), f32[16,32,128]{2,1,0:T(8,128)S(1)}, u32[]{:S(2)}, u32[]{:S(2)}) %all-to-all-start.1) | async-done | bytes 262176 | tf_op jit(solution)/shard_map/all_to_all | solution.py:492
  47.2 4.6 %copy.52 = bf16[4,8,256,256]{3,2,0,1:T(8,128)(2,1)} copy(bf16[4,8,256,256]{3,2,1,0:T(8,128)(2,1)} %param.14) | data formatting | bytes 8388608 | tf_op args[1]
  54.8 3.1 %collective-permute-start.18 = (bf16[2,272,256]{2,1,0:T(8,128)(2,1)S(1)}, bf16[2,272,256]{2,1,0:T(8,128)(2,1)S(1)}, u32[]{:S(2)}, u32[]{:S(2)}) collective-permute-start(bf16[2,272,256]{2,1,0:T(8,128)(2,1)S(1)} %get-tuple-element.36), channel_id=1, source_target_pairs={{0,96},{16,112},{32,64},{48,80},{64,32},{80,48},{96,0},{112,16},{1... | collective-permute-start | bytes 835592 | tf_op jit(solution)/shard_map/ppermute | solution.py:487
  59.7 4.7 %all-to-all-start.2 = ((bf16[8,4,256,256]{3,2,1,0:T(8,128)(2,1)}), bf16[8,4,256,256]{3,2,1,0:T(8,128)(2,1)}, u32[]{:S(2)}, u32[]{:S(2)}) async-start(bf16[8,4,256,256]{3,2,1,0:T(8,128)(2,1)} %bitcast.77), calls=%async_computation.2 | async-start | bytes 8388608 | tf_op jit(solution)/shard_map/all_to_all | solution.py:492
  66.1 14.4 %collective-permute-done.6 = bf16[64,5120]{1,0:T(8,128)(2,1)S(1)} collective-permute-done((bf16[64,5120]{1,0:T(8,128)(2,1)S(1)}, bf16[64,5120]{1,0:T(8,128)(2,1)S(1)}, u32[]{:S(2)}, u32[]{:S(2)}) %collective-permute-start.6) | collective-permute-done | bytes 655392 | tf_op jit(solution)/shard_map/ppermute | solution.py:559
  80.5 11.9 %project.1 = bf16[8,64,640]{2,1,0:T(8,128)(2,1)} custom-call(s32[8]{0:T(128)} %copy-done.7, s32[16]{0:T(128)} %fusion.31.spot_ref, bf16[512,5120]{1,0:T(8,128)(2,1)} %all-gather.3.cloned.1.call-done.tokens_ref, bf16[5120,512]{1,0:T(8,128)(2,1)} %query_ref.1, bf16[128,5120]{1,0:T(8,128)(2,1)} %bitcast.94, bf16[16,32,128]{2,1,0:T(8,128)(2,1)} %bitcast.84, ...), custom_call_target="tpu_custom_call" | custom-call | flops 33554432000 | bytes 13000000 | tf_op jit(solution)/shard_map/project/pallas_call | solution.py:146
  97.1 2.7 %collective-permute-start.10 = (bf16[2,64,640]{2,1,0:T(8,128)(2,1)S(1)}, bf16[2,64,640]{2,1,0:T(8,128)(2,1)S(1)}, u32[]{:S(2)}, u32[]{:S(2)}) collective-permute-start(bf16[2,64,640]{2,1,0:T(8,128)(2,1)S(1)} %get-tuple-element.44), channel_id=1, source_target_pairs={{0,96},{16,112},{32,64},{48,80},{64,32},{80,48},{96,0},{112,16},{1... | collective-permute-start | bytes 491528 | tf_op jit(solution)/shard_map/ppermute | solution.py:487
  102.0 4.9 %collective-permute-done.10 = bf16[2,64,640]{2,1,0:T(8,128)(2,1)S(1)} collective-permute-done((bf16[2,64,640]{2,1,0:T(8,128)(2,1)S(1)}, bf16[2,64,640]{2,1,0:T(8,128)(2,1)S(1)}, u32[]{:S(2)}, u32[]{:S(2)}) %collective-permute-start.10) | collective-permute-done | bytes 163872 | tf_op jit(solution)/shard_map/ppermute | solution.py:487
  111.7 3.5 %collective-permute-done.13 = bf16[2,64,640]{2,1,0:T(8,128)(2,1)S(1)} collective-permute-done((bf16[2,64,640]{2,1,0:T(8,128)(2,1)S(1)}, bf16[2,64,640]{2,1,0:T(8,128)(2,1)S(1)}, u32[]{:S(2)}, u32[]{:S(2)}) %collective-permute-start.13) | collective-permute-done | bytes 163872 | tf_op jit(solution)/shard_map/ppermute | solution.py:579
  115.2 3.5 %collective-permute-done.12 = bf16[2,64,640]{2,1,0:T(8,128)(2,1)S(1)} collective-permute-done((bf16[2,64,640]{2,1,0:T(8,128)(2,1)S(1)}, bf16[2,64,640]{2,1,0:T(8,128)(2,1)S(1)}, u32[]{:S(2)}, u32[]{:S(2)}) %collective-permute-start.12) | collective-permute-done | bytes 163872 | tf_op jit(solution)/shard_map/ppermute | solution.py:579
  119.6 18.3 %attend.1 = bf16[8,2,32,1152]{3,2,1,0:T(8,128)(2,1)} custom-call(s32[8]{0:T(128)} %copy-done.8, s32[8]{0:T(128)} %get-tuple-element.29.local_ref, s32[8]{0:T(128)} %broadcast_xor_fusion.reach_ref, s32[2]{0:T(128)} %pad_add_fusion.1.place_ref, bf16[8,64,640]{2,1,0:T(8,128)(2,1)} %pad_maximum_fusion.1.own_ref, ...), custom_call_target="tpu_custom_call" | custom-call | flops 76504104960 | bytes 8000000 | tf_op jit(solution)/shard_map/attend/pallas_call | solution.py:305
  138.0 7.1 %all-to-all-start.3 = ((bf16[16,32,1152]{2,1,0:T(8,128)(2,1)}), bf16[16,32,1152]{2,1,0:T(8,128)(2,1)S(1)}, u32[]{:S(2)}, u32[]{:S(2)}) async-start(bf16[16,32,1152]{2,1,0:T(8,128)(2,1)} %bitcast.79), calls=%async_computation.3 | async-start | bytes 2359296 | tf_op jit(solution)/shard_map/all_to_all | solution.py:492
  145.8 16.0 %all-to-all-done.3 = bf16[16,32,1152]{2,1,0:T(8,128)(2,1)S(1)} async-done(((bf16[16,32,1152]{2,1,0:T(8,128)(2,1)}), bf16[16,32,1152]{2,1,0:T(8,128)(2,1)S(1)}, u32[]{:S(2)}, u32[]{:S(2)}) %all-to-all-start.3) | async-done | bytes 1179680 | tf_op jit(solution)/shard_map/all_to_all | solution.py:492
  162.8 7.6 %left_product.1 = (bf16[256,1024]{1,0:T(8,128)(2,1)}, bf16[64,3072]{1,0:T(8,128)(2,1)}, bf16[64,3072]{1,0:T(8,128)(2,1)}, bf16[64,3072]{1,0:T(8,128)(2,1)}, bf16[64,3072]{1,0:T(8,128)(2,1)}) custom-call(s32[3]{0:T(128)} %pad_add_fusion.place_ref, bf16[8,2,32,1152]{3,2,1,0:T(8,128)(2,1)} %bitcast.78, bf16[512,5120]{1,0:T(8,128)(2,1)} %own_ref.3, ...), custom_call_target="tpu_custom_call" | custom-call | flops 5368709120 | bytes 8000000 | tf_op jit(solution)/shard_map/left_product/pallas_call | solution.py:419
  173.8 4.3 %right_product.1 = (bf16[128,2048]{1,0:T(8,128)(2,1)}, bf16[128,2048]{1,0:T(8,128)(2,1)}) custom-call(bf16[256,1024]{1,0:T(8,128)(2,1)} %get-tuple-element.26.mixed_ref, bf16[512,5120]{1,0:T(8,128)(2,1)} %own_ref.3, bf16[512,5120]{1,0:T(8,128)(2,1)} %all-gather.5.cloned.1.call-done.other_ref), custom_call_target="tpu_custom_call" | custom-call | flops 5368709120 | bytes 8000000 | tf_op jit(solution)/shard_map/right_product/pallas_call | solution.py:443
  178.1 2.7 %collective-permute-start.23 = (bf16[128,2048]{1,0:T(8,128)(2,1)}, bf16[128,2048]{1,0:T(8,128)(2,1)S(1)}, u32[]{:S(2)}, u32[]{:S(2)}) collective-permute-start(bf16[128,2048]{1,0:T(8,128)(2,1)} %get-tuple-element.28), channel_id=1, source_target_pairs={{0,3},{1,2},{2,1},{3,0},{4,7},{5,6},{6,5},{7,4},{8,11},{9,10},{10,... | collective-permute-start | bytes 1572872 | tf_op jit(solution)/shard_map/ppermute | solution.py:613
  180.8 9.3 %collective-permute-done.21 = bf16[64,3072]{1,0:T(8,128)(2,1)S(1)} collective-permute-done((bf16[64,3072]{1,0:T(8,128)(2,1)}, bf16[64,3072]{1,0:T(8,128)(2,1)S(1)}, u32[]{:S(2)}, u32[]{:S(2)}) %collective-permute-start.21) | collective-permute-done | bytes 393248 | tf_op jit(solution)/shard_map/ppermute | solution.py:611
  190.1 3.7 %collective-permute-done.19 = bf16[64,3072]{1,0:T(8,128)(2,1)S(1)} collective-permute-done((bf16[64,3072]{1,0:T(8,128)(2,1)}, bf16[64,3072]{1,0:T(8,128)(2,1)S(1)}, u32[]{:S(2)}, u32[]{:S(2)}) %collective-permute-start.19) | collective-permute-done | bytes 393248 | tf_op jit(solution)/shard_map/ppermute | solution.py:611
  194.1 2.8 %collective-permute-start.22 = (bf16[32,3072]{1,0:T(8,128)(2,1)S(1)}, bf16[32,3072]{1,0:T(8,128)(2,1)S(1)}, u32[]{:S(2)}, u32[]{:S(2)}) collective-permute-start(bf16[32,3072]{1,0:T(8,128)(2,1)S(1)} %slice.55), channel_id=1, source_target_pairs={{0,3},{1,2},{2,1},{3,0},{4,7},{5,6},{6,5},{7,4},{8,11},{9,10},{10,... | collective-permute-start | bytes 589832 | tf_op jit(solution)/shard_map/ppermute | solution.py:615
  198.6 2.8 %collective-permute-done.22 = bf16[32,3072]{1,0:T(8,128)(2,1)S(1)} collective-permute-done((bf16[32,3072]{1,0:T(8,128)(2,1)S(1)}, bf16[32,3072]{1,0:T(8,128)(2,1)S(1)}, u32[]{:S(2)}, u32[]{:S(2)}) %collective-permute-start.22) | collective-permute-done | bytes 196640 | tf_op jit(solution)/shard_map/ppermute | solution.py:615
  202.6 3.9 %collective-permute-done.24 = bf16[32,2048]{1,0:T(8,128)(2,1)S(1)} collective-permute-done((bf16[32,2048]{1,0:T(8,128)(2,1)S(1)}, bf16[32,2048]{1,0:T(8,128)(2,1)S(1)}, u32[]{:S(2)}, u32[]{:S(2)}) %collective-permute-start.24) | collective-permute-done | bytes 131104 | tf_op jit(solution)/shard_map/ppermute | solution.py:618
  (129 shorter events, 46.2 us)
Async XLA Ops:
  6.5 74.0 %all-gather.3.cloned.1.call-start = ((), (), s32[]{:S(2)}) async-start(), calls=%async_computation.4 | async-start | bytes 5570560 | tf_op jit(solution)/shard_map/all_gather | solution.py:518
  9.5 16.8 %all-to-all-start = ((bf16[16,32,320]{2,1,0:T(8,128)(2,1)}), bf16[16,32,320]{2,1,0:T(8,128)(2,1)S(1)}, u32[]{:S(2)}, u32[]{:S(2)}) async-start(bf16[16,32,320]{2,1,0:T(8,128)(2,1)} %bitcast.76), calls=%async_computation | async-start | bytes 786432 | tf_op jit(solution)/shard_map/all_to_all | solution.py:492
  18.2 35.3 %collective-permute-start.15 = (bf16[4,1,272,256]{3,2,1,0:T(8,128)(2,1)}, bf16[4,1,272,256]{3,2,1,0:T(8,128)(2,1)}, u32[]{:S(2)}, u32[]{:S(2)}) collective-permute-start(bf16[4,1,272,256]{3,2,1,0:T(8,128)(2,1)} %get-tuple-element.37), channel_id=1, source_target_pairs={{0,16},{16,0},{32,48},{48,32},{64,80},{80,64},{96,112},{112,96},{1... | collective-permute-start | bytes 1671176 | tf_op jit(solution)/shard_map/ppermute | solution.py:482
  27.4 11.8 %all-to-all-start.1 = ((f32[16,32,128]{2,1,0:T(8,128)}), f32[16,32,128]{2,1,0:T(8,128)S(1)}, u32[]{:S(2)}, u32[]{:S(2)}) async-start(f32[16,32,128]{2,1,0:T(8,128)} %bitcast.13), calls=%async_computation.1 | async-start | bytes 524288 | tf_op jit(solution)/shard_map/all_to_all | solution.py:492
  45.7 6.2 %collective-permute-start.5 = (bf16[4,32,128]{2,1,0:T(8,128)(2,1)S(1)}, bf16[4,32,128]{2,1,0:T(8,128)(2,1)S(1)}, u32[]{:S(2)}, u32[]{:S(2)}) collective-permute-start(bf16[4,32,128]{2,1,0:T(8,128)(2,1)S(1)} %get-tuple-element.51), channel_id=1, source_target_pairs={{0,12},{1,13},{2,14},{3,15},{4,0},{5,1},{6,2},{7,3},{8,4},{9,5},{1... | collective-permute-start | bytes 98312 | tf_op jit(solution)/shard_map/ppermute | solution.py:549
  52.9 27.6 %collective-permute-start.6 = (bf16[64,5120]{1,0:T(8,128)(2,1)S(1)}, bf16[64,5120]{1,0:T(8,128)(2,1)S(1)}, u32[]{:S(2)}, u32[]{:S(2)}) collective-permute-start(bf16[64,5120]{1,0:T(8,128)(2,1)S(1)} %constant_dynamic-slice_fusion.2), channel_id=1, source_target_pairs={{0,1},{1,0},{2,3},{3,2},{4,5},{5,4},{6,7},{7,6},{8,9},{9,8},{10,11... | collective-permute-start | bytes 1966088 | tf_op jit(solution)/shard_map/ppermute | solution.py:559
  54.8 9.9 %collective-permute-start.18 = (bf16[2,272,256]{2,1,0:T(8,128)(2,1)S(1)}, bf16[2,272,256]{2,1,0:T(8,128)(2,1)S(1)}, u32[]{:S(2)}, u32[]{:S(2)}) collective-permute-start(bf16[2,272,256]{2,1,0:T(8,128)(2,1)S(1)} %get-tuple-element.36), channel_id=1, source_target_pairs={{0,96},{16,112},{32,64},{48,80},{64,32},{80,48},{96,0},{112,16},{1... | collective-permute-start | bytes 835592 | tf_op jit(solution)/shard_map/ppermute | solution.py:487
  57.9 7.0 %collective-permute-start.17 = (bf16[2,272,256]{2,1,0:T(8,128)(2,1)S(1)}, bf16[2,272,256]{2,1,0:T(8,128)(2,1)S(1)}, u32[]{:S(2)}, u32[]{:S(2)}) collective-permute-start(bf16[2,272,256]{2,1,0:T(8,128)(2,1)S(1)} %get-tuple-element.35), channel_id=1, source_target_pairs={{0,64},{16,80},{32,96},{48,112},{64,0},{80,16},{96,32},{112,48},{1... | collective-permute-start | bytes 835592 | tf_op jit(solution)/shard_map/ppermute | solution.py:487
  57.9 8.0 %collective-permute-start.16 = (bf16[2,272,256]{2,1,0:T(8,128)(2,1)S(1)}, bf16[2,272,256]{2,1,0:T(8,128)(2,1)S(1)}, u32[]{:S(2)}, u32[]{:S(2)}) collective-permute-start(bf16[2,272,256]{2,1,0:T(8,128)(2,1)S(1)} %get-tuple-element.34), channel_id=1, source_target_pairs={{0,32},{16,48},{32,0},{48,16},{64,96},{80,112},{96,64},{112,80},{1... | collective-permute-start | bytes 835592 | tf_op jit(solution)/shard_map/ppermute | solution.py:487
  59.7 59.9 %all-to-all-start.2 = ((bf16[8,4,256,256]{3,2,1,0:T(8,128)(2,1)}), bf16[8,4,256,256]{3,2,1,0:T(8,128)(2,1)}, u32[]{:S(2)}, u32[]{:S(2)}) async-start(bf16[8,4,256,256]{3,2,1,0:T(8,128)(2,1)} %bitcast.77), calls=%async_computation.2 | async-start | bytes 8388608 | tf_op jit(solution)/shard_map/all_to_all | solution.py:492
  64.4 97.3 %all-gather.5.cloned.1.call-start = ((), (), s32[]{:S(2)}) async-start(), calls=%async_computation.5 | async-start | bytes 5898240 | tf_op jit(solution)/shard_map/all_gather | solution.py:561
  97.1 9.8 %collective-permute-start.10 = (bf16[2,64,640]{2,1,0:T(8,128)(2,1)S(1)}, bf16[2,64,640]{2,1,0:T(8,128)(2,1)S(1)}, u32[]{:S(2)}, u32[]{:S(2)}) collective-permute-start(bf16[2,64,640]{2,1,0:T(8,128)(2,1)S(1)} %get-tuple-element.44), channel_id=1, source_target_pairs={{0,96},{16,112},{32,64},{48,80},{64,32},{80,48},{96,0},{112,16},{1... | collective-permute-start | bytes 491528 | tf_op jit(solution)/shard_map/ppermute | solution.py:487
  99.8 7.5 %collective-permute-start.9 = (bf16[2,64,640]{2,1,0:T(8,128)(2,1)S(1)}, bf16[2,64,640]{2,1,0:T(8,128)(2,1)S(1)}, u32[]{:S(2)}, u32[]{:S(2)}) collective-permute-start(bf16[2,64,640]{2,1,0:T(8,128)(2,1)S(1)} %get-tuple-element.43), channel_id=1, source_target_pairs={{0,64},{16,80},{32,96},{48,112},{64,0},{80,16},{96,32},{112,48},{1... | collective-permute-start | bytes 491528 | tf_op jit(solution)/shard_map/ppermute | solution.py:487
  100.2 8.1 %collective-permute-start.8 = (bf16[2,64,640]{2,1,0:T(8,128)(2,1)S(1)}, bf16[2,64,640]{2,1,0:T(8,128)(2,1)S(1)}, u32[]{:S(2)}, u32[]{:S(2)}) collective-permute-start(bf16[2,64,640]{2,1,0:T(8,128)(2,1)S(1)} %get-tuple-element.42), channel_id=1, source_target_pairs={{0,32},{16,48},{32,0},{48,16},{64,96},{80,112},{96,64},{112,80},{1... | collective-permute-start | bytes 491528 | tf_op jit(solution)/shard_map/ppermute | solution.py:487
  101.5 9.3 %collective-permute-start.11 = (bf16[2,64,640]{2,1,0:T(8,128)(2,1)S(1)}, bf16[2,64,640]{2,1,0:T(8,128)(2,1)S(1)}, u32[]{:S(2)}, u32[]{:S(2)}) collective-permute-start(bf16[2,64,640]{2,1,0:T(8,128)(2,1)S(1)} %get-tuple-element.41), channel_id=1, source_target_pairs={{0,1},{1,0},{2,3},{3,2},{4,5},{5,4},{6,7},{7,6},{8,9},{9,8},{10,11... | collective-permute-start | bytes 491528 | tf_op jit(solution)/shard_map/ppermute | solution.py:579
  107.3 7.8 %collective-permute-start.13 = (bf16[2,64,640]{2,1,0:T(8,128)(2,1)S(1)}, bf16[2,64,640]{2,1,0:T(8,128)(2,1)S(1)}, u32[]{:S(2)}, u32[]{:S(2)}) collective-permute-start(bf16[2,64,640]{2,1,0:T(8,128)(2,1)S(1)} %collective-permute-done.9), channel_id=1, source_target_pairs={{0,1},{1,0},{2,3},{3,2},{4,5},{5,4},{6,7},{7,6},{8,9},{9,8},{10,11... | collective-permute-start | bytes 491528 | tf_op jit(solution)/shard_map/ppermute | solution.py:579
  108.4 10.3 %collective-permute-start.12 = (bf16[2,64,640]{2,1,0:T(8,128)(2,1)S(1)}, bf16[2,64,640]{2,1,0:T(8,128)(2,1)S(1)}, u32[]{:S(2)}, u32[]{:S(2)}) collective-permute-start(bf16[2,64,640]{2,1,0:T(8,128)(2,1)S(1)} %collective-permute-done.8), channel_id=1, source_target_pairs={{0,1},{1,0},{2,3},{3,2},{4,5},{5,4},{6,7},{7,6},{8,9},{9,8},{10,11... | collective-permute-start | bytes 491528 | tf_op jit(solution)/shard_map/ppermute | solution.py:579
  138.0 23.8 %all-to-all-start.3 = ((bf16[16,32,1152]{2,1,0:T(8,128)(2,1)}), bf16[16,32,1152]{2,1,0:T(8,128)(2,1)S(1)}, u32[]{:S(2)}, u32[]{:S(2)}) async-start(bf16[16,32,1152]{2,1,0:T(8,128)(2,1)} %bitcast.79), calls=%async_computation.3 | async-start | bytes 2359296 | tf_op jit(solution)/shard_map/all_to_all | solution.py:492
  170.4 19.8 %collective-permute-start.21 = (bf16[64,3072]{1,0:T(8,128)(2,1)}, bf16[64,3072]{1,0:T(8,128)(2,1)S(1)}, u32[]{:S(2)}, u32[]{:S(2)}) collective-permute-start(bf16[64,3072]{1,0:T(8,128)(2,1)} %get-tuple-element.25), channel_id=1, source_target_pairs={{0,12},{1,13},{2,14},{3,15},{4,0},{5,1},{6,2},{7,3},{8,4},{9,5},{1... | collective-permute-start | bytes 1179656 | tf_op jit(solution)/shard_map/ppermute | solution.py:611
  172.7 17.5 %collective-permute-start.20 = (bf16[64,3072]{1,0:T(8,128)(2,1)}, bf16[64,3072]{1,0:T(8,128)(2,1)S(1)}, u32[]{:S(2)}, u32[]{:S(2)}) collective-permute-start(bf16[64,3072]{1,0:T(8,128)(2,1)} %get-tuple-element.24), channel_id=1, source_target_pairs={{0,8},{1,9},{2,10},{3,11},{4,12},{5,13},{6,14},{7,15},{8,0},{9,1},... | collective-permute-start | bytes 1179656 | tf_op jit(solution)/shard_map/ppermute | solution.py:611
  173.2 20.7 %collective-permute-start.19 = (bf16[64,3072]{1,0:T(8,128)(2,1)}, bf16[64,3072]{1,0:T(8,128)(2,1)S(1)}, u32[]{:S(2)}, u32[]{:S(2)}) collective-permute-start(bf16[64,3072]{1,0:T(8,128)(2,1)} %get-tuple-element.23), channel_id=1, source_target_pairs={{0,4},{1,5},{2,6},{3,7},{4,8},{5,9},{6,10},{7,11},{8,12},{9,13},{1... | collective-permute-start | bytes 1179656 | tf_op jit(solution)/shard_map/ppermute | solution.py:611
  178.1 18.8 %collective-permute-start.23 = (bf16[128,2048]{1,0:T(8,128)(2,1)}, bf16[128,2048]{1,0:T(8,128)(2,1)S(1)}, u32[]{:S(2)}, u32[]{:S(2)}) collective-permute-start(bf16[128,2048]{1,0:T(8,128)(2,1)} %get-tuple-element.28), channel_id=1, source_target_pairs={{0,3},{1,2},{2,1},{3,0},{4,7},{5,6},{6,5},{7,4},{8,11},{9,10},{10,... | collective-permute-start | bytes 1572872 | tf_op jit(solution)/shard_map/ppermute | solution.py:613
  194.1 7.4 %collective-permute-start.22 = (bf16[32,3072]{1,0:T(8,128)(2,1)S(1)}, bf16[32,3072]{1,0:T(8,128)(2,1)S(1)}, u32[]{:S(2)}, u32[]{:S(2)}) collective-permute-start(bf16[32,3072]{1,0:T(8,128)(2,1)S(1)} %slice.55), channel_id=1, source_target_pairs={{0,3},{1,2},{2,1},{3,0},{4,7},{5,6},{6,5},{7,4},{8,11},{9,10},{10,... | collective-permute-start | bytes 589832 | tf_op jit(solution)/shard_map/ppermute | solution.py:615
  197.8 8.7 %collective-permute-start.24 = (bf16[32,2048]{1,0:T(8,128)(2,1)S(1)}, bf16[32,2048]{1,0:T(8,128)(2,1)S(1)}, u32[]{:S(2)}, u32[]{:S(2)}) collective-permute-start(bf16[32,2048]{1,0:T(8,128)(2,1)S(1)} %get-tuple-element.47), channel_id=1, source_target_pairs={{0,4},{1,5},{2,6},{3,7},{4,8},{5,9},{6,10},{7,11},{8,12},{9,13},{1... | collective-permute-start | bytes 393224 | tf_op jit(solution)/shard_map/ppermute | solution.py:618
  (22 other events, 158.8 us)
Sparse Core Ops, SparseCore 0:
  9.5 69.3 all-gather.2
  96.1 37.5 all-gather.4

commit v8 on v7

--- a/solution.py
+++ b/solution.py
@@ -325,7 +325,7 @@
             ),
         ),
         out_shape=jax.ShapeDtypeStruct((GROUPS, 2, HALF_ROWS, BACK_WIDTH), jnp.bfloat16),
-        compiler_params=pltpu.CompilerParams(vmem_limit_bytes=60 * 2**20),
+        compiler_params=pltpu.CompilerParams(vmem_limit_bytes=30 * 2**20),
         cost_estimate=pl.CostEstimate(
             flops=20 * GROUPS * 512 * 2432 * 384,
             bytes_accessed=8_000_000,

time: 215 us -> 213 us (level)
  other arithmetic: 14.5 us -> 11 us
  waiting for transfers between devices: 81.1 us -> 83.6 us
    unnamed x27 -> x25, local copies, waits for them, and re-layouts: 5.7 us -> 5.7 us
  transfers between devices with their start and end apart: 33 -> 33, of which waited for: 19 -> 19; matrix products, arithmetic and copies ran while one was open for 12% -> 10% of each run, Pallas kernels for 16% -> 16%
where the time goes in v8:
time: 213 us
  waiting for transfers between devices  83.6 us (39%)
  starting transfers between devices  51 us (24%)
  Pallas kernels  41.1 us (19%)
  between operations  13.8 us (6%)
  local copies, waits for them, and re-layouts  11 us (5%)
  other arithmetic  11 us (5%)
    all_to_all x4, waiting for transfers between devices, swap(): lax.all_to_all(block, axes, split_axis=0, concat_axis=0, tiled=True, axis...  28 us
    all_to_all x4, starting transfers between devices, swap(): lax.all_to_all(block, axes, split_axis=0, concat_axis=0, tiled=True, axis...  23 us
    pallas_call x1, Pallas kernels, attend(): pl.pallas_call(attend_kernel, grid_spec=pltpu.PrefetchScalarGridSpec(num_...  17.3 us
    ppermute x1, waiting for transfers between devices, shards(): weight_slice = lax.ppermute(weight_slice, 'ad', PARTNERS)  14.7 us
    ppermute x3, waiting for transfers between devices, shards(): lax.ppermute(by_y[k], 'ad', along_y(k))  12.8 us
    pallas_call x1, Pallas kernels, project(): pl.pallas_call(project_kernel, grid_spec=pltpu.PrefetchScalarGridSpec(num...  12 us
    ppermute x4, waiting for transfers between devices, shards(): lax.ppermute(part, 'ad', PARTNERS)  9.54 us
    pallas_call x1, Pallas kernels, left_product(): pl.pallas_call(left_kernel, grid_spec=pltpu.PrefetchScalarGridSpec(num_sc...  7.54 us
  transfers between devices with their start and end apart: 33, of which 19 were waited for; matrix products, arithmetic and copies ran while one was open for 10% of the time, Pallas kernels for 16%

profile of v8, /device:TPU:1, one launch (start us, length us, event | category | flops | bytes accessed | tf_op | source)
XLA Modules:
  0.0 212.6 jit_solution(13709959318469657256)
XLA Ops:
  9.5 7.6 %all-to-all-start = ((bf16[16,32,320]{2,1,0:T(8,128)(2,1)}), bf16[16,32,320]{2,1,0:T(8,128)(2,1)S(1)}, u32[]{:S(2)}, u32[]{:S(2)}) async-start(bf16[16,32,320]{2,1,0:T(8,128)(2,1)} %bitcast.76), calls=%async_computation | async-start | bytes 786432 | tf_op jit(solution)/shard_map/all_to_all | solution.py:492
  21.4 4.9 %all-to-all-done = bf16[16,32,320]{2,1,0:T(8,128)(2,1)S(1)} async-done(((bf16[16,32,320]{2,1,0:T(8,128)(2,1)}), bf16[16,32,320]{2,1,0:T(8,128)(2,1)S(1)}, u32[]{:S(2)}, u32[]{:S(2)}) %all-to-all-start) | async-done | bytes 327712 | tf_op jit(solution)/shard_map/all_to_all | solution.py:492
  27.4 3.5 %all-to-all-start.1 = ((f32[16,32,128]{2,1,0:T(8,128)}), f32[16,32,128]{2,1,0:T(8,128)S(1)}, u32[]{:S(2)}, u32[]{:S(2)}) async-start(f32[16,32,128]{2,1,0:T(8,128)} %bitcast.13), calls=%async_computation.1 | async-start | bytes 524288 | tf_op jit(solution)/shard_map/all_to_all | solution.py:492
  32.1 7.1 %all-to-all-done.1 = f32[16,32,128]{2,1,0:T(8,128)S(1)} async-done(((f32[16,32,128]{2,1,0:T(8,128)}), f32[16,32,128]{2,1,0:T(8,128)S(1)}, u32[]{:S(2)}, u32[]{:S(2)}) %all-to-all-start.1) | async-done | bytes 262176 | tf_op jit(solution)/shard_map/all_to_all | solution.py:492
  47.2 4.6 %copy.52 = bf16[4,8,256,256]{3,2,0,1:T(8,128)(2,1)} copy(bf16[4,8,256,256]{3,2,1,0:T(8,128)(2,1)} %param.14) | data formatting | bytes 8388608 | tf_op args[1]
  53.8 3.0 %collective-permute-start.18 = (bf16[2,272,256]{2,1,0:T(8,128)(2,1)}, bf16[2,272,256]{2,1,0:T(8,128)(2,1)S(1)}, u32[]{:S(2)}, u32[]{:S(2)}) collective-permute-start(bf16[2,272,256]{2,1,0:T(8,128)(2,1)} %get-tuple-element.36), channel_id=1, source_target_pairs={{0,96},{16,112},{32,64},{48,80},{64,32},{80,48},{96,0},{112,16},{1... | collective-permute-start | bytes 835592 | tf_op jit(solution)/shard_map/ppermute | solution.py:487
  58.5 4.7 %all-to-all-start.2 = ((bf16[8,4,256,256]{3,2,1,0:T(8,128)(2,1)}), bf16[8,4,256,256]{3,2,1,0:T(8,128)(2,1)}, u32[]{:S(2)}, u32[]{:S(2)}) async-start(bf16[8,4,256,256]{3,2,1,0:T(8,128)(2,1)} %bitcast.78), calls=%async_computation.2 | async-start | bytes 8388608 | tf_op jit(solution)/shard_map/all_to_all | solution.py:492
  65.8 14.7 %collective-permute-done.6 = bf16[64,5120]{1,0:T(8,128)(2,1)S(1)} collective-permute-done((bf16[64,5120]{1,0:T(8,128)(2,1)S(1)}, bf16[64,5120]{1,0:T(8,128)(2,1)S(1)}, u32[]{:S(2)}, u32[]{:S(2)}) %collective-permute-start.6) | collective-permute-done | bytes 655392 | tf_op jit(solution)/shard_map/ppermute | solution.py:559
  80.5 12.0 %project.1 = bf16[8,64,640]{2,1,0:T(8,128)(2,1)} custom-call(s32[8]{0:T(128)} %copy-done.7, s32[16]{0:T(128)} %fusion.31.spot_ref, bf16[512,5120]{1,0:T(8,128)(2,1)} %all-gather.3.cloned.1.call-done.tokens_ref, bf16[5120,512]{1,0:T(8,128)(2,1)} %query_ref.1, bf16[128,5120]{1,0:T(8,128)(2,1)} %bitcast.94, bf16[16,32,128]{2,1,0:T(8,128)(2,1)} %bitcast.84, ...), custom_call_target="tpu_custom_call" | custom-call | flops 33554432000 | bytes 13000000 | tf_op jit(solution)/shard_map/project/pallas_call | solution.py:146
  97.1 2.7 %collective-permute-start.10 = (bf16[2,64,640]{2,1,0:T(8,128)(2,1)S(1)}, bf16[2,64,640]{2,1,0:T(8,128)(2,1)S(1)}, u32[]{:S(2)}, u32[]{:S(2)}) collective-permute-start(bf16[2,64,640]{2,1,0:T(8,128)(2,1)S(1)} %get-tuple-element.44), channel_id=1, source_target_pairs={{0,96},{16,112},{32,64},{48,80},{64,32},{80,48},{96,0},{112,16},{1... | collective-permute-start | bytes 491528 | tf_op jit(solution)/shard_map/ppermute | solution.py:487
  102.0 4.9 %collective-permute-done.10 = bf16[2,64,640]{2,1,0:T(8,128)(2,1)S(1)} collective-permute-done((bf16[2,64,640]{2,1,0:T(8,128)(2,1)S(1)}, bf16[2,64,640]{2,1,0:T(8,128)(2,1)S(1)}, u32[]{:S(2)}, u32[]{:S(2)}) %collective-permute-start.10) | collective-permute-done | bytes 163872 | tf_op jit(solution)/shard_map/ppermute | solution.py:487
  111.7 3.5 %collective-permute-done.13 = bf16[2,64,640]{2,1,0:T(8,128)(2,1)S(1)} collective-permute-done((bf16[2,64,640]{2,1,0:T(8,128)(2,1)S(1)}, bf16[2,64,640]{2,1,0:T(8,128)(2,1)S(1)}, u32[]{:S(2)}, u32[]{:S(2)}) %collective-permute-start.13) | collective-permute-done | bytes 163872 | tf_op jit(solution)/shard_map/ppermute | solution.py:579
  115.2 3.5 %collective-permute-done.12 = bf16[2,64,640]{2,1,0:T(8,128)(2,1)S(1)} collective-permute-done((bf16[2,64,640]{2,1,0:T(8,128)(2,1)S(1)}, bf16[2,64,640]{2,1,0:T(8,128)(2,1)S(1)}, u32[]{:S(2)}, u32[]{:S(2)}) %collective-permute-start.12) | collective-permute-done | bytes 163872 | tf_op jit(solution)/shard_map/ppermute | solution.py:579
  118.8 17.3 %attend.1 = bf16[8,2,32,1152]{3,2,1,0:T(8,128)(2,1)} custom-call(s32[8]{0:T(128)S(1)} %get-tuple-element.30.order_ref, s32[8]{0:T(128)S(1)} %get-tuple-element.29.local_ref, s32[8]{0:T(128)S(1)} %broadcast_xor_fusion.reach_ref, s32[2]{0:T(128)S(1)} %pad_add_fusion.1.place_ref, bf16[8,64,640]{2,1,0:T(8,128)(2,1)S(1)} %pad_maximum_fusion.1.own_ref, ...), custom_call_target="tpu_custom_call" | custom-call | flops 76504104960 | bytes 8000000 | tf_op jit(solution)/shard_map/attend/pallas_call | solution.py:305
  136.1 7.1 %all-to-all-start.3 = ((bf16[16,32,1152]{2,1,0:T(8,128)(2,1)}), bf16[16,32,1152]{2,1,0:T(8,128)(2,1)S(1)}, u32[]{:S(2)}, u32[]{:S(2)}) async-start(bf16[16,32,1152]{2,1,0:T(8,128)(2,1)} %bitcast.40), calls=%async_computation.3 | async-start | bytes 2359296 | tf_op jit(solution)/shard_map/all_to_all | solution.py:492
  143.9 16.0 %all-to-all-done.3 = bf16[16,32,1152]{2,1,0:T(8,128)(2,1)S(1)} async-done(((bf16[16,32,1152]{2,1,0:T(8,128)(2,1)}), bf16[16,32,1152]{2,1,0:T(8,128)(2,1)S(1)}, u32[]{:S(2)}, u32[]{:S(2)}) %all-to-all-start.3) | async-done | bytes 1179680 | tf_op jit(solution)/shard_map/all_to_all | solution.py:492
  161.0 7.5 %left_product.1 = (bf16[256,1024]{1,0:T(8,128)(2,1)}, bf16[64,3072]{1,0:T(8,128)(2,1)}, bf16[64,3072]{1,0:T(8,128)(2,1)}, bf16[64,3072]{1,0:T(8,128)(2,1)}, bf16[64,3072]{1,0:T(8,128)(2,1)}) custom-call(s32[3]{0:T(128)} %pad_add_fusion.place_ref, bf16[8,2,32,1152]{3,2,1,0:T(8,128)(2,1)} %bitcast.79, bf16[512,5120]{1,0:T(8,128)(2,1)} %own_ref.3, ...), custom_call_target="tpu_custom_call" | custom-call | flops 5368709120 | bytes 8000000 | tf_op jit(solution)/shard_map/left_product/pallas_call | solution.py:419
  172.1 4.3 %right_product.1 = (bf16[128,2048]{1,0:T(8,128)(2,1)}, bf16[128,2048]{1,0:T(8,128)(2,1)}) custom-call(bf16[256,1024]{1,0:T(8,128)(2,1)} %get-tuple-element.26.mixed_ref, bf16[512,5120]{1,0:T(8,128)(2,1)} %own_ref.3, bf16[512,5120]{1,0:T(8,128)(2,1)} %all-gather.5.cloned.1.call-done.other_ref), custom_call_target="tpu_custom_call" | custom-call | flops 5368709120 | bytes 8000000 | tf_op jit(solution)/shard_map/right_product/pallas_call | solution.py:443
  176.4 2.9 %collective-permute-start.23 = (bf16[128,2048]{1,0:T(8,128)(2,1)}, bf16[128,2048]{1,0:T(8,128)(2,1)S(1)}, u32[]{:S(2)}, u32[]{:S(2)}) collective-permute-start(bf16[128,2048]{1,0:T(8,128)(2,1)} %get-tuple-element.28), channel_id=1, source_target_pairs={{0,3},{1,2},{2,1},{3,0},{4,7},{5,6},{6,5},{7,4},{8,11},{9,10},{10,... | collective-permute-start | bytes 1572872 | tf_op jit(solution)/shard_map/ppermute | solution.py:613
  179.4 9.1 %collective-permute-done.21 = bf16[64,3072]{1,0:T(8,128)(2,1)S(1)} collective-permute-done((bf16[64,3072]{1,0:T(8,128)(2,1)}, bf16[64,3072]{1,0:T(8,128)(2,1)S(1)}, u32[]{:S(2)}, u32[]{:S(2)}) %collective-permute-start.21) | collective-permute-done | bytes 393248 | tf_op jit(solution)/shard_map/ppermute | solution.py:611
  188.5 3.7 %collective-permute-done.19 = bf16[64,3072]{1,0:T(8,128)(2,1)S(1)} collective-permute-done((bf16[64,3072]{1,0:T(8,128)(2,1)}, bf16[64,3072]{1,0:T(8,128)(2,1)S(1)}, u32[]{:S(2)}, u32[]{:S(2)}) %collective-permute-start.19) | collective-permute-done | bytes 393248 | tf_op jit(solution)/shard_map/ppermute | solution.py:611
  192.4 2.9 %collective-permute-start.22 = (bf16[32,3072]{1,0:T(8,128)(2,1)S(1)}, bf16[32,3072]{1,0:T(8,128)(2,1)S(1)}, u32[]{:S(2)}, u32[]{:S(2)}) collective-permute-start(bf16[32,3072]{1,0:T(8,128)(2,1)S(1)} %slice.55), channel_id=1, source_target_pairs={{0,3},{1,2},{2,1},{3,0},{4,7},{5,6},{6,5},{7,4},{8,11},{9,10},{10,... | collective-permute-start | bytes 589832 | tf_op jit(solution)/shard_map/ppermute | solution.py:615
  197.2 2.9 %collective-permute-done.22 = bf16[32,3072]{1,0:T(8,128)(2,1)S(1)} collective-permute-done((bf16[32,3072]{1,0:T(8,128)(2,1)S(1)}, bf16[32,3072]{1,0:T(8,128)(2,1)S(1)}, u32[]{:S(2)}, u32[]{:S(2)}) %collective-permute-start.22) | collective-permute-done | bytes 196640 | tf_op jit(solution)/shard_map/ppermute | solution.py:615
  201.1 3.8 %collective-permute-done.24 = bf16[32,2048]{1,0:T(8,128)(2,1)S(1)} collective-permute-done((bf16[32,2048]{1,0:T(8,128)(2,1)S(1)}, bf16[32,2048]{1,0:T(8,128)(2,1)S(1)}, u32[]{:S(2)}, u32[]{:S(2)}) %collective-permute-start.24) | collective-permute-done | bytes 131104 | tf_op jit(solution)/shard_map/ppermute | solution.py:618
  (127 shorter events, 44.3 us)
Async XLA Ops:
  6.5 74.0 %all-gather.3.cloned.1.call-start = ((), (), s32[]{:S(2)}) async-start(), calls=%async_computation.4 | async-start | bytes 5570560 | tf_op jit(solution)/shard_map/all_gather | solution.py:518
  9.5 16.8 %all-to-all-start = ((bf16[16,32,320]{2,1,0:T(8,128)(2,1)}), bf16[16,32,320]{2,1,0:T(8,128)(2,1)S(1)}, u32[]{:S(2)}, u32[]{:S(2)}) async-start(bf16[16,32,320]{2,1,0:T(8,128)(2,1)} %bitcast.76), calls=%async_computation | async-start | bytes 786432 | tf_op jit(solution)/shard_map/all_to_all | solution.py:492
  18.3 34.7 %collective-permute-start.15 = (bf16[4,1,272,256]{3,2,1,0:T(8,128)(2,1)}, bf16[4,1,272,256]{3,2,1,0:T(8,128)(2,1)S(1)}, u32[]{:S(2)}, u32[]{:S(2)}) collective-permute-start(bf16[4,1,272,256]{3,2,1,0:T(8,128)(2,1)} %get-tuple-element.37), channel_id=1, source_target_pairs={{0,16},{16,0},{32,48},{48,32},{64,80},{80,64},{96,112},{112,96},{1... | collective-permute-start | bytes 1671176 | tf_op jit(solution)/shard_map/ppermute | solution.py:482
  27.4 11.8 %all-to-all-start.1 = ((f32[16,32,128]{2,1,0:T(8,128)}), f32[16,32,128]{2,1,0:T(8,128)S(1)}, u32[]{:S(2)}, u32[]{:S(2)}) async-start(f32[16,32,128]{2,1,0:T(8,128)} %bitcast.13), calls=%async_computation.1 | async-start | bytes 524288 | tf_op jit(solution)/shard_map/all_to_all | solution.py:492
  45.7 6.2 %collective-permute-start.5 = (bf16[4,32,128]{2,1,0:T(8,128)(2,1)S(1)}, bf16[4,32,128]{2,1,0:T(8,128)(2,1)S(1)}, u32[]{:S(2)}, u32[]{:S(2)}) collective-permute-start(bf16[4,32,128]{2,1,0:T(8,128)(2,1)S(1)} %get-tuple-element.51), channel_id=1, source_target_pairs={{0,12},{1,13},{2,14},{3,15},{4,0},{5,1},{6,2},{7,3},{8,4},{9,5},{1... | collective-permute-start | bytes 98312 | tf_op jit(solution)/shard_map/ppermute | solution.py:549
  52.9 27.6 %collective-permute-start.6 = (bf16[64,5120]{1,0:T(8,128)(2,1)S(1)}, bf16[64,5120]{1,0:T(8,128)(2,1)S(1)}, u32[]{:S(2)}, u32[]{:S(2)}) collective-permute-start(bf16[64,5120]{1,0:T(8,128)(2,1)S(1)} %constant_dynamic-slice_fusion.2), channel_id=1, source_target_pairs={{0,1},{1,0},{2,3},{3,2},{4,5},{5,4},{6,7},{7,6},{8,9},{9,8},{10,11... | collective-permute-start | bytes 1966088 | tf_op jit(solution)/shard_map/ppermute | solution.py:559
  53.8 10.6 %collective-permute-start.18 = (bf16[2,272,256]{2,1,0:T(8,128)(2,1)}, bf16[2,272,256]{2,1,0:T(8,128)(2,1)S(1)}, u32[]{:S(2)}, u32[]{:S(2)}) collective-permute-start(bf16[2,272,256]{2,1,0:T(8,128)(2,1)} %get-tuple-element.36), channel_id=1, source_target_pairs={{0,96},{16,112},{32,64},{48,80},{64,32},{80,48},{96,0},{112,16},{1... | collective-permute-start | bytes 835592 | tf_op jit(solution)/shard_map/ppermute | solution.py:487
  56.8 7.6 %collective-permute-start.17 = (bf16[2,272,256]{2,1,0:T(8,128)(2,1)S(1)}, bf16[2,272,256]{2,1,0:T(8,128)(2,1)S(1)}, u32[]{:S(2)}, u32[]{:S(2)}) collective-permute-start(bf16[2,272,256]{2,1,0:T(8,128)(2,1)S(1)} %get-tuple-element.35), channel_id=1, source_target_pairs={{0,64},{16,80},{32,96},{48,112},{64,0},{80,16},{96,32},{112,48},{1... | collective-permute-start | bytes 835592 | tf_op jit(solution)/shard_map/ppermute | solution.py:487
  56.8 7.9 %collective-permute-start.16 = (bf16[2,272,256]{2,1,0:T(8,128)(2,1)S(1)}, bf16[2,272,256]{2,1,0:T(8,128)(2,1)}, u32[]{:S(2)}, u32[]{:S(2)}) collective-permute-start(bf16[2,272,256]{2,1,0:T(8,128)(2,1)S(1)} %get-tuple-element.34), channel_id=1, source_target_pairs={{0,32},{16,48},{32,0},{48,16},{64,96},{80,112},{96,64},{112,80},{1... | collective-permute-start | bytes 835592 | tf_op jit(solution)/shard_map/ppermute | solution.py:487
  58.5 60.3 %all-to-all-start.2 = ((bf16[8,4,256,256]{3,2,1,0:T(8,128)(2,1)}), bf16[8,4,256,256]{3,2,1,0:T(8,128)(2,1)}, u32[]{:S(2)}, u32[]{:S(2)}) async-start(bf16[8,4,256,256]{3,2,1,0:T(8,128)(2,1)} %bitcast.78), calls=%async_computation.2 | async-start | bytes 8388608 | tf_op jit(solution)/shard_map/all_to_all | solution.py:492
  63.2 96.7 %all-gather.5.cloned.1.call-start = ((), (), s32[]{:S(2)}) async-start(), calls=%async_computation.5 | async-start | bytes 5898240 | tf_op jit(solution)/shard_map/all_gather | solution.py:561
  97.1 9.8 %collective-permute-start.10 = (bf16[2,64,640]{2,1,0:T(8,128)(2,1)S(1)}, bf16[2,64,640]{2,1,0:T(8,128)(2,1)S(1)}, u32[]{:S(2)}, u32[]{:S(2)}) collective-permute-start(bf16[2,64,640]{2,1,0:T(8,128)(2,1)S(1)} %get-tuple-element.44), channel_id=1, source_target_pairs={{0,96},{16,112},{32,64},{48,80},{64,32},{80,48},{96,0},{112,16},{1... | collective-permute-start | bytes 491528 | tf_op jit(solution)/shard_map/ppermute | solution.py:487
  99.8 7.5 %collective-permute-start.9 = (bf16[2,64,640]{2,1,0:T(8,128)(2,1)S(1)}, bf16[2,64,640]{2,1,0:T(8,128)(2,1)S(1)}, u32[]{:S(2)}, u32[]{:S(2)}) collective-permute-start(bf16[2,64,640]{2,1,0:T(8,128)(2,1)S(1)} %get-tuple-element.43), channel_id=1, source_target_pairs={{0,64},{16,80},{32,96},{48,112},{64,0},{80,16},{96,32},{112,48},{1... | collective-permute-start | bytes 491528 | tf_op jit(solution)/shard_map/ppermute | solution.py:487
  100.2 8.1 %collective-permute-start.8 = (bf16[2,64,640]{2,1,0:T(8,128)(2,1)S(1)}, bf16[2,64,640]{2,1,0:T(8,128)(2,1)S(1)}, u32[]{:S(2)}, u32[]{:S(2)}) collective-permute-start(bf16[2,64,640]{2,1,0:T(8,128)(2,1)S(1)} %get-tuple-element.42), channel_id=1, source_target_pairs={{0,32},{16,48},{32,0},{48,16},{64,96},{80,112},{96,64},{112,80},{1... | collective-permute-start | bytes 491528 | tf_op jit(solution)/shard_map/ppermute | solution.py:487
  101.5 7.7 %collective-permute-start.11 = (bf16[2,64,640]{2,1,0:T(8,128)(2,1)S(1)}, bf16[2,64,640]{2,1,0:T(8,128)(2,1)S(1)}, u32[]{:S(2)}, u32[]{:S(2)}) collective-permute-start(bf16[2,64,640]{2,1,0:T(8,128)(2,1)S(1)} %get-tuple-element.41), channel_id=1, source_target_pairs={{0,1},{1,0},{2,3},{3,2},{4,5},{5,4},{6,7},{7,6},{8,9},{9,8},{10,11... | collective-permute-start | bytes 491528 | tf_op jit(solution)/shard_map/ppermute | solution.py:579
  107.3 7.8 %collective-permute-start.13 = (bf16[2,64,640]{2,1,0:T(8,128)(2,1)S(1)}, bf16[2,64,640]{2,1,0:T(8,128)(2,1)S(1)}, u32[]{:S(2)}, u32[]{:S(2)}) collective-permute-start(bf16[2,64,640]{2,1,0:T(8,128)(2,1)S(1)} %collective-permute-done.9), channel_id=1, source_target_pairs={{0,1},{1,0},{2,3},{3,2},{4,5},{5,4},{6,7},{7,6},{8,9},{9,8},{10,11... | collective-permute-start | bytes 491528 | tf_op jit(solution)/shard_map/ppermute | solution.py:579
  108.4 10.3 %collective-permute-start.12 = (bf16[2,64,640]{2,1,0:T(8,128)(2,1)S(1)}, bf16[2,64,640]{2,1,0:T(8,128)(2,1)S(1)}, u32[]{:S(2)}, u32[]{:S(2)}) collective-permute-start(bf16[2,64,640]{2,1,0:T(8,128)(2,1)S(1)} %collective-permute-done.8), channel_id=1, source_target_pairs={{0,1},{1,0},{2,3},{3,2},{4,5},{5,4},{6,7},{7,6},{8,9},{9,8},{10,11... | collective-permute-start | bytes 491528 | tf_op jit(solution)/shard_map/ppermute | solution.py:579
  136.1 23.8 %all-to-all-start.3 = ((bf16[16,32,1152]{2,1,0:T(8,128)(2,1)}), bf16[16,32,1152]{2,1,0:T(8,128)(2,1)S(1)}, u32[]{:S(2)}, u32[]{:S(2)}) async-start(bf16[16,32,1152]{2,1,0:T(8,128)(2,1)} %bitcast.40), calls=%async_computation.3 | async-start | bytes 2359296 | tf_op jit(solution)/shard_map/all_to_all | solution.py:492
  168.5 20.0 %collective-permute-start.21 = (bf16[64,3072]{1,0:T(8,128)(2,1)}, bf16[64,3072]{1,0:T(8,128)(2,1)S(1)}, u32[]{:S(2)}, u32[]{:S(2)}) collective-permute-start(bf16[64,3072]{1,0:T(8,128)(2,1)} %get-tuple-element.25), channel_id=1, source_target_pairs={{0,12},{1,13},{2,14},{3,15},{4,0},{5,1},{6,2},{7,3},{8,4},{9,5},{1... | collective-permute-start | bytes 1179656 | tf_op jit(solution)/shard_map/ppermute | solution.py:611
  171.0 17.5 %collective-permute-start.20 = (bf16[64,3072]{1,0:T(8,128)(2,1)}, bf16[64,3072]{1,0:T(8,128)(2,1)S(1)}, u32[]{:S(2)}, u32[]{:S(2)}) collective-permute-start(bf16[64,3072]{1,0:T(8,128)(2,1)} %get-tuple-element.24), channel_id=1, source_target_pairs={{0,8},{1,9},{2,10},{3,11},{4,12},{5,13},{6,14},{7,15},{8,0},{9,1},... | collective-permute-start | bytes 1179656 | tf_op jit(solution)/shard_map/ppermute | solution.py:611
  171.5 20.7 %collective-permute-start.19 = (bf16[64,3072]{1,0:T(8,128)(2,1)}, bf16[64,3072]{1,0:T(8,128)(2,1)S(1)}, u32[]{:S(2)}, u32[]{:S(2)}) collective-permute-start(bf16[64,3072]{1,0:T(8,128)(2,1)} %get-tuple-element.23), channel_id=1, source_target_pairs={{0,4},{1,5},{2,6},{3,7},{4,8},{5,9},{6,10},{7,11},{8,12},{9,13},{1... | collective-permute-start | bytes 1179656 | tf_op jit(solution)/shard_map/ppermute | solution.py:611
  176.4 18.9 %collective-permute-start.23 = (bf16[128,2048]{1,0:T(8,128)(2,1)}, bf16[128,2048]{1,0:T(8,128)(2,1)S(1)}, u32[]{:S(2)}, u32[]{:S(2)}) collective-permute-start(bf16[128,2048]{1,0:T(8,128)(2,1)} %get-tuple-element.28), channel_id=1, source_target_pairs={{0,3},{1,2},{2,1},{3,0},{4,7},{5,6},{6,5},{7,4},{8,11},{9,10},{10,... | collective-permute-start | bytes 1572872 | tf_op jit(solution)/shard_map/ppermute | solution.py:613
  192.4 7.7 %collective-permute-start.22 = (bf16[32,3072]{1,0:T(8,128)(2,1)S(1)}, bf16[32,3072]{1,0:T(8,128)(2,1)S(1)}, u32[]{:S(2)}, u32[]{:S(2)}) collective-permute-start(bf16[32,3072]{1,0:T(8,128)(2,1)S(1)} %slice.55), channel_id=1, source_target_pairs={{0,3},{1,2},{2,1},{3,0},{4,7},{5,6},{6,5},{7,4},{8,11},{9,10},{10,... | collective-permute-start | bytes 589832 | tf_op jit(solution)/shard_map/ppermute | solution.py:615
  196.4 8.5 %collective-permute-start.24 = (bf16[32,2048]{1,0:T(8,128)(2,1)S(1)}, bf16[32,2048]{1,0:T(8,128)(2,1)S(1)}, u32[]{:S(2)}, u32[]{:S(2)}) collective-permute-start(bf16[32,2048]{1,0:T(8,128)(2,1)S(1)} %get-tuple-element.47), channel_id=1, source_target_pairs={{0,4},{1,5},{2,6},{3,7},{4,8},{5,9},{6,10},{7,11},{8,12},{9,13},{1... | collective-permute-start | bytes 393224 | tf_op jit(solution)/shard_map/ppermute | solution.py:618
  (21 other events, 131.6 us)
Sparse Core Ops, SparseCore 0:
  9.5 69.3 all-gather.2
  96.1 38.1 all-gather.4

commit v9 on v8

--- a/solution.py
+++ b/solution.py
@@ -476,11 +476,18 @@
 
 
 def exchange_groups(blocks, group):
+    return exchange_along_z(exchange_cores(blocks, group), group)
+
+
+def exchange_cores(blocks, group):
     by_core = blocks.reshape((GROUPS // 2, 2) + blocks.shape[1:])
     kept = lax.dynamic_index_in_dim(by_core, group % 2, 1, keepdims=True)
     given = lax.dynamic_index_in_dim(by_core, 1 - group % 2, 1, keepdims=True)
     given = lax.ppermute(given, "grp", across_groups(1))
-    both = jnp.concatenate([kept, given], axis=1)
+    return jnp.concatenate([kept, given], axis=1)
+
+
+def exchange_along_z(both, group):
     arrived = []
     for k in range(GROUPS // 2):
         block = lax.dynamic_index_in_dim(both, (group // 2) ^ k, 0, keepdims=False)
@@ -522,7 +529,7 @@
     slot_suffix = jnp.concatenate(
         [slot_suffix, jnp.broadcast_to(slot_lengths, (GROUPS, SLOT_SAMPLES, 2 * HEAD_SIZE))], axis=1
     )
-    suffix = jnp.concatenate(exchange_groups(slot_suffix, group), axis=0)
+    both = exchange_cores(slot_suffix, group)
 
     owners = jnp.arange(GROUPS, dtype=jnp.int32)
     local_of_slot = lax.dynamic_index_in_dim(local_table, group, 1, keepdims=False)
@@ -552,14 +559,15 @@
 
     slice_rows = OWN_WIDTH // GROUPS
     weight_slice = lax.dynamic_slice_in_dim(output_weight, group * slice_rows, slice_rows, 0)
-    low_rank, head_pages, weight_slice = lax.optimization_barrier(
-        (low_rank, jnp.swapaxes(prompt_cache, 0, 1), weight_slice)
+    low_rank, head_pages, weight_slice, both = lax.optimization_barrier(
+        (low_rank, jnp.swapaxes(prompt_cache, 0, 1), weight_slice, both)
     )
     arrived = swap(head_pages, "ad", ROLE_GROUPS)
     weight_slice = lax.ppermute(weight_slice, "ad", PARTNERS)
     part_rows, weight_slice = lax.optimization_barrier((part_rows, weight_slice))
     other_weight = lax.all_gather(weight_slice, "grp", axis=0, tiled=True)
 
+    suffix = jnp.concatenate(exchange_along_z(both, group), axis=0)
     steps = jnp.arange(DECODE_STEPS, dtype=jnp.int32)
     position = (PROMPT_TOKENS + suffix_lengths[:, None] + steps[None, :]).astype(jnp.float32)
     cosine, sine = angle_tables(position.reshape(ROWS))

time: 213 us -> 213 us (level)
  waiting for transfers between devices: 83.6 us -> 81.3 us
    ppermute x3, waiting for transfers between devices: 0.35 us -> 4.97 us  [shards(): lax.ppermute(ring, 'ad', along_y(k))]
    ppermute x1, waiting for transfers between devices: 14.7 us -> 10.1 us  [shards(): weight_slice = lax.ppermute(weight_slice, 'ad', PARTNERS)]
    ppermute x3, waiting for transfers between devices: 2.7 us -> 0.01 us  [shards(): lax.ppermute(rank_rows, 'ad', along_x(k))]
  transfers between devices with their start and end apart: 33 -> 33, of which waited for: 19 -> 20; matrix products, arithmetic and copies ran while one was open for 10% -> 10% of each run, Pallas kernels for 16% -> 16%
where the time goes in v9:
time: 213 us; the launch traced here: 212 us
  waiting for transfers between devices  81.3 us (38%)
  starting transfers between devices  52.1 us (24%)
  Pallas kernels  41.2 us (19%)
  between operations  13.8 us (6%)
  local copies, waits for them, and re-layouts  11.9 us (6%)
  other arithmetic  9.53 us (4%)
  matrix products  2.16 us (1%)
    all_to_all x4, waiting for transfers between devices, swap(): lax.all_to_all(block, axes, split_axis=0, concat_axis=0, tiled=True, axis...  27 us
    all_to_all x4, starting transfers between devices, swap(): lax.all_to_all(block, axes, split_axis=0, concat_axis=0, tiled=True, axis...  22.6 us
    pallas_call x1, Pallas kernels, attend(): pl.pallas_call(attend_kernel, grid_spec=pltpu.PrefetchScalarGridSpec(num_...  17.4 us
    ppermute x3, waiting for transfers between devices, shards(): lax.ppermute(by_y[k], 'ad', along_y(k))  13.1 us
    pallas_call x1, Pallas kernels, project(): pl.pallas_call(project_kernel, grid_spec=pltpu.PrefetchScalarGridSpec(num...  11.9 us
    ppermute x1, waiting for transfers between devices, shards(): weight_slice = lax.ppermute(weight_slice, 'ad', PARTNERS)  10.1 us
    ppermute x4, waiting for transfers between devices, shards(): lax.ppermute(part, 'ad', PARTNERS)  9.72 us
    ppermute x6, starting transfers between devices, exchange_along_z(): lax.ppermute(block, 'grp', across_groups(2 * k))  7.75 us
  transfers between devices with their start and end apart: 33, of which 20 were waited for; matrix products, arithmetic and copies ran while one was open for 10% of the time, Pallas kernels for 16%

profile of v9, /device:TPU:1, one launch (start us, length us, event | category | flops | bytes accessed | tf_op | source)
XLA Modules:
  0.0 211.9 jit_solution(10759520532840454005)
XLA Ops:
  9.5 7.6 %all-to-all-start = ((bf16[16,32,320]{2,1,0:T(8,128)(2,1)}), bf16[16,32,320]{2,1,0:T(8,128)(2,1)}, u32[]{:S(2)}, u32[]{:S(2)}) async-start(bf16[16,32,320]{2,1,0:T(8,128)(2,1)} %bitcast.76), calls=%async_computation | async-start | bytes 786432 | tf_op jit(solution)/shard_map/all_to_all | solution.py:499
  22.7 3.7 %all-to-all-done = bf16[16,32,320]{2,1,0:T(8,128)(2,1)} async-done(((bf16[16,32,320]{2,1,0:T(8,128)(2,1)}), bf16[16,32,320]{2,1,0:T(8,128)(2,1)}, u32[]{:S(2)}, u32[]{:S(2)}) %all-to-all-start) | async-done | bytes 327712 | tf_op jit(solution)/shard_map/all_to_all | solution.py:499
  28.5 3.5 %all-to-all-start.1 = ((f32[16,32,128]{2,1,0:T(8,128)}), f32[16,32,128]{2,1,0:T(8,128)S(1)}, u32[]{:S(2)}, u32[]{:S(2)}) async-start(f32[16,32,128]{2,1,0:T(8,128)} %bitcast.13), calls=%async_computation.1 | async-start | bytes 524288 | tf_op jit(solution)/shard_map/all_to_all | solution.py:499
  32.2 7.4 %all-to-all-done.1 = f32[16,32,128]{2,1,0:T(8,128)S(1)} async-done(((f32[16,32,128]{2,1,0:T(8,128)}), f32[16,32,128]{2,1,0:T(8,128)S(1)}, u32[]{:S(2)}, u32[]{:S(2)}) %all-to-all-start.1) | async-done | bytes 262176 | tf_op jit(solution)/shard_map/all_to_all | solution.py:499
  42.2 4.6 %copy.52 = bf16[4,8,256,256]{3,2,0,1:T(8,128)(2,1)} copy(bf16[4,8,256,256]{3,2,1,0:T(8,128)(2,1)} %param.14) | data formatting | bytes 8388608 | tf_op args[1]
  56.6 3.6 %collective-permute-start.18 = (bf16[2,272,256]{2,1,0:T(8,128)(2,1)}, bf16[2,272,256]{2,1,0:T(8,128)(2,1)S(1)}, u32[]{:S(2)}, u32[]{:S(2)}) collective-permute-start(bf16[2,272,256]{2,1,0:T(8,128)(2,1)} %get-tuple-element.36), channel_id=1, source_target_pairs={{0,96},{16,112},{32,64},{48,80},{64,32},{80,48},{96,0},{112,16},{1... | collective-permute-start | bytes 835592 | tf_op jit(solution)/shard_map/ppermute | solution.py:494
  61.9 4.6 %all-to-all-start.2 = ((bf16[8,4,256,256]{3,2,1,0:T(8,128)(2,1)}), bf16[8,4,256,256]{3,2,1,0:T(8,128)(2,1)}, u32[]{:S(2)}, u32[]{:S(2)}) async-start(bf16[8,4,256,256]{3,2,1,0:T(8,128)(2,1)} %bitcast.78), calls=%async_computation.2 | async-start | bytes 8388608 | tf_op jit(solution)/shard_map/all_to_all | solution.py:499
  69.7 10.1 %collective-permute-done.7 = bf16[64,5120]{1,0:T(8,128)(2,1)S(1)} collective-permute-done((bf16[64,5120]{1,0:T(8,128)(2,1)S(1)}, bf16[64,5120]{1,0:T(8,128)(2,1)S(1)}, u32[]{:S(2)}, u32[]{:S(2)}) %collective-permute-start.7) | collective-permute-done | bytes 655392 | tf_op jit(solution)/shard_map/ppermute | solution.py:566
  79.8 11.9 %project.1 = bf16[8,64,640]{2,1,0:T(8,128)(2,1)} custom-call(s32[8]{0:T(128)} %copy-done.7, s32[16]{0:T(128)} %fusion.23.spot_ref, bf16[512,5120]{1,0:T(8,128)(2,1)} %all-gather.3.cloned.1.call-done.tokens_ref, bf16[5120,512]{1,0:T(8,128)(2,1)} %query_ref.1, bf16[128,5120]{1,0:T(8,128)(2,1)} %bitcast.93, bf16[16,32,128]{2,1,0:T(8,128)(2,1)} %bitcast.83, ...), custom_call_target="tpu_custom_call" | custom-call | flops 33554432000 | bytes 13000000 | tf_op jit(solution)/shard_map/project/pallas_call | solution.py:146
  96.5 2.9 %collective-permute-start.11 = (bf16[2,64,640]{2,1,0:T(8,128)(2,1)S(1)}, bf16[2,64,640]{2,1,0:T(8,128)(2,1)S(1)}, u32[]{:S(2)}, u32[]{:S(2)}) collective-permute-start(bf16[2,64,640]{2,1,0:T(8,128)(2,1)S(1)} %get-tuple-element.46), channel_id=1, source_target_pairs={{0,96},{16,112},{32,64},{48,80},{64,32},{80,48},{96,0},{112,16},{1... | collective-permute-start | bytes 491528 | tf_op jit(solution)/shard_map/ppermute | solution.py:494
  101.4 5.1 %collective-permute-done.11 = bf16[2,64,640]{2,1,0:T(8,128)(2,1)S(1)} collective-permute-done((bf16[2,64,640]{2,1,0:T(8,128)(2,1)S(1)}, bf16[2,64,640]{2,1,0:T(8,128)(2,1)S(1)}, u32[]{:S(2)}, u32[]{:S(2)}) %collective-permute-start.11) | collective-permute-done | bytes 163872 | tf_op jit(solution)/shard_map/ppermute | solution.py:494
  108.6 2.7 %collective-permute-done.15 = bf16[2,64,640]{2,1,0:T(8,128)(2,1)S(1)} collective-permute-done((bf16[2,64,640]{2,1,0:T(8,128)(2,1)S(1)}, bf16[2,64,640]{2,1,0:T(8,128)(2,1)S(1)}, u32[]{:S(2)}, u32[]{:S(2)}) %collective-permute-start.15) | collective-permute-done | bytes 163872 | tf_op jit(solution)/shard_map/ppermute | solution.py:587
  111.3 3.5 %collective-permute-done.14 = bf16[2,64,640]{2,1,0:T(8,128)(2,1)S(1)} collective-permute-done((bf16[2,64,640]{2,1,0:T(8,128)(2,1)S(1)}, bf16[2,64,640]{2,1,0:T(8,128)(2,1)S(1)}, u32[]{:S(2)}, u32[]{:S(2)}) %collective-permute-start.14) | collective-permute-done | bytes 163872 | tf_op jit(solution)/shard_map/ppermute | solution.py:587
  114.8 3.5 %collective-permute-done.13 = bf16[2,64,640]{2,1,0:T(8,128)(2,1)S(1)} collective-permute-done((bf16[2,64,640]{2,1,0:T(8,128)(2,1)S(1)}, bf16[2,64,640]{2,1,0:T(8,128)(2,1)S(1)}, u32[]{:S(2)}, u32[]{:S(2)}) %collective-permute-start.13) | collective-permute-done | bytes 163872 | tf_op jit(solution)/shard_map/ppermute | solution.py:587
  118.4 17.4 %attend.1 = bf16[8,2,32,1152]{3,2,1,0:T(8,128)(2,1)} custom-call(s32[8]{0:T(128)S(1)} %get-tuple-element.32.order_ref, s32[8]{0:T(128)S(1)} %get-tuple-element.31.local_ref, s32[8]{0:T(128)S(1)} %broadcast_xor_fusion.reach_ref, s32[2]{0:T(128)S(1)} %pad_add_fusion.1.place_ref, bf16[8,64,640]{2,1,0:T(8,128)(2,1)S(1)} %pad_maximum_fusion.2.own_ref, ...), custom_call_target="tpu_custom_call" | custom-call | flops 76504104960 | bytes 8000000 | tf_op jit(solution)/shard_map/attend/pallas_call | solution.py:305
  135.8 6.9 %all-to-all-start.3 = ((bf16[16,32,1152]{2,1,0:T(8,128)(2,1)}), bf16[16,32,1152]{2,1,0:T(8,128)(2,1)S(1)}, u32[]{:S(2)}, u32[]{:S(2)}) async-start(bf16[16,32,1152]{2,1,0:T(8,128)(2,1)} %bitcast.40), calls=%async_computation.3 | async-start | bytes 2359296 | tf_op jit(solution)/shard_map/all_to_all | solution.py:499
  143.3 16.0 %all-to-all-done.3 = bf16[16,32,1152]{2,1,0:T(8,128)(2,1)S(1)} async-done(((bf16[16,32,1152]{2,1,0:T(8,128)(2,1)}), bf16[16,32,1152]{2,1,0:T(8,128)(2,1)S(1)}, u32[]{:S(2)}, u32[]{:S(2)}) %all-to-all-start.3) | async-done | bytes 1179680 | tf_op jit(solution)/shard_map/all_to_all | solution.py:499
  160.4 7.5 %left_product.1 = (bf16[256,1024]{1,0:T(8,128)(2,1)}, bf16[64,3072]{1,0:T(8,128)(2,1)}, bf16[64,3072]{1,0:T(8,128)(2,1)}, bf16[64,3072]{1,0:T(8,128)(2,1)}, bf16[64,3072]{1,0:T(8,128)(2,1)}) custom-call(s32[3]{0:T(128)} %pad_add_fusion.place_ref, bf16[8,2,32,1152]{3,2,1,0:T(8,128)(2,1)} %bitcast.79, bf16[512,5120]{1,0:T(8,128)(2,1)} %own_ref.3, ...), custom_call_target="tpu_custom_call" | custom-call | flops 5368709120 | bytes 8000000 | tf_op jit(solution)/shard_map/left_product/pallas_call | solution.py:419
  171.5 4.3 %right_product.1 = (bf16[128,2048]{1,0:T(8,128)(2,1)}, bf16[128,2048]{1,0:T(8,128)(2,1)}) custom-call(bf16[256,1024]{1,0:T(8,128)(2,1)} %get-tuple-element.28.mixed_ref, bf16[512,5120]{1,0:T(8,128)(2,1)} %own_ref.3, bf16[512,5120]{1,0:T(8,128)(2,1)} %all-gather.5.cloned.1.call-done.other_ref), custom_call_target="tpu_custom_call" | custom-call | flops 5368709120 | bytes 8000000 | tf_op jit(solution)/shard_map/right_product/pallas_call | solution.py:443
  175.9 2.7 %collective-permute-start.23 = (bf16[128,2048]{1,0:T(8,128)(2,1)}, bf16[128,2048]{1,0:T(8,128)(2,1)S(1)}, u32[]{:S(2)}, u32[]{:S(2)}) collective-permute-start(bf16[128,2048]{1,0:T(8,128)(2,1)} %get-tuple-element.30), channel_id=1, source_target_pairs={{0,3},{1,2},{2,1},{3,0},{4,7},{5,6},{6,5},{7,4},{8,11},{9,10},{10,... | collective-permute-start | bytes 1572872 | tf_op jit(solution)/shard_map/ppermute | solution.py:621
  178.6 9.4 %collective-permute-done.21 = bf16[64,3072]{1,0:T(8,128)(2,1)S(1)} collective-permute-done((bf16[64,3072]{1,0:T(8,128)(2,1)}, bf16[64,3072]{1,0:T(8,128)(2,1)S(1)}, u32[]{:S(2)}, u32[]{:S(2)}) %collective-permute-start.21) | collective-permute-done | bytes 393248 | tf_op jit(solution)/shard_map/ppermute | solution.py:619
  188.0 3.7 %collective-permute-done.19 = bf16[64,3072]{1,0:T(8,128)(2,1)S(1)} collective-permute-done((bf16[64,3072]{1,0:T(8,128)(2,1)}, bf16[64,3072]{1,0:T(8,128)(2,1)S(1)}, u32[]{:S(2)}, u32[]{:S(2)}) %collective-permute-start.19) | collective-permute-done | bytes 393248 | tf_op jit(solution)/shard_map/ppermute | solution.py:619
  196.4 2.9 %collective-permute-done.22 = bf16[32,3072]{1,0:T(8,128)(2,1)S(1)} collective-permute-done((bf16[32,3072]{1,0:T(8,128)(2,1)S(1)}, bf16[32,3072]{1,0:T(8,128)(2,1)S(1)}, u32[]{:S(2)}, u32[]{:S(2)}) %collective-permute-start.22) | collective-permute-done | bytes 196640 | tf_op jit(solution)/shard_map/ppermute | solution.py:623
  200.4 3.9 %collective-permute-done.24 = bf16[32,2048]{1,0:T(8,128)(2,1)S(1)} collective-permute-done((bf16[32,2048]{1,0:T(8,128)(2,1)S(1)}, bf16[32,2048]{1,0:T(8,128)(2,1)S(1)}, u32[]{:S(2)}, u32[]{:S(2)}) %collective-permute-start.24) | collective-permute-done | bytes 131104 | tf_op jit(solution)/shard_map/ppermute | solution.py:626
  (128 shorter events, 48.7 us)
Async XLA Ops:
  6.5 73.3 %all-gather.3.cloned.1.call-start = ((), (), s32[]{:S(2)}) async-start(), calls=%async_computation.4 | async-start | bytes 5570560 | tf_op jit(solution)/shard_map/all_gather | solution.py:525
  9.5 16.9 %all-to-all-start = ((bf16[16,32,320]{2,1,0:T(8,128)(2,1)}), bf16[16,32,320]{2,1,0:T(8,128)(2,1)}, u32[]{:S(2)}, u32[]{:S(2)}) async-start(bf16[16,32,320]{2,1,0:T(8,128)(2,1)} %bitcast.76), calls=%async_computation | async-start | bytes 786432 | tf_op jit(solution)/shard_map/all_to_all | solution.py:499
  17.5 31.0 %collective-permute-start.6 = (bf16[4,1,272,256]{3,2,1,0:T(8,128)(2,1)S(1)}, bf16[4,1,272,256]{3,2,1,0:T(8,128)(2,1)S(1)}, u32[]{:S(2)}, u32[]{:S(2)}) collective-permute-start(bf16[4,1,272,256]{3,2,1,0:T(8,128)(2,1)S(1)} %get-tuple-element.40), channel_id=1, source_target_pairs={{0,16},{16,0},{32,48},{48,32},{64,80},{80,64},{96,112},{112,96},{1... | collective-permute-start | bytes 1671176 | tf_op jit(solution)/shard_map/ppermute | solution.py:486
  28.5 11.1 %all-to-all-start.1 = ((f32[16,32,128]{2,1,0:T(8,128)}), f32[16,32,128]{2,1,0:T(8,128)S(1)}, u32[]{:S(2)}, u32[]{:S(2)}) async-start(f32[16,32,128]{2,1,0:T(8,128)} %bitcast.13), calls=%async_computation.1 | async-start | bytes 524288 | tf_op jit(solution)/shard_map/all_to_all | solution.py:499
  39.6 7.2 %collective-permute-start.2 = (bf16[32,128]{1,0:T(8,128)(2,1)S(1)}, bf16[32,128]{1,0:T(8,128)(2,1)S(1)}, u32[]{:S(2)}, u32[]{:S(2)}) collective-permute-start(bf16[32,128]{1,0:T(8,128)(2,1)S(1)} %reduce_sum.69), channel_id=1, source_target_pairs={{0,3},{1,0},{2,1},{3,2},{4,7},{5,4},{6,5},{7,6},{8,11},{9,8},{10,9... | collective-permute-start | bytes 24584 | tf_op jit(solution)/shard_map/ppermute | solution.py:553
  54.2 25.5 %collective-permute-start.7 = (bf16[64,5120]{1,0:T(8,128)(2,1)S(1)}, bf16[64,5120]{1,0:T(8,128)(2,1)S(1)}, u32[]{:S(2)}, u32[]{:S(2)}) collective-permute-start(bf16[64,5120]{1,0:T(8,128)(2,1)S(1)} %constant_dynamic-slice_fusion.2), channel_id=1, source_target_pairs={{0,1},{1,0},{2,3},{3,2},{4,5},{5,4},{6,7},{7,6},{8,9},{9,8},{10,11... | collective-permute-start | bytes 1966088 | tf_op jit(solution)/shard_map/ppermute | solution.py:566
  56.6 10.5 %collective-permute-start.18 = (bf16[2,272,256]{2,1,0:T(8,128)(2,1)}, bf16[2,272,256]{2,1,0:T(8,128)(2,1)S(1)}, u32[]{:S(2)}, u32[]{:S(2)}) collective-permute-start(bf16[2,272,256]{2,1,0:T(8,128)(2,1)} %get-tuple-element.36), channel_id=1, source_target_pairs={{0,96},{16,112},{32,64},{48,80},{64,32},{80,48},{96,0},{112,16},{1... | collective-permute-start | bytes 835592 | tf_op jit(solution)/shard_map/ppermute | solution.py:494
  60.1 7.3 %collective-permute-start.17 = (bf16[2,272,256]{2,1,0:T(8,128)(2,1)}, bf16[2,272,256]{2,1,0:T(8,128)(2,1)}, u32[]{:S(2)}, u32[]{:S(2)}) collective-permute-start(bf16[2,272,256]{2,1,0:T(8,128)(2,1)} %get-tuple-element.37), channel_id=1, source_target_pairs={{0,64},{16,80},{32,96},{48,112},{64,0},{80,16},{96,32},{112,48},{1... | collective-permute-start | bytes 835592 | tf_op jit(solution)/shard_map/ppermute | solution.py:494
  60.1 8.4 %collective-permute-start.16 = (bf16[2,272,256]{2,1,0:T(8,128)(2,1)S(1)}, bf16[2,272,256]{2,1,0:T(8,128)(2,1)}, u32[]{:S(2)}, u32[]{:S(2)}) collective-permute-start(bf16[2,272,256]{2,1,0:T(8,128)(2,1)S(1)} %get-tuple-element.38), channel_id=1, source_target_pairs={{0,32},{16,48},{32,0},{48,16},{64,96},{80,112},{96,64},{112,80},{1... | collective-permute-start | bytes 835592 | tf_op jit(solution)/shard_map/ppermute | solution.py:494
  61.9 56.5 %all-to-all-start.2 = ((bf16[8,4,256,256]{3,2,1,0:T(8,128)(2,1)}), bf16[8,4,256,256]{3,2,1,0:T(8,128)(2,1)}, u32[]{:S(2)}, u32[]{:S(2)}) async-start(bf16[8,4,256,256]{3,2,1,0:T(8,128)(2,1)} %bitcast.78), calls=%async_computation.2 | async-start | bytes 8388608 | tf_op jit(solution)/shard_map/all_to_all | solution.py:499
  66.5 92.9 %all-gather.5.cloned.1.call-start = ((), (), s32[]{:S(2)}) async-start(), calls=%async_computation.5 | async-start | bytes 5898240 | tf_op jit(solution)/shard_map/all_gather | solution.py:568
  96.5 10.0 %collective-permute-start.11 = (bf16[2,64,640]{2,1,0:T(8,128)(2,1)S(1)}, bf16[2,64,640]{2,1,0:T(8,128)(2,1)S(1)}, u32[]{:S(2)}, u32[]{:S(2)}) collective-permute-start(bf16[2,64,640]{2,1,0:T(8,128)(2,1)S(1)} %get-tuple-element.46), channel_id=1, source_target_pairs={{0,96},{16,112},{32,64},{48,80},{64,32},{80,48},{96,0},{112,16},{1... | collective-permute-start | bytes 491528 | tf_op jit(solution)/shard_map/ppermute | solution.py:494
  99.4 7.3 %collective-permute-start.10 = (bf16[2,64,640]{2,1,0:T(8,128)(2,1)S(1)}, bf16[2,64,640]{2,1,0:T(8,128)(2,1)S(1)}, u32[]{:S(2)}, u32[]{:S(2)}) collective-permute-start(bf16[2,64,640]{2,1,0:T(8,128)(2,1)S(1)} %get-tuple-element.45), channel_id=1, source_target_pairs={{0,64},{16,80},{32,96},{48,112},{64,0},{80,16},{96,32},{112,48},{1... | collective-permute-start | bytes 491528 | tf_op jit(solution)/shard_map/ppermute | solution.py:494
  99.7 8.2 %collective-permute-start.9 = (bf16[2,64,640]{2,1,0:T(8,128)(2,1)S(1)}, bf16[2,64,640]{2,1,0:T(8,128)(2,1)S(1)}, u32[]{:S(2)}, u32[]{:S(2)}) collective-permute-start(bf16[2,64,640]{2,1,0:T(8,128)(2,1)S(1)} %get-tuple-element.44), channel_id=1, source_target_pairs={{0,32},{16,48},{32,0},{48,16},{64,96},{80,112},{96,64},{112,80},{1... | collective-permute-start | bytes 491528 | tf_op jit(solution)/shard_map/ppermute | solution.py:494
  101.1 7.5 %collective-permute-start.12 = (bf16[2,64,640]{2,1,0:T(8,128)(2,1)S(1)}, bf16[2,64,640]{2,1,0:T(8,128)(2,1)S(1)}, u32[]{:S(2)}, u32[]{:S(2)}) collective-permute-start(bf16[2,64,640]{2,1,0:T(8,128)(2,1)S(1)} %get-tuple-element.43), channel_id=1, source_target_pairs={{0,1},{1,0},{2,3},{3,2},{4,5},{5,4},{6,7},{7,6},{8,9},{9,8},{10,11... | collective-permute-start | bytes 491528 | tf_op jit(solution)/shard_map/ppermute | solution.py:587
  106.7 8.0 %collective-permute-start.14 = (bf16[2,64,640]{2,1,0:T(8,128)(2,1)S(1)}, bf16[2,64,640]{2,1,0:T(8,128)(2,1)S(1)}, u32[]{:S(2)}, u32[]{:S(2)}) collective-permute-start(bf16[2,64,640]{2,1,0:T(8,128)(2,1)S(1)} %collective-permute-done.10), channel_id=1, source_target_pairs={{0,1},{1,0},{2,3},{3,2},{4,5},{5,4},{6,7},{7,6},{8,9},{9,8},{10,11... | collective-permute-start | bytes 491528 | tf_op jit(solution)/shard_map/ppermute | solution.py:587
  107.9 10.3 %collective-permute-start.13 = (bf16[2,64,640]{2,1,0:T(8,128)(2,1)S(1)}, bf16[2,64,640]{2,1,0:T(8,128)(2,1)S(1)}, u32[]{:S(2)}, u32[]{:S(2)}) collective-permute-start(bf16[2,64,640]{2,1,0:T(8,128)(2,1)S(1)} %collective-permute-done.9), channel_id=1, source_target_pairs={{0,1},{1,0},{2,3},{3,2},{4,5},{5,4},{6,7},{7,6},{8,9},{9,8},{10,11... | collective-permute-start | bytes 491528 | tf_op jit(solution)/shard_map/ppermute | solution.py:587
  135.8 23.6 %all-to-all-start.3 = ((bf16[16,32,1152]{2,1,0:T(8,128)(2,1)}), bf16[16,32,1152]{2,1,0:T(8,128)(2,1)S(1)}, u32[]{:S(2)}, u32[]{:S(2)}) async-start(bf16[16,32,1152]{2,1,0:T(8,128)(2,1)} %bitcast.40), calls=%async_computation.3 | async-start | bytes 2359296 | tf_op jit(solution)/shard_map/all_to_all | solution.py:499
  167.9 20.1 %collective-permute-start.21 = (bf16[64,3072]{1,0:T(8,128)(2,1)}, bf16[64,3072]{1,0:T(8,128)(2,1)S(1)}, u32[]{:S(2)}, u32[]{:S(2)}) collective-permute-start(bf16[64,3072]{1,0:T(8,128)(2,1)} %get-tuple-element.27), channel_id=1, source_target_pairs={{0,12},{1,13},{2,14},{3,15},{4,0},{5,1},{6,2},{7,3},{8,4},{9,5},{1... | collective-permute-start | bytes 1179656 | tf_op jit(solution)/shard_map/ppermute | solution.py:619
  170.5 17.5 %collective-permute-start.20 = (bf16[64,3072]{1,0:T(8,128)(2,1)}, bf16[64,3072]{1,0:T(8,128)(2,1)S(1)}, u32[]{:S(2)}, u32[]{:S(2)}) collective-permute-start(bf16[64,3072]{1,0:T(8,128)(2,1)} %get-tuple-element.26), channel_id=1, source_target_pairs={{0,8},{1,9},{2,10},{3,11},{4,12},{5,13},{6,14},{7,15},{8,0},{9,1},... | collective-permute-start | bytes 1179656 | tf_op jit(solution)/shard_map/ppermute | solution.py:619
  170.9 20.8 %collective-permute-start.19 = (bf16[64,3072]{1,0:T(8,128)(2,1)}, bf16[64,3072]{1,0:T(8,128)(2,1)S(1)}, u32[]{:S(2)}, u32[]{:S(2)}) collective-permute-start(bf16[64,3072]{1,0:T(8,128)(2,1)} %get-tuple-element.25), channel_id=1, source_target_pairs={{0,4},{1,5},{2,6},{3,7},{4,8},{5,9},{6,10},{7,11},{8,12},{9,13},{1... | collective-permute-start | bytes 1179656 | tf_op jit(solution)/shard_map/ppermute | solution.py:619
  175.9 18.8 %collective-permute-start.23 = (bf16[128,2048]{1,0:T(8,128)(2,1)}, bf16[128,2048]{1,0:T(8,128)(2,1)S(1)}, u32[]{:S(2)}, u32[]{:S(2)}) collective-permute-start(bf16[128,2048]{1,0:T(8,128)(2,1)} %get-tuple-element.30), channel_id=1, source_target_pairs={{0,3},{1,2},{2,1},{3,0},{4,7},{5,6},{6,5},{7,4},{8,11},{9,10},{10,... | collective-permute-start | bytes 1572872 | tf_op jit(solution)/shard_map/ppermute | solution.py:621
  191.9 7.3 %collective-permute-start.22 = (bf16[32,3072]{1,0:T(8,128)(2,1)S(1)}, bf16[32,3072]{1,0:T(8,128)(2,1)S(1)}, u32[]{:S(2)}, u32[]{:S(2)}) collective-permute-start(bf16[32,3072]{1,0:T(8,128)(2,1)S(1)} %slice.55), channel_id=1, source_target_pairs={{0,3},{1,2},{2,1},{3,0},{4,7},{5,6},{6,5},{7,4},{8,11},{9,10},{10,... | collective-permute-start | bytes 589832 | tf_op jit(solution)/shard_map/ppermute | solution.py:623
  195.6 8.7 %collective-permute-start.24 = (bf16[32,2048]{1,0:T(8,128)(2,1)S(1)}, bf16[32,2048]{1,0:T(8,128)(2,1)S(1)}, u32[]{:S(2)}, u32[]{:S(2)}) collective-permute-start(bf16[32,2048]{1,0:T(8,128)(2,1)S(1)} %get-tuple-element.49), channel_id=1, source_target_pairs={{0,4},{1,5},{2,6},{3,7},{4,8},{5,9},{6,10},{7,11},{8,12},{9,13},{1... | collective-permute-start | bytes 393224 | tf_op jit(solution)/shard_map/ppermute | solution.py:626
  (21 other events, 130.6 us)
Sparse Core Ops, SparseCore 0:
  9.5 66.6 all-gather.2
  95.5 37.5 all-gather.4
